TPU v7x, 128 devices: a whole 4x4x4 slice. The times are simulated.
128 devices in a mesh: section: 8 (over y_lo, z), dp: 16 (over y_hi, x, core).
Axes of the slice: x: 4, y: 4 (y_hi: 2, y_lo: 2; y = y_hi * 2 + y_lo), z: 4, core: 2. Of those that a mesh axis runs over, the one named last changes fastest.
Arguments:
- activations: bfloat16 [8, 2, 1536, 5120], P('section', None, 'dp'), may hold values from -1 to 1
- norm_gain: float32 [8, 5120], P('section'), may hold values from 0.1 to 1.9
- key_weight: bfloat16 [8, 5120, 512], P('section'), may hold values from -0.59765625 to 0.59765625
- key_gain: float32 [8, 128], P('section'), may hold values from 0.1 to 1.9
- key_cotangent: bfloat16 [8, 2, 1536, 512], P('section', None, 'dp'), may hold values from -2 to 2
- upstream: bfloat16 [2, 1536, 5120], P(None, 'dp'), may hold values from -3 to 3
- master: float32 [8, 5120, 512], P('section', 'dp'), may hold values from -0.6 to 0.6
- first_moment: float32 [8, 5120, 512], P('section', 'dp'), may hold values from -6 to 6
- second_moment: float32 [8, 5120, 512], P('section', 'dp'), may hold values from 1 to 30
Outputs:
- input_grad: bfloat16 [8, 2, 1536, 5120], P('section', None, 'dp')
- new_weight: bfloat16 [8, 5120, 512], P('section')
- new_master: float32 [8, 5120, 512], P('section', 'dp')
- new_first: float32 [8, 5120, 512], P('section', 'dp')
- new_second: float32 [8, 5120, 512], P('section', 'dp')
All inputs are finite; a program needn't handle non-finite values.
Results may differ from a plain program's by a relative error of at most 0.0048.
Values may be sent and summed in bfloat16 or wider, within the bound.
No kernel may reach another device: no remote copies, remote signals or barrier semaphores. Data moves between devices by JAX's collectives and lax.ppermute only.
A program may use at most 128 MiB of HBM per device.

v0:
```python
import jax
import jax.numpy as jnp
from jax import lax
from jax.sharding import PartitionSpec as P

HEAD = 128
HEADS_KV = 4


beta_one = 0.9
beta_two = 0.95
learn_rate = 0.002
decay_rate = 0.1
adam_eps = 1e-08


def passed_along(block, axis, distance):
    devices = range(lax.axis_size(axis))
    route = [(i - distance, i) for i in devices if i - distance in devices]
    return lax.ppermute(block, axis, route)


def body(
    activations,
    norm_gain,
    key_weight,
    key_gain,
    key_cotangent,
    upstream,
    master,
    first_moment,
    second_moment,
):
    acts = activations[0]
    weight = key_weight[0]
    gain_row = norm_gain[0]
    micro, tok_rows, width = acts.shape
    xfloat = acts.astype(jnp.float32).reshape(micro * tok_rows, width)
    inv_rms = lax.rsqrt(jnp.mean(xfloat * xfloat, axis=-1, keepdims=True) + 1e-06)
    normed = (xfloat * inv_rms * gain_row).astype(jnp.bfloat16)
    raw_keys = jnp.dot(normed, weight, preferred_element_type=jnp.float32)
    nrows = raw_keys.shape[0]
    heads = raw_keys.reshape(nrows, HEADS_KV, HEAD)
    head_inv = lax.rsqrt(jnp.mean(heads * heads, axis=-1, keepdims=True) + 1e-06)
    scaled = key_cotangent[0].astype(jnp.float32).reshape(nrows, HEADS_KV, HEAD) * key_gain[0]
    key_grad = head_inv * (
        scaled - heads * head_inv * head_inv * jnp.mean(scaled * heads, axis=-1, keepdims=True)
    )
    key_grad = key_grad.reshape(nrows, HEADS_KV * HEAD).astype(jnp.bfloat16)
    weight_grad = lax.psum_scatter(
        lax.dot_general(
            normed, key_grad, (((0,), (0,)), ((), ())), preferred_element_type=jnp.float32
        ).astype(jnp.bfloat16),
        "dp",
        scatter_dimension=0,
        tiled=True,
    ).astype(jnp.float32)
    normed_grad = lax.dot_general(
        key_grad, weight, (((1,), (1,)), ((), ())), preferred_element_type=jnp.float32
    )
    gated = gain_row * normed_grad
    term = inv_rms * (
        gated - xfloat * inv_rms * inv_rms * jnp.mean(xfloat * gated, axis=-1, keepdims=True)
    )
    term = term.reshape(micro, tok_rows, width)
    is_top = lax.axis_index("section") == lax.axis_size("section") - 1
    term = term + jnp.where(is_top, upstream.astype(jnp.float32), jnp.zeros_like(term))

    def carry_step(turn, state):
        running, moving = state
        moving = passed_along(moving, "section", -1)
        return (running + moving, moving)

    total, unused = lax.fori_loop(0, lax.axis_size("section") - 1, carry_step, (term, term))
    input_grad = total.astype(jnp.bfloat16)[None]
    master_rows = master[0]
    new_first = beta_one * first_moment[0] + (1.0 - beta_one) * weight_grad
    new_second = beta_two * second_moment[0] + (1.0 - beta_two) * weight_grad * weight_grad
    corr_one = 1.0 - beta_one**10
    corr_two = 1.0 - beta_two**10
    update = (
        new_first / corr_one / (jnp.sqrt(new_second / corr_two) + adam_eps)
        + decay_rate * master_rows
    )
    new_master = master_rows - learn_rate * update
    new_weight = lax.all_gather(new_master.astype(jnp.bfloat16), "dp", axis=0, tiled=True)
    return (input_grad, new_weight[None], new_master[None], new_first[None], new_second[None])


def solution(mesh):
    return jax.shard_map(
        body,
        mesh=mesh,
        in_specs=(
            P("section", None, "dp", None),
            P("section", None),
            P("section", None, None),
            P("section", None),
            P("section", None, "dp", None),
            P(None, "dp", None),
            P("section", "dp", None),
            P("section", "dp", None),
            P("section", "dp", None),
        ),
        out_specs=(
            P("section", None, "dp", None),
            P("section", None, None),
            P("section", "dp", None),
            P("section", "dp", None),
            P("section", "dp", None),
        ),
        check_vma=False,
    )
```

profile of v0, /device:TPU:114, one launch (start us, length us, event | category | flops | bytes accessed | tf_op | source)
XLA Modules:
  0.0 841.7 jit_solution(13375134769266984749)
XLA Ops:
  7.2 2.0 multiply_reduce_fusion.1
  9.2 1.1 reshape.91
  10.3 8.1 copy.18
  19.0 4.7 multiply_reduce_fusion.3
  24.0 3.9 convolution_convert_fusion
  28.0 83.2 %reduce-scatter.2.cloned.1.call-done = bf16[320,512]{1,0:T(8,128)(2,1)} async-done(((bf16[5120,512]{1,0:T(8,128)(2,1)}), bf16[320,512]{1,0:T(8,128)(2,1)}) %reduce-scatter.2.cloned.1.call-update) | async-done | bytes 327696 | tf_op jit(solution)/shard_map/reduce_scatter | solution.py:50
  111.2 3.1 fusion.12
  114.4 4.4 multiply_reduce_fusion
  121.0 1.9 copy-done
  123.0 1.9 copy.39
  124.9 701.1 %while.12 = (s32[]{:T(128)}, f32[2,96,5120]{2,1,0:T(8,128)}, f32[2,96,5120]{2,1,0:T(8,128)}, s32[]{:T(128)}) while((s32[]{:T(128)}, f32[2,96,5120]{2,1,0:T(8,128)}, f32[2,96,5120]{2,1,0:T(8,128)}, s32[]{:T(128)}) %tuple.38), condition=%wide.region_5.6_spmd, body=%wide.region_4.0_spmd.sunk | while | flops 983042 | bytes 66846868 | solution.py:74
  124.9 2.7 collective-permute-start
  127.6 102.9 %collective-permute-done = f32[2,96,5120]{2,1,0:T(8,128)} collective-permute-done((f32[2,96,5120]{2,1,0:T(8,128)}, f32[2,96,5120]{2,1,0:T(8,128)}, u32[]{:S(2)}, u32[]{:S(2)}) %collective-permute-start) | collective-permute-done | bytes 3932192 | tf_op jit(solution)/shard_map/while/body/eval_jaxpr/ppermute | solution.py:20
  230.5 4.4 copy.45
  234.9 3.1 add.90
  238.0 1.9 copy-done.2
  239.9 1.9 collective-permute-start
  241.8 88.6 %collective-permute-done = f32[2,96,5120]{2,1,0:T(8,128)} collective-permute-done((f32[2,96,5120]{2,1,0:T(8,128)}, f32[2,96,5120]{2,1,0:T(8,128)}, u32[]{:S(2)}, u32[]{:S(2)}) %collective-permute-start) | collective-permute-done | bytes 3932192 | tf_op jit(solution)/shard_map/while/body/eval_jaxpr/ppermute | solution.py:20
  330.4 4.4 copy.45
  334.9 3.1 add.90
  338.0 1.9 copy-done.2
  339.9 1.9 collective-permute-start
  341.8 87.7 %collective-permute-done = f32[2,96,5120]{2,1,0:T(8,128)} collective-permute-done((f32[2,96,5120]{2,1,0:T(8,128)}, f32[2,96,5120]{2,1,0:T(8,128)}, u32[]{:S(2)}, u32[]{:S(2)}) %collective-permute-start) | collective-permute-done | bytes 3932192 | tf_op jit(solution)/shard_map/while/body/eval_jaxpr/ppermute | solution.py:20
  429.5 4.4 copy.45
  433.9 3.1 add.90
  437.0 1.9 copy-done.2
  439.0 1.9 collective-permute-start
  440.9 86.8 %collective-permute-done = f32[2,96,5120]{2,1,0:T(8,128)} collective-permute-done((f32[2,96,5120]{2,1,0:T(8,128)}, f32[2,96,5120]{2,1,0:T(8,128)}, u32[]{:S(2)}, u32[]{:S(2)}) %collective-permute-start) | collective-permute-done | bytes 3932192 | tf_op jit(solution)/shard_map/while/body/eval_jaxpr/ppermute | solution.py:20
  527.7 4.4 copy.45
  532.1 3.1 add.90
  535.2 1.9 copy-done.2
  537.1 1.9 collective-permute-start
  539.0 85.8 %collective-permute-done = f32[2,96,5120]{2,1,0:T(8,128)} collective-permute-done((f32[2,96,5120]{2,1,0:T(8,128)}, f32[2,96,5120]{2,1,0:T(8,128)}, u32[]{:S(2)}, u32[]{:S(2)}) %collective-permute-start) | collective-permute-done | bytes 3932192 | tf_op jit(solution)/shard_map/while/body/eval_jaxpr/ppermute | solution.py:20
  624.9 4.4 copy.45
  629.3 3.1 add.90
  632.4 1.9 copy-done.2
  634.3 1.9 collective-permute-start
  636.3 84.9 %collective-permute-done = f32[2,96,5120]{2,1,0:T(8,128)} collective-permute-done((f32[2,96,5120]{2,1,0:T(8,128)}, f32[2,96,5120]{2,1,0:T(8,128)}, u32[]{:S(2)}, u32[]{:S(2)}) %collective-permute-start) | collective-permute-done | bytes 3932192 | tf_op jit(solution)/shard_map/while/body/eval_jaxpr/ppermute | solution.py:20
  721.2 4.4 copy.45
  725.6 3.1 add.90
  728.7 1.9 copy-done.2
  730.6 1.9 collective-permute-start
  732.6 84.0 %collective-permute-done = f32[2,96,5120]{2,1,0:T(8,128)} collective-permute-done((f32[2,96,5120]{2,1,0:T(8,128)}, f32[2,96,5120]{2,1,0:T(8,128)}, u32[]{:S(2)}, u32[]{:S(2)}) %collective-permute-start) | collective-permute-done | bytes 3932192 | tf_op jit(solution)/shard_map/while/body/eval_jaxpr/ppermute | solution.py:20
  816.6 4.4 copy.45
  821.0 3.1 add.90
  824.1 1.9 copy-done.2
  826.0 3.6 convert_bitcast_fusion
  829.7 5.2 copy.49
  (47 shorter events, 3.4 us)
Async XLA Ops:
  7.2 104.0 %reduce-scatter.2.cloned.1.call-start = ((), (), s32[]{:S(2)}) async-start(), calls=%async_computation.1 | async-start | bytes 5570560 | tf_op jit(solution)/shard_map/reduce_scatter | solution.py:50
  10.3 8.1 copy-start.3
  10.3 8.1 copy-start.7
  18.4 0.7 copy-start.8
  27.9 83.2 %copy-start.5 = (f32[1,320,512]{2,1,0:T(8,128)S(1)}, f32[1,320,512]{2,1,0:T(8,128)}, u32[]{:S(2)}) copy-start(f32[1,320,512]{2,1,0:T(8,128)} %param.19) | copy-start | bytes 1966084
  27.9 83.2 %copy-start.6 = (f32[1,320,512]{2,1,0:T(8,128)S(1)}, f32[1,320,512]{2,1,0:T(8,128)}, u32[]{:S(2)}) copy-start(f32[1,320,512]{2,1,0:T(8,128)} %param.18) | copy-start | bytes 1966084
  28.0 801.7 %all-gather.2.cloned.1.call-start = ((), (), s32[]{:S(2)}) async-start(), calls=%async_computation.2 | async-start | bytes 5570560 | tf_op jit(solution)/shard_map/all_gather | solution.py:86
  118.8 1.6 copy-start.4
  121.0 1.9 copy-start
  124.9 105.6 %collective-permute-start = (f32[2,96,5120]{2,1,0:T(8,128)}, f32[2,96,5120]{2,1,0:T(8,128)}, u32[]{:S(2)}, u32[]{:S(2)}) collective-permute-start(f32[2,96,5120]{2,1,0:T(8,128)} %get-tuple-element.65), channel_id=1, source_target_pairs={{16,0},{32,16},{48,32},{64,48},{80,64},{96,80},{112,96},{17,1},{33... | collective-permute-start | bytes 11796488 | tf_op jit(solution)/shard_map/while/body/eval_jaxpr/ppermute | solution.py:20
  127.6 107.3 %copy-start.1 = (f32[2,96,5120]{2,1,0:T(8,128)S(1)}, f32[2,96,5120]{2,1,0:T(8,128)}, u32[]{:S(2)}) copy-start(f32[2,96,5120]{2,1,0:T(8,128)} %get-tuple-element.64) | copy-start | bytes 11796484 | tf_op jit(solution)/shard_map/while
  238.0 1.9 copy-start.2
  239.9 90.5 %collective-permute-start = (f32[2,96,5120]{2,1,0:T(8,128)}, f32[2,96,5120]{2,1,0:T(8,128)}, u32[]{:S(2)}, u32[]{:S(2)}) collective-permute-start(f32[2,96,5120]{2,1,0:T(8,128)} %get-tuple-element.65), channel_id=1, source_target_pairs={{16,0},{32,16},{48,32},{64,48},{80,64},{96,80},{112,96},{17,1},{33... | collective-permute-start | bytes 11796488 | tf_op jit(solution)/shard_map/while/body/eval_jaxpr/ppermute | solution.py:20
  241.8 93.0 %copy-start.1 = (f32[2,96,5120]{2,1,0:T(8,128)S(1)}, f32[2,96,5120]{2,1,0:T(8,128)}, u32[]{:S(2)}) copy-start(f32[2,96,5120]{2,1,0:T(8,128)} %get-tuple-element.64) | copy-start | bytes 11796484 | tf_op jit(solution)/shard_map/while
  338.0 1.9 copy-start.2
  339.9 89.6 %collective-permute-start = (f32[2,96,5120]{2,1,0:T(8,128)}, f32[2,96,5120]{2,1,0:T(8,128)}, u32[]{:S(2)}, u32[]{:S(2)}) collective-permute-start(f32[2,96,5120]{2,1,0:T(8,128)} %get-tuple-element.65), channel_id=1, source_target_pairs={{16,0},{32,16},{48,32},{64,48},{80,64},{96,80},{112,96},{17,1},{33... | collective-permute-start | bytes 11796488 | tf_op jit(solution)/shard_map/while/body/eval_jaxpr/ppermute | solution.py:20
  341.8 92.1 %copy-start.1 = (f32[2,96,5120]{2,1,0:T(8,128)S(1)}, f32[2,96,5120]{2,1,0:T(8,128)}, u32[]{:S(2)}) copy-start(f32[2,96,5120]{2,1,0:T(8,128)} %get-tuple-element.64) | copy-start | bytes 11796484 | tf_op jit(solution)/shard_map/while
  437.0 1.9 copy-start.2
  439.0 88.7 %collective-permute-start = (f32[2,96,5120]{2,1,0:T(8,128)}, f32[2,96,5120]{2,1,0:T(8,128)}, u32[]{:S(2)}, u32[]{:S(2)}) collective-permute-start(f32[2,96,5120]{2,1,0:T(8,128)} %get-tuple-element.65), channel_id=1, source_target_pairs={{16,0},{32,16},{48,32},{64,48},{80,64},{96,80},{112,96},{17,1},{33... | collective-permute-start | bytes 11796488 | tf_op jit(solution)/shard_map/while/body/eval_jaxpr/ppermute | solution.py:20
  440.9 91.2 %copy-start.1 = (f32[2,96,5120]{2,1,0:T(8,128)S(1)}, f32[2,96,5120]{2,1,0:T(8,128)}, u32[]{:S(2)}) copy-start(f32[2,96,5120]{2,1,0:T(8,128)} %get-tuple-element.64) | copy-start | bytes 11796484 | tf_op jit(solution)/shard_map/while
  535.2 1.9 copy-start.2
  537.1 87.8 %collective-permute-start = (f32[2,96,5120]{2,1,0:T(8,128)}, f32[2,96,5120]{2,1,0:T(8,128)}, u32[]{:S(2)}, u32[]{:S(2)}) collective-permute-start(f32[2,96,5120]{2,1,0:T(8,128)} %get-tuple-element.65), channel_id=1, source_target_pairs={{16,0},{32,16},{48,32},{64,48},{80,64},{96,80},{112,96},{17,1},{33... | collective-permute-start | bytes 11796488 | tf_op jit(solution)/shard_map/while/body/eval_jaxpr/ppermute | solution.py:20
  539.0 90.3 %copy-start.1 = (f32[2,96,5120]{2,1,0:T(8,128)S(1)}, f32[2,96,5120]{2,1,0:T(8,128)}, u32[]{:S(2)}) copy-start(f32[2,96,5120]{2,1,0:T(8,128)} %get-tuple-element.64) | copy-start | bytes 11796484 | tf_op jit(solution)/shard_map/while
  632.4 1.9 copy-start.2
  634.3 86.9 %collective-permute-start = (f32[2,96,5120]{2,1,0:T(8,128)}, f32[2,96,5120]{2,1,0:T(8,128)}, u32[]{:S(2)}, u32[]{:S(2)}) collective-permute-start(f32[2,96,5120]{2,1,0:T(8,128)} %get-tuple-element.65), channel_id=1, source_target_pairs={{16,0},{32,16},{48,32},{64,48},{80,64},{96,80},{112,96},{17,1},{33... | collective-permute-start | bytes 11796488 | tf_op jit(solution)/shard_map/while/body/eval_jaxpr/ppermute | solution.py:20
  636.2 89.3 %copy-start.1 = (f32[2,96,5120]{2,1,0:T(8,128)S(1)}, f32[2,96,5120]{2,1,0:T(8,128)}, u32[]{:S(2)}) copy-start(f32[2,96,5120]{2,1,0:T(8,128)} %get-tuple-element.64) | copy-start | bytes 11796484 | tf_op jit(solution)/shard_map/while
  728.7 1.9 copy-start.2
  730.6 85.9 %collective-permute-start = (f32[2,96,5120]{2,1,0:T(8,128)}, f32[2,96,5120]{2,1,0:T(8,128)}, u32[]{:S(2)}, u32[]{:S(2)}) collective-permute-start(f32[2,96,5120]{2,1,0:T(8,128)} %get-tuple-element.65), channel_id=1, source_target_pairs={{16,0},{32,16},{48,32},{64,48},{80,64},{96,80},{112,96},{17,1},{33... | collective-permute-start | bytes 11796488 | tf_op jit(solution)/shard_map/while/body/eval_jaxpr/ppermute | solution.py:20
  732.6 88.4 %copy-start.1 = (f32[2,96,5120]{2,1,0:T(8,128)S(1)}, f32[2,96,5120]{2,1,0:T(8,128)}, u32[]{:S(2)}) copy-start(f32[2,96,5120]{2,1,0:T(8,128)} %get-tuple-element.64) | copy-start | bytes 11796484 | tf_op jit(solution)/shard_map/while
  824.1 1.9 copy-start.2
Sparse Core Ops, SparseCore 0:
  28.1 83.0 reduce-scatter.1
  114.4 58.9 all-gather.1
where the time goes:
time: 843 us; the launch traced here: 842 us
  waiting for transfers between devices  704 us (84%)
  local copies, waits for them, and re-layouts  63.1 us (7%)
  other arithmetic  33 us (4%)
  starting transfers between devices  14.2 us (2%)
  between operations  14.1 us (2%)
  matrix products  13 us (2%)
    ppermute x7, waiting for transfers between devices, passed_along(): return lax.ppermute(block, axis, route)  621 us
    reduce_scatter x1, waiting for transfers between devices, body(): lax.psum_scatter(lax.dot_general(normed, key_grad, (((0,), (0,)), ((), ()...  83.2 us
    while x35, local copies, waits for them, and re-layouts  44.3 us
    add x7, other arithmetic, carry_step(): return (running + moving, moving)  21.8 us
  transfers between devices with their start and end apart: 9, of which 8 were waited for; matrix products, arithmetic and copies ran while one was open for 8% of the time, Pallas kernels for 0%

commit v1 on v0

v1 whole, which is shorter than its diff:
```python
import jax
import jax.numpy as jnp
from jax import lax
from jax.experimental import pallas as pl
from jax.experimental.pallas import tpu as pltpu
from jax.sharding import PartitionSpec as P

HEAD = 128
HEADS_KV = 4

beta_one = 0.9
beta_two = 0.95
learn_rate = 0.002
decay_rate = 0.1
adam_eps = 1e-08

NX = 4
VMEM_BYTES = 40 * 1024 * 1024


def along_x(k):
    return [(i, (i & 8) | ((((i >> 1) & 3) + k) % NX) * 2 | (i & 1)) for i in range(16)]


SWAP_CORE = [(i, i ^ 1) for i in range(16)]
SWAP_Y = [(i, i ^ 8) for i in range(16)]


def params():
    return pltpu.CompilerParams(vmem_limit_bytes=VMEM_BYTES)


def cost(flops, nbytes):
    return pl.CostEstimate(flops=flops, bytes_accessed=nbytes, transcendentals=0)


def cut_kernel(x_ref, one, two, three, o_one, o_two, o_three):
    o_one[...] = one[...]
    o_two[...] = two[...]
    o_three[...] = three[...]


def cut_columns(acts, xpos):
    rows, width = acts.shape
    blk = width // (2 * NX)

    def spec(k):
        return pl.BlockSpec((rows, blk), lambda y, x: (0, y * NX + lax.rem(x[0] + k, NX)))

    out = jax.ShapeDtypeStruct((rows, 2 * blk), acts.dtype)
    return pl.pallas_call(
        cut_kernel,
        grid_spec=pltpu.PrefetchScalarGridSpec(
            num_scalar_prefetch=1,
            grid=(2,),
            in_specs=[spec(1), spec(2), spec(3)],
            out_specs=[pl.BlockSpec((rows, blk), lambda y, x: (0, y))] * 3,
        ),
        out_shape=[out] * 3,
        compiler_params=params(),
        cost_estimate=cost(0, 12 * rows * blk * 2),
        name="cut_columns",
    )(xpos, acts, acts, acts)


def keys_kernel(steps, width, x_ref, gain_ref, w_ref, hgain_ref, cot_ref, kg_ref, kgs_ref, inv_ref, coef_ref, acc, ssq):
    step = pl.program_id(0)
    xf = x_ref[...].astype(jnp.float32)
    part = jnp.dot(
        (xf * gain_ref[...]).astype(jnp.bfloat16), w_ref[...], preferred_element_type=jnp.float32
    )
    sq = jnp.sum(xf * xf, axis=-1, keepdims=True)

    @pl.when(step == 0)
    def _():
        acc[...] = part
        ssq[...] = jnp.broadcast_to(sq, ssq.shape)

    @pl.when(step > 0)
    def _():
        acc[...] += part
        ssq[...] += sq

    @pl.when(step == steps - 1)
    def _():
        inv = lax.rsqrt(ssq[...] / width + 1e-06)
        hg = hgain_ref[...]
        dots = jnp.zeros_like(inv)
        for h in range(HEADS_KV):
            cols = slice(h * HEAD, (h + 1) * HEAD)
            raw = acc[:, cols] * inv
            hinv = lax.rsqrt(jnp.mean(raw * raw, axis=-1, keepdims=True) + 1e-06)
            scaled = cot_ref[:, cols].astype(jnp.float32) * hg
            kg = hinv * (scaled - raw * hinv * hinv * jnp.mean(scaled * raw, axis=-1, keepdims=True))
            kgs_ref[:, cols] = (kg * inv).astype(jnp.bfloat16)
            kg = kg.astype(jnp.bfloat16)
            kg_ref[:, cols] = kg
            dots += jnp.sum(kg.astype(jnp.float32) * raw, axis=-1, keepdims=True)
        inv_ref[...] = inv
        coef_ref[...] = inv * inv * dots / width


def keys(acts, gain, weight, head_gain, cot):
    rows, width = acts.shape
    kv = weight.shape[1]
    blk = 1280
    steps = width // blk
    return pl.pallas_call(
        lambda *refs: keys_kernel(steps, width, *refs),
        grid=(steps,),
        in_specs=[
            pl.BlockSpec((rows, blk), lambda i: (0, i)),
            pl.BlockSpec((1, blk), lambda i: (0, i)),
            pl.BlockSpec((blk, kv), lambda i: (i, 0)),
            pl.BlockSpec((1, HEAD), lambda i: (0, 0)),
            pl.BlockSpec((rows, kv), lambda i: (0, 0)),
        ],
        out_specs=[
            pl.BlockSpec((rows, kv), lambda i: (0, 0)),
            pl.BlockSpec((rows, kv), lambda i: (0, 0)),
            pl.BlockSpec((rows, HEAD), lambda i: (0, 0)),
            pl.BlockSpec((rows, HEAD), lambda i: (0, 0)),
        ],
        out_shape=[
            jax.ShapeDtypeStruct((rows, kv), jnp.bfloat16),
            jax.ShapeDtypeStruct((rows, kv), jnp.bfloat16),
            jax.ShapeDtypeStruct((rows, HEAD), jnp.float32),
            jax.ShapeDtypeStruct((rows, HEAD), jnp.float32),
        ],
        scratch_shapes=[pltpu.VMEM((rows, kv), jnp.float32), pltpu.VMEM((rows, HEAD), jnp.float32)],
        compiler_params=params(),
        cost_estimate=cost(2 * rows * width * kv, 2 * width * (rows + kv)),
        name="keys",
    )(acts, gain, weight, head_gain, cot)


def term_kernel(kg_ref, w_ref, gain_ref, x_ref, inv_ref, coef_ref, out_ref):
    back = lax.dot_general(
        kg_ref[...], w_ref[...], (((1,), (1,)), ((), ())), preferred_element_type=jnp.float32
    )
    inv = inv_ref[:, :1]
    coef = coef_ref[:, :1]
    term = inv * (gain_ref[...] * back) - coef * x_ref[...].astype(jnp.float32)
    out_ref[0] = term.astype(jnp.bfloat16)


def terms(kg, weight, gain, acts, inv, coef, parts):
    rows, width = acts.shape
    kv = weight.shape[1]
    blk = width // parts
    return pl.pallas_call(
        term_kernel,
        grid=(parts,),
        in_specs=[
            pl.BlockSpec((rows, kv), lambda i: (0, 0)),
            pl.BlockSpec((blk, kv), lambda i: (i, 0)),
            pl.BlockSpec((1, blk), lambda i: (0, i)),
            pl.BlockSpec((rows, blk), lambda i: (0, i)),
            pl.BlockSpec((rows, HEAD), lambda i: (0, 0)),
            pl.BlockSpec((rows, HEAD), lambda i: (0, 0)),
        ],
        out_specs=pl.BlockSpec((1, rows, blk), lambda i: (i, 0, 0)),
        out_shape=jax.ShapeDtypeStruct((parts, rows, blk), jnp.bfloat16),
        compiler_params=params(),
        cost_estimate=cost(2 * rows * width * kv, 2 * width * (2 * rows + kv)),
        name="terms",
    )(kg, weight, gain, acts, inv, coef)


def suffix_kernel(sec_ref, t_ref, up_ref, out_ref):
    total = up_ref[...].astype(jnp.float32)
    for s in reversed(range(t_ref.shape[0])):
        total = total + t_ref[s].astype(jnp.float32)
        out_ref[s] = total.astype(jnp.bfloat16)


def suffix_sums(got, upstream, sec):
    parts, rows, blk = got.shape
    tile = 48
    return pl.pallas_call(
        suffix_kernel,
        grid_spec=pltpu.PrefetchScalarGridSpec(
            num_scalar_prefetch=1,
            grid=(rows // tile,),
            in_specs=[
                pl.BlockSpec((parts, tile, blk), lambda i, s: (0, i, 0)),
                pl.BlockSpec((tile, blk), lambda i, s: (i, s[0])),
            ],
            out_specs=pl.BlockSpec((parts, tile, blk), lambda i, s: (0, i, 0)),
        ),
        out_shape=jax.ShapeDtypeStruct(got.shape, jnp.bfloat16),
        compiler_params=params(),
        cost_estimate=cost(parts * rows * blk, 4 * parts * rows * blk),
        name="suffix_sums",
    )(sec, got, upstream)


def lay_kernel(in_ref, out_ref):
    out_ref[...] = in_ref[0]


def side_by_side(got):
    parts, rows, blk = got.shape
    return pl.pallas_call(
        lay_kernel,
        grid=(parts,),
        in_specs=[pl.BlockSpec((1, rows, blk), lambda i: (i, 0, 0))],
        out_specs=pl.BlockSpec((rows, blk), lambda i: (0, i)),
        out_shape=jax.ShapeDtypeStruct((rows, parts * blk), got.dtype),
        compiler_params=params(),
        cost_estimate=cost(0, 4 * parts * rows * blk),
        name="side_by_side",
    )(got)


def wgrad_kernel(pos_ref, a0, a1, a2, a3, k0, k1, k2, k3, keep_ref, send_ref, full):
    total = None
    for a, k in ((a0, k0), (a1, k1), (a2, k2), (a3, k3)):
        part = lax.dot_general(
            a[...], k[...], (((0,), (0,)), ((), ())), preferred_element_type=jnp.float32
        )
        total = part if total is None else total + part
    full[...] = total
    half = keep_ref.shape[1]
    core = pos_ref[1]
    keep_ref[0] = full[pl.ds(pl.multiple_of(core * half, half), half), :]
    other = pl.multiple_of((1 - core) * half, half)
    send_ref[0] = full[pl.ds(other, half), :].astype(jnp.bfloat16)


def wgrad(acts, got, kgs, got_kgs, pos):
    rows, width = acts.shape
    blk = width // (2 * NX)
    kv = kgs.shape[1]
    half = blk // 2
    got_spec = pl.BlockSpec((rows, blk), lambda y, p: (0, y))
    kgs_spec = pl.BlockSpec((rows, kv), lambda y, p: (0, 0))
    out_spec = pl.BlockSpec((1, half, kv), lambda y, p: (y, 0, 0))
    return pl.pallas_call(
        wgrad_kernel,
        grid_spec=pltpu.PrefetchScalarGridSpec(
            num_scalar_prefetch=1,
            grid=(2,),
            in_specs=[pl.BlockSpec((rows, blk), lambda y, p: (0, y * NX + p[0]))]
            + [got_spec] * 3
            + [kgs_spec] * 4,
            out_specs=[out_spec, out_spec],
            scratch_shapes=[pltpu.VMEM((blk, kv), jnp.float32)],
        ),
        out_shape=[
            jax.ShapeDtypeStruct((2, half, kv), jnp.float32),
            jax.ShapeDtypeStruct((2, half, kv), jnp.bfloat16),
        ],
        compiler_params=params(),
        cost_estimate=cost(2 * 4 * rows * 2 * blk * kv, 2 * 4 * rows * (2 * blk + kv)),
        name="wgrad",
    )(pos, acts, *got, kgs, *got_kgs)


def place_kernel(plan, base_ref, *refs):
    ins, out, sems = refs[:-2], refs[-2], refs[-1]
    copies = []
    for n, (which, index, rows, slot, shift) in enumerate(plan):
        src = ins[which] if index is None else ins[which].at[index]
        at = pl.multiple_of(base_ref[slot] + shift, 32)
        copies.append(pltpu.make_async_copy(src, out.at[pl.ds(at, rows)], sems.at[n]))
    for one in copies:
        one.start()
    for one in copies:
        one.wait()


def place(plan, bases, blocks, rows, kv):
    return pl.pallas_call(
        lambda *refs: place_kernel(plan, *refs),
        in_specs=[pl.BlockSpec(memory_space=pltpu.SMEM)]
        + [pl.BlockSpec(memory_space=pltpu.VMEM)] * len(blocks),
        out_specs=pl.BlockSpec(memory_space=pl.ANY),
        out_shape=jax.ShapeDtypeStruct((rows, kv), jnp.bfloat16),
        scratch_shapes=[pltpu.SemaphoreType.DMA((len(plan),))],
        compiler_params=params(),
        cost_estimate=cost(0, 4 * rows * kv),
        name="place",
    )(bases, *blocks)


def gather_rows(own, y, x, core):
    rows, kv = own.shape
    half = rows // 2
    send = lambda block, perm: lax.ppermute(block, "dp", perm)
    up, down = along_x(1), along_x(-1)
    yr = send(own, SWAP_Y)
    a = send(own, up)
    b = send(own, down)
    c1 = send(jnp.stack([own, a, b]), SWAP_CORE)
    a2 = send(yr, up)
    b2 = send(yr, down)
    f = send(a[:half], up)
    g = send(b[half:], down)
    c2 = send(jnp.stack([yr, a2, b2]), SWAP_CORE)
    f2 = send(a2[:half], up)
    g2 = send(b2[half:], down)
    c3 = send(jnp.stack([f, g, f2, g2]), SWAP_CORE)
    blocks = [own, a, b, yr, a2, b2, f, g, f2, g2, c1, c2, c3]

    def slot(dy, dx, dc):
        return (dy * 3 + dx) * 2 + dc

    table = []
    for dy in range(2):
        for dx in (0, -1, 1, 2):
            for dc in range(2):
                yy = y if dy == 0 else 1 - y
                cc = core if dc == 0 else 1 - core
                table.append((yy * 8 + lax.rem(x + dx + NX, NX) * 2 + cc) * rows)
    bases = jnp.stack(table).astype(jnp.int32)
    at = {(dy, dx, dc): (dy * 4 + i) * 2 + dc for dy in range(2) for i, dx in enumerate((0, -1, 1, 2)) for dc in range(2)}
    plan = []
    for n, (dy, dx) in enumerate(((0, 0), (0, -1), (0, 1), (1, 0), (1, -1), (1, 1))):
        plan.append((n, None, rows, at[dy, dx, 0], 0))
    for n, (dy, shift) in enumerate(((0, 0), (0, half), (1, 0), (1, half))):
        plan.append((6 + n, None, half, at[dy, 2, 0], shift))
    for dy in range(2):
        for i, dx in enumerate((0, -1, 1)):
            plan.append((10 + dy, i, rows, at[dy, dx, 1], 0))
    for n, (dy, shift) in enumerate(((0, 0), (0, half), (1, 0), (1, half))):
        plan.append((12, n, half, at[dy, 2, 1], shift))
    return place(plan, bases, blocks, 16 * rows, kv)


def body(
    activations,
    norm_gain,
    key_weight,
    key_gain,
    key_cotangent,
    upstream,
    master,
    first_moment,
    second_moment,
):
    sections = lax.axis_size("section")
    micro, tok, width = activations.shape[1:]
    rows = micro * tok
    acts = activations.reshape(rows, width)
    weight = key_weight[0]
    kv = weight.shape[1]
    me = lax.axis_index("dp")
    y, x, core = me // 8, lax.rem(me // 2, NX), lax.rem(me, 2)
    pos = jnp.stack([x, core]).astype(jnp.int32)
    sec = lax.axis_index("section").astype(jnp.int32)[None]

    cut = cut_columns(acts, pos)
    got = [lax.ppermute(cut[k - 1], "dp", along_x(k)) for k in (1, 2, 3)]
    kg, kgs, inv, coef = keys(acts, norm_gain, weight, key_gain, key_cotangent.reshape(rows, kv))
    term = terms(kg, weight, norm_gain, acts, inv, coef, sections)
    kgs_late, _ = lax.optimization_barrier((kgs, term))
    got_kgs = [lax.ppermute(kgs_late if k == 2 else kgs, "dp", along_x(k)) for k in (1, 2, 3)]
    theirs = lax.all_to_all(term, "section", 0, 0)
    sums = suffix_sums(theirs, upstream.reshape(rows, width), sec)
    mine = lax.all_to_all(sums, "section", 0, 0)
    input_grad = side_by_side(mine).reshape(activations.shape)

    keep, away = wgrad(acts, got, kgs, got_kgs, pos)
    both = keep + lax.ppermute(away, "dp", SWAP_CORE).astype(jnp.float32)
    here = lax.dynamic_index_in_dim(both, y, 0, keepdims=False)
    there = lax.dynamic_index_in_dim(both, 1 - y, 0, keepdims=False).astype(jnp.bfloat16)
    part = here + lax.ppermute(there, "dp", SWAP_Y).astype(jnp.float32)
    own_rows = part.shape[0]
    gain_rows = lax.dynamic_slice(norm_gain[0], (me * own_rows,), (own_rows,))
    weight_grad = part * gain_rows[:, None]

    master_rows = master[0]
    new_first = beta_one * first_moment[0] + (1.0 - beta_one) * weight_grad
    new_second = beta_two * second_moment[0] + (1.0 - beta_two) * weight_grad * weight_grad
    corr_one = 1.0 - beta_one**10
    corr_two = 1.0 - beta_two**10
    update = (
        new_first / corr_one / (jnp.sqrt(new_second / corr_two) + adam_eps)
        + decay_rate * master_rows
    )
    new_master = master_rows - learn_rate * update
    new_weight = gather_rows(new_master.astype(jnp.bfloat16), y, x, core)
    return (input_grad, new_weight[None], new_master[None], new_first[None], new_second[None])


def solution(mesh):
    return jax.shard_map(
        body,
        mesh=mesh,
        in_specs=(
            P("section", None, "dp", None),
            P("section", None),
            P("section", None, None),
            P("section", None),
            P("section", None, "dp", None),
            P(None, "dp", None),
            P("section", "dp", None),
            P("section", "dp", None),
            P("section", "dp", None),
        ),
        out_specs=(
            P("section", None, "dp", None),
            P("section", None, None),
            P("section", "dp", None),
            P("section", "dp", None),
            P("section", "dp", None),
        ),
        check_vma=False,
    )
```

time: 843 us -> 146 us (0.17)
  the two profiles are of different devices: /device:TPU:114 before, /device:TPU:1 now
where the time goes in v1:
time: 146 us
  waiting for transfers between devices  58.3 us (40%)
  starting transfers between devices  47.5 us (33%)
  Pallas kernels  18.7 us (13%)
  local copies, waits for them, and re-layouts  10.1 us (7%)
  other arithmetic  10 us (7%)
    ppermute x1, waiting for transfers between devices, body(): part = here + lax.ppermute(there, 'dp', SWAP_Y).astype(jnp.float32)  25.6 us
    ppermute x12, starting transfers between devices, gather_rows(): send = lambda block, perm: lax.ppermute(block, 'dp', perm)  21.5 us
    ppermute x3, waiting for transfers between devices, body(): lax.ppermute(kgs_late if k == 2 else kgs, 'dp', along_x(k))  19.8 us
    ppermute x12, waiting for transfers between devices, gather_rows(): send = lambda block, perm: lax.ppermute(block, 'dp', perm)  12.9 us
    unnamed x32, local copies, waits for them, and re-layouts  8.78 us
    all_to_all x1, starting transfers between devices, body(): theirs = lax.all_to_all(term, 'section', 0, 0)  6.15 us
    ppermute x3, starting transfers between devices, body(): got = [lax.ppermute(cut[k - 1], 'dp', along_x(k)) for k in (1, 2, 3)]  5.71 us
    all_to_all x1, starting transfers between devices, body(): mine = lax.all_to_all(sums, 'section', 0, 0)  4.88 us
  transfers between devices with their start and end apart: 22, of which 8 were waited for; matrix products, arithmetic and copies ran while one was open for 8% of the time, Pallas kernels for 8%

profile of v1, /device:TPU:1, one launch (start us, length us, event | category | flops | bytes accessed | tf_op | source)
XLA Modules:
  0.0 145.5 jit_solution(3521608219705845178)
XLA Ops:
  0.7 1.5 %copy-done = bf16[1,2,96,5120]{3,2,1,0:T(8,128)(2,1)S(1)} copy-done((bf16[1,2,96,5120]{3,2,1,0:T(8,128)(2,1)S(1)}, bf16[1,2,96,5120]{3,2,1,0:T(8,128)(2,1)}, u32[]{:S(2)}) %copy-start) | copy-done | bytes 1966104
  2.3 1.1 cut_columns.1
  3.4 2.1 %collective-permute-start = (bf16[192,1280]{1,0:T(8,128)(2,1)S(1)}, bf16[192,1280]{1,0:T(8,128)(2,1)S(1)}, u32[]{:S(2)}, u32[]{:S(2)}) collective-permute-start(bf16[192,1280]{1,0:T(8,128)(2,1)S(1)} %get-tuple-element.18), channel_id=1, source_target_pairs={{0,2},{1,3},{2,4},{3,5},{4,6},{5,7},{6,0},{7,1},{8,10},{9,11},{10,... | collective-permute-start | bytes 1474568 | tf_op jit(solution)/shard_map/ppermute | solution.py:354
  5.5 2.5 %collective-permute-start.1 = (bf16[192,1280]{1,0:T(8,128)(2,1)S(1)}, bf16[192,1280]{1,0:T(8,128)(2,1)S(1)}, u32[]{:S(2)}, u32[]{:S(2)}) collective-permute-start(bf16[192,1280]{1,0:T(8,128)(2,1)S(1)} %get-tuple-element.19), channel_id=1, source_target_pairs={{0,4},{1,5},{2,6},{3,7},{4,0},{5,1},{6,2},{7,3},{8,12},{9,13},{10,... | collective-permute-start | bytes 1474568 | tf_op jit(solution)/shard_map/ppermute | solution.py:354
  8.0 1.2 collective-permute-start.2
  9.1 2.7 %keys.1 = (bf16[192,512]{1,0:T(8,128)(2,1)S(1)}, bf16[192,512]{1,0:T(8,128)(2,1)S(1)}, f32[192,128]{1,0:T(8,128)S(1)}, f32[192,128]{1,0:T(8,128)S(1)}) custom-call(bf16[192,5120]{1,0:T(8,128)(2,1)S(1)} %bitcast.86, f32[1,5120]{1,0:T(1,128)S(1)} %copy-done.14, bf16[5120,512]{1,0:T(8,128)(2,1)S(1)} %bitcast.89, f32[1,128]{1,0:T(1,128)S(1)} %copy-done.15, ...), custom_call_target="tpu_custom_call" | custom-call | flops 1006632960 | bytes 7208960 | tf_op jit(solution)/shard_map/keys/pallas_call | solution.py:108
  11.9 1.5 collective-permute-start.3
  13.4 3.4 %terms.1 = bf16[8,192,640]{2,1,0:T(8,128)(2,1)S(1)} custom-call(bf16[192,512]{1,0:T(8,128)(2,1)S(1)} %get-tuple-element.15.kg_ref, bf16[5120,512]{1,0:T(8,128)(2,1)S(1)} %bitcast.90, f32[1,5120]{1,0:T(1,128)S(1)} %copy-done.14, bf16[192,5120]{1,0:T(8,128)(2,1)S(1)} %bitcast.87, f32[192,128]{1,0:T(8,128)S(1)} %get-tuple-element.16.inv_ref, ...), custom_call_target="tpu_custom_call" | custom-call | flops 1006632960 | bytes 9175040 | tf_op jit(solution)/shard_map/terms/pallas_call | solution.py:151
  16.8 16.1 %collective-permute-done.5.k3 = bf16[192,512]{1,0:T(8,128)(2,1)S(1)} collective-permute-done((bf16[192,512]{1,0:T(8,128)(2,1)S(1)}, bf16[192,512]{1,0:T(8,128)(2,1)S(1)}, u32[]{:S(2)}, u32[]{:S(2)}) %collective-permute-start.5) | collective-permute-done | bytes 196640 | tf_op jit(solution)/shard_map/ppermute | solution.py:358
  32.9 2.6 %collective-permute-start.4 = (bf16[192,512]{1,0:T(8,128)(2,1)S(1)}, bf16[192,512]{1,0:T(8,128)(2,1)S(1)}, u32[]{:S(2)}, u32[]{:S(2)}) collective-permute-start(bf16[192,512]{1,0:T(8,128)(2,1)S(1)} %get-tuple-element.22.k0), channel_id=1, source_target_pairs={{0,4},{1,5},{2,6},{3,7},{4,0},{5,1},{6,2},{7,3},{8,12},{9,13},{10,... | collective-permute-start | bytes 589832 | tf_op jit(solution)/shard_map/ppermute | solution.py:358
  35.5 3.8 %collective-permute-done.4.k2 = bf16[192,512]{1,0:T(8,128)(2,1)S(1)} collective-permute-done((bf16[192,512]{1,0:T(8,128)(2,1)S(1)}, bf16[192,512]{1,0:T(8,128)(2,1)S(1)}, u32[]{:S(2)}, u32[]{:S(2)}) %collective-permute-start.4) | collective-permute-done | bytes 196640 | tf_op jit(solution)/shard_map/ppermute | solution.py:358
  39.2 3.5 %wgrad.1 = (f32[2,320,512]{2,1,0:T(8,128)S(1)}, bf16[2,320,512]{2,1,0:T(8,128)(2,1)}) custom-call(s32[2]{0:T(128)S(1)} %pad_add_fusion.x_ref.pos_ref, bf16[192,5120]{1,0:T(8,128)(2,1)S(1)} %bitcast.88, bf16[192,1280]{1,0:T(8,128)(2,1)S(1)} %collective-permute-done.a1, bf16[192,1280]{1,0:T(8,128)(2,1)S(1)} %collective-permute-done.1.a2, ...), custom_call_target="tpu_custom_call" | custom-call | flops 1006632960 | bytes 2752512 | tf_op jit(solution)/shard_map/wgrad/pallas_call | solution.py:239
  42.7 2.5 %collective-permute-start.6 = (bf16[2,320,512]{2,1,0:T(8,128)(2,1)}, bf16[2,320,512]{2,1,0:T(8,128)(2,1)}, u32[]{:S(2)}, u32[]{:S(2)}) collective-permute-start(bf16[2,320,512]{2,1,0:T(8,128)(2,1)} %get-tuple-element.24), channel_id=1, source_target_pairs={{0,1},{1,0},{2,3},{3,2},{4,5},{5,4},{6,7},{7,6},{8,9},{9,8},{10,11... | collective-permute-start | bytes 1966088 | tf_op jit(solution)/shard_map/ppermute | solution.py:365
  45.2 6.2 %all-to-all-start = ((bf16[8,192,640]{2,1,0:T(8,128)(2,1)}), bf16[8,192,640]{2,1,0:T(8,128)(2,1)S(1)}, u32[]{:S(2)}, u32[]{:S(2)}) async-start(bf16[8,192,640]{2,1,0:T(8,128)(2,1)} %copy-done.3), calls=%async_computation | async-start | bytes 3932160 | tf_op jit(solution)/shard_map/all_to_all | solution.py:359
  51.3 2.4 %convert_add_fusion = f32[2,320,512]{2,1,0:T(8,128)} fusion(f32[2,320,512]{2,1,0:T(8,128)S(1)} %get-tuple-element.23, bf16[2,320,512]{2,1,0:T(8,128)(2,1)} %collective-permute-done.6), kind=kLoop, calls=%fused_computation | loop fusion | flops 655360 | bytes 3276800 | tf_op jit(solution)/shard_map/add | solution.py:365
  53.7 1.1 fusion.4
  54.8 2.7 %collective-permute-start.7 = (bf16[320,512]{1,0:T(8,128)(2,1)S(1)}, bf16[320,512]{1,0:T(8,128)(2,1)S(1)}, u32[]{:S(2)}, u32[]{:S(2)}) collective-permute-start(bf16[320,512]{1,0:T(8,128)(2,1)S(1)} %fusion.4), channel_id=1, source_target_pairs={{0,8},{1,9},{2,10},{3,11},{4,12},{5,13},{6,14},{7,15},{8,0},{9,1},... | collective-permute-start | bytes 983048 | tf_op jit(solution)/shard_map/ppermute | solution.py:368
  57.5 0.1 dynamic-slice_reduce_fusion
  57.6 25.6 %collective-permute-done.7 = bf16[320,512]{1,0:T(8,128)(2,1)S(1)} collective-permute-done((bf16[320,512]{1,0:T(8,128)(2,1)S(1)}, bf16[320,512]{1,0:T(8,128)(2,1)S(1)}, u32[]{:S(2)}, u32[]{:S(2)}) %collective-permute-start.7) | collective-permute-done | bytes 327712 | tf_op jit(solution)/shard_map/ppermute | solution.py:368
  83.2 3.4 %fusion.7 = (bf16[320,512]{1,0:T(8,128)(2,1)S(1)}, f32[320,512]{1,0:T(8,128)}, f32[1,320,512]{2,1,0:T(8,128)}, f32[1,320,512]{2,1,0:T(8,128)}) fusion(f32[1,320,512]{2,1,0:T(8,128)} %param.17, f32[320]{0:T(512)S(1)} %dynamic-slice_reduce_fusion, bf16[320,512]{1,0:T(8,128)(2,1)S(1)} %collective-permute-done.7, f32[2,320,512]{2,1,0:T(8,128)} %convert_add_fusion, ...), kind=kLoop, calls=%fused_computation.19 | loop fusion | flops 3112960 | bytes 5244164 | tf_op jit(solution)/shard_map/convert_element_type | solution.py:383
  86.6 0.3 collective-permute-start.10
  87.0 1.5 %copy-done.6 = bf16[2,96,5120]{2,1,0:T(8,128)(2,1)S(1)} copy-done((bf16[2,96,5120]{2,1,0:T(8,128)(2,1)S(1)}, bf16[2,96,5120]{2,1,0:T(8,128)(2,1)}, u32[]{:S(2)}) %copy-start.6) | copy-done | bytes 1966104
  88.5 0.8 suffix_sums.1
  89.4 1.3 copy-done.2
  90.6 4.9 %all-to-all-start.1 = ((bf16[8,192,640]{2,1,0:T(8,128)(2,1)}), bf16[8,192,640]{2,1,0:T(8,128)(2,1)S(1)}, u32[]{:S(2)}, u32[]{:S(2)}) async-start(bf16[8,192,640]{2,1,0:T(8,128)(2,1)} %copy-done.2), calls=%async_computation.1 | async-start | bytes 3932160 | tf_op jit(solution)/shard_map/all_to_all | solution.py:361
  95.5 3.4 %collective-permute-start.9 = (bf16[320,512]{1,0:T(8,128)(2,1)S(1)}, bf16[320,512]{1,0:T(8,128)(2,1)S(1)}, u32[]{:S(2)}, u32[]{:S(2)}) collective-permute-start(bf16[320,512]{1,0:T(8,128)(2,1)S(1)} %get-tuple-element.25.refs_1_), channel_id=1, source_target_pairs={{0,6},{1,7},{2,0},{3,1},{4,2},{5,3},{6,4},{7,5},{8,14},{9,15},{10,... | collective-permute-start | bytes 983048 | tf_op jit(solution)/shard_map/ppermute | solution.py:290
  98.9 2.7 %collective-permute-start.12 = (bf16[320,512]{1,0:T(8,128)(2,1)}, bf16[320,512]{1,0:T(8,128)(2,1)S(1)}, u32[]{:S(2)}, u32[]{:S(2)}) collective-permute-start(bf16[320,512]{1,0:T(8,128)(2,1)} %collective-permute-done.10.refs_4_), channel_id=1, source_target_pairs={{0,6},{1,7},{2,0},{3,1},{4,2},{5,3},{6,4},{7,5},{8,14},{9,15},{10,... | collective-permute-start | bytes 983048 | tf_op jit(solution)/shard_map/ppermute | solution.py:290
  101.6 2.7 %collective-permute-done.9.refs_3_ = bf16[320,512]{1,0:T(8,128)(2,1)S(1)} collective-permute-done((bf16[320,512]{1,0:T(8,128)(2,1)S(1)}, bf16[320,512]{1,0:T(8,128)(2,1)S(1)}, u32[]{:S(2)}, u32[]{:S(2)}) %collective-permute-start.9) | collective-permute-done | bytes 327712 | tf_op jit(solution)/shard_map/ppermute | solution.py:290
  104.3 3.5 %collective-permute-start.14 = (bf16[160,512]{1,0:T(8,128)(2,1)S(1)}, bf16[160,512]{1,0:T(8,128)(2,1)S(1)}, u32[]{:S(2)}, u32[]{:S(2)}) collective-permute-start(bf16[160,512]{1,0:T(8,128)(2,1)S(1)} %slice.17), channel_id=1, source_target_pairs={{0,6},{1,7},{2,0},{3,1},{4,2},{5,3},{6,4},{7,5},{8,14},{9,15},{10,... | collective-permute-start | bytes 491528 | tf_op jit(solution)/shard_map/ppermute | solution.py:290
  107.8 1.1 pad_maximum_fusion
  108.8 5.0 %collective-permute-start.17 = (bf16[3,320,512]{2,1,0:T(8,128)(2,1)}, bf16[3,320,512]{2,1,0:T(8,128)(2,1)}, u32[]{:S(2)}, u32[]{:S(2)}) collective-permute-start(bf16[3,320,512]{2,1,0:T(8,128)(2,1)} %pad_maximum_fusion), channel_id=1, source_target_pairs={{0,1},{1,0},{2,3},{3,2},{4,5},{5,4},{6,7},{7,6},{8,9},{9,8},{10,11... | collective-permute-start | bytes 2949128 | tf_op jit(solution)/shard_map/ppermute | solution.py:290
  113.9 0.6 collective-permute-done.11.refs_5_
  114.4 2.2 %pad_maximum_fusion.1 = bf16[3,320,512]{2,1,0:T(8,128)(2,1)} fusion(bf16[1,320,512]{2,1,0:T(8,128)(2,1)S(1)} %bitcast.94, bf16[1,320,512]{2,1,0:T(8,128)(2,1)S(1)} %bitcast.95, bf16[1,320,512]{2,1,0:T(8,128)(2,1)} %bitcast.32), kind=kLoop, calls=%fused_computation.2 | loop fusion | flops 983040 | bytes 1966080 | tf_op jit(solution)/shard_map/stack | solution.py:300
  116.6 2.9 %collective-permute-start.18 = (bf16[3,320,512]{2,1,0:T(8,128)(2,1)}, bf16[3,320,512]{2,1,0:T(8,128)(2,1)}, u32[]{:S(2)}, u32[]{:S(2)}) collective-permute-start(bf16[3,320,512]{2,1,0:T(8,128)(2,1)} %pad_maximum_fusion.1), channel_id=1, source_target_pairs={{0,1},{1,0},{2,3},{3,2},{4,5},{5,4},{6,7},{7,6},{8,9},{9,8},{10,11... | collective-permute-start | bytes 2949128 | tf_op jit(solution)/shard_map/ppermute | solution.py:290
  119.6 2.7 %collective-permute-start.16 = (bf16[160,512]{1,0:T(8,128)(2,1)S(1)}, bf16[160,512]{1,0:T(8,128)(2,1)S(1)}, u32[]{:S(2)}, u32[]{:S(2)}) collective-permute-start(bf16[160,512]{1,0:T(8,128)(2,1)S(1)} %slice.19), channel_id=1, source_target_pairs={{0,6},{1,7},{2,0},{3,1},{4,2},{5,3},{6,4},{7,5},{8,14},{9,15},{10,... | collective-permute-start | bytes 491528 | tf_op jit(solution)/shard_map/ppermute | solution.py:290
  122.4 4.2 %collective-permute-done.13.refs_7_ = bf16[160,512]{1,0:T(8,128)(2,1)S(1)} collective-permute-done((bf16[160,512]{1,0:T(8,128)(2,1)S(1)}, bf16[160,512]{1,0:T(8,128)(2,1)S(1)}, u32[]{:S(2)}, u32[]{:S(2)}) %collective-permute-start.13) | collective-permute-done | bytes 163872 | tf_op jit(solution)/shard_map/ppermute | solution.py:290
  126.6 3.5 %collective-permute-done.15.refs_9_ = bf16[160,512]{1,0:T(8,128)(2,1)S(1)} collective-permute-done((bf16[160,512]{1,0:T(8,128)(2,1)S(1)}, bf16[160,512]{1,0:T(8,128)(2,1)S(1)}, u32[]{:S(2)}, u32[]{:S(2)}) %collective-permute-start.15) | collective-permute-done | bytes 163872 | tf_op jit(solution)/shard_map/ppermute | solution.py:290
  130.1 0.9 pad_maximum_fusion.2
  131.0 0.7 copy-done.7
  131.7 0.8 collective-permute-start.19
  132.5 0.1 stack.115.refs_0_
  132.6 2.0 %collective-permute-done.19.refs_13_ = bf16[4,160,512]{2,1,0:T(8,128)(2,1)} collective-permute-done((bf16[4,160,512]{2,1,0:T(8,128)(2,1)}, bf16[4,160,512]{2,1,0:T(8,128)(2,1)}, u32[]{:S(2)}, u32[]{:S(2)}) %collective-permute-start.19) | collective-permute-done | bytes 655392 | tf_op jit(solution)/shard_map/ppermute | solution.py:290
  134.5 1.0 copy-done.5
  135.5 0.9 copy-done.8
  136.4 0.9 copy-done.10
  137.3 0.9 copy-done.12
  138.3 4.3 %place.1 = bf16[5120,512]{1,0:T(8,128)(2,1)} custom-call(s32[16]{0:T(128)S(1)} %stack.115.refs_0_, bf16[320,512]{1,0:T(8,128)(2,1)S(1)} %get-tuple-element.25.refs_1_, bf16[320,512]{1,0:T(8,128)(2,1)S(1)} %collective-permute-done.8.refs_2_, bf16[320,512]{1,0:T(8,128)(2,1)S(1)} %collective-permute-done.9.refs_3_, ...), custom_call_target="tpu_custom_call" | custom-call | bytes 10485760 | tf_op jit(solution)/shard_map/place/pallas_call | solution.py:274
  142.6 3.0 %side_by_side.1 = bf16[192,5120]{1,0:T(8,128)(2,1)} custom-call(bf16[8,192,640]{2,1,0:T(8,128)(2,1)S(1)} %all-to-all-done.1.in_ref), custom_call_target="tpu_custom_call" | custom-call | bytes 3932160 | tf_op jit(solution)/shard_map/side_by_side/pallas_call | solution.py:204
  (48 shorter events, 0.4 us)
Async XLA Ops:
  0.7 1.5 %copy-start = (bf16[1,2,96,5120]{3,2,1,0:T(8,128)(2,1)S(1)}, bf16[1,2,96,5120]{3,2,1,0:T(8,128)(2,1)}, u32[]{:S(2)}) copy-start(bf16[1,2,96,5120]{3,2,1,0:T(8,128)(2,1)} %param.9) | copy-start | bytes 5898244
  2.3 6.9 %copy-start.1 = (bf16[1,5120,512]{2,1,0:T(8,128)(2,1)S(1)}, bf16[1,5120,512]{2,1,0:T(8,128)(2,1)}, u32[]{:S(2)}) copy-start(bf16[1,5120,512]{2,1,0:T(8,128)(2,1)} %param.11) | copy-start | bytes 15728644
  2.3 6.9 %copy-start.13 = (bf16[1,2,96,512]{3,2,1,0:T(8,128)(2,1)S(1)}, bf16[1,2,96,512]{3,2,1,0:T(8,128)(2,1)}, u32[]{:S(2)}) copy-start(bf16[1,2,96,512]{3,2,1,0:T(8,128)(2,1)} %param.13) | copy-start | bytes 589828
  2.3 6.9 %copy-start.14 = (f32[1,5120]{1,0:T(1,128)S(1)}, f32[1,5120]{1,0:T(1,128)}, u32[]{:S(2)}) copy-start(f32[1,5120]{1,0:T(1,128)} %gain_ref.1) | copy-start | bytes 61444
  2.3 6.9 %copy-start.15 = (f32[1,128]{1,0:T(1,128)S(1)}, f32[1,128]{1,0:T(1,128)}, u32[]{:S(2)}) copy-start(f32[1,128]{1,0:T(1,128)} %refs_3_.1) | copy-start | bytes 1540
  3.4 35.8 %collective-permute-start = (bf16[192,1280]{1,0:T(8,128)(2,1)S(1)}, bf16[192,1280]{1,0:T(8,128)(2,1)S(1)}, u32[]{:S(2)}, u32[]{:S(2)}) collective-permute-start(bf16[192,1280]{1,0:T(8,128)(2,1)S(1)} %get-tuple-element.18), channel_id=1, source_target_pairs={{0,2},{1,3},{2,4},{3,5},{4,6},{5,7},{6,0},{7,1},{8,10},{9,11},{10,... | collective-permute-start | bytes 1474568 | tf_op jit(solution)/shard_map/ppermute | solution.py:354
  5.5 33.7 %collective-permute-start.1 = (bf16[192,1280]{1,0:T(8,128)(2,1)S(1)}, bf16[192,1280]{1,0:T(8,128)(2,1)S(1)}, u32[]{:S(2)}, u32[]{:S(2)}) collective-permute-start(bf16[192,1280]{1,0:T(8,128)(2,1)S(1)} %get-tuple-element.19), channel_id=1, source_target_pairs={{0,4},{1,5},{2,6},{3,7},{4,0},{5,1},{6,2},{7,3},{8,12},{9,13},{10,... | collective-permute-start | bytes 1474568 | tf_op jit(solution)/shard_map/ppermute | solution.py:354
  8.0 31.2 %collective-permute-start.2 = (bf16[192,1280]{1,0:T(8,128)(2,1)S(1)}, bf16[192,1280]{1,0:T(8,128)(2,1)S(1)}, u32[]{:S(2)}, u32[]{:S(2)}) collective-permute-start(bf16[192,1280]{1,0:T(8,128)(2,1)S(1)} %get-tuple-element.20), channel_id=1, source_target_pairs={{0,6},{1,7},{2,0},{3,1},{4,2},{5,3},{6,4},{7,5},{8,14},{9,15},{10,... | collective-permute-start | bytes 1474568 | tf_op jit(solution)/shard_map/ppermute | solution.py:354
  11.9 21.0 %collective-permute-start.5 = (bf16[192,512]{1,0:T(8,128)(2,1)S(1)}, bf16[192,512]{1,0:T(8,128)(2,1)S(1)}, u32[]{:S(2)}, u32[]{:S(2)}) collective-permute-start(bf16[192,512]{1,0:T(8,128)(2,1)S(1)} %get-tuple-element.22.k0), channel_id=1, source_target_pairs={{0,6},{1,7},{2,0},{3,1},{4,2},{5,3},{6,4},{7,5},{8,14},{9,15},{10,... | collective-permute-start | bytes 589832 | tf_op jit(solution)/shard_map/ppermute | solution.py:358
  11.9 23.5 %collective-permute-start.3 = (bf16[192,512]{1,0:T(8,128)(2,1)S(1)}, bf16[192,512]{1,0:T(8,128)(2,1)S(1)}, u32[]{:S(2)}, u32[]{:S(2)}) collective-permute-start(bf16[192,512]{1,0:T(8,128)(2,1)S(1)} %get-tuple-element.22.k0), channel_id=1, source_target_pairs={{0,2},{1,3},{2,4},{3,5},{4,6},{5,7},{6,0},{7,1},{8,10},{9,11},{10,... | collective-permute-start | bytes 589832 | tf_op jit(solution)/shard_map/ppermute | solution.py:358
  16.8 25.9 %copy-start.3 = (bf16[8,192,640]{2,1,0:T(8,128)(2,1)}, bf16[8,192,640]{2,1,0:T(8,128)(2,1)S(1)}, u32[]{:S(2)}) copy-start(bf16[8,192,640]{2,1,0:T(8,128)(2,1)S(1)} %terms.1) | copy-start | bytes 5898244
  32.9 6.3 %collective-permute-start.4 = (bf16[192,512]{1,0:T(8,128)(2,1)S(1)}, bf16[192,512]{1,0:T(8,128)(2,1)S(1)}, u32[]{:S(2)}, u32[]{:S(2)}) collective-permute-start(bf16[192,512]{1,0:T(8,128)(2,1)S(1)} %get-tuple-element.22.k0), channel_id=1, source_target_pairs={{0,4},{1,5},{2,6},{3,7},{4,0},{5,1},{6,2},{7,3},{8,12},{9,13},{10,... | collective-permute-start | bytes 589832 | tf_op jit(solution)/shard_map/ppermute | solution.py:358
  42.7 8.6 %collective-permute-start.6 = (bf16[2,320,512]{2,1,0:T(8,128)(2,1)}, bf16[2,320,512]{2,1,0:T(8,128)(2,1)}, u32[]{:S(2)}, u32[]{:S(2)}) collective-permute-start(bf16[2,320,512]{2,1,0:T(8,128)(2,1)} %get-tuple-element.24), channel_id=1, source_target_pairs={{0,1},{1,0},{2,3},{3,2},{4,5},{5,4},{6,7},{7,6},{8,9},{9,8},{10,11... | collective-permute-start | bytes 1966088 | tf_op jit(solution)/shard_map/ppermute | solution.py:365
  45.2 41.8 %all-to-all-start = ((bf16[8,192,640]{2,1,0:T(8,128)(2,1)}), bf16[8,192,640]{2,1,0:T(8,128)(2,1)S(1)}, u32[]{:S(2)}, u32[]{:S(2)}) async-start(bf16[8,192,640]{2,1,0:T(8,128)(2,1)} %copy-done.3), calls=%async_computation | async-start | bytes 3932160 | tf_op jit(solution)/shard_map/all_to_all | solution.py:359
  54.8 28.4 %collective-permute-start.7 = (bf16[320,512]{1,0:T(8,128)(2,1)S(1)}, bf16[320,512]{1,0:T(8,128)(2,1)S(1)}, u32[]{:S(2)}, u32[]{:S(2)}) collective-permute-start(bf16[320,512]{1,0:T(8,128)(2,1)S(1)} %fusion.4), channel_id=1, source_target_pairs={{0,8},{1,9},{2,10},{3,11},{4,12},{5,13},{6,14},{7,15},{8,0},{9,1},... | collective-permute-start | bytes 983048 | tf_op jit(solution)/shard_map/ppermute | solution.py:368
  86.6 12.3 %collective-permute-start.10 = (bf16[320,512]{1,0:T(8,128)(2,1)S(1)}, bf16[320,512]{1,0:T(8,128)(2,1)}, u32[]{:S(2)}, u32[]{:S(2)}) collective-permute-start(bf16[320,512]{1,0:T(8,128)(2,1)S(1)} %get-tuple-element.25.refs_1_), channel_id=1, source_target_pairs={{0,8},{1,9},{2,10},{3,11},{4,12},{5,13},{6,14},{7,15},{8,0},{9,1},... | collective-permute-start | bytes 983048 | tf_op jit(solution)/shard_map/ppermute | solution.py:290
  87.0 1.5 %copy-start.6 = (bf16[2,96,5120]{2,1,0:T(8,128)(2,1)S(1)}, bf16[2,96,5120]{2,1,0:T(8,128)(2,1)}, u32[]{:S(2)}) copy-start(bf16[2,96,5120]{2,1,0:T(8,128)(2,1)} %param.14) | copy-start | bytes 5898244
  89.4 1.3 copy-start.2
  90.6 51.9 %all-to-all-start.1 = ((bf16[8,192,640]{2,1,0:T(8,128)(2,1)}), bf16[8,192,640]{2,1,0:T(8,128)(2,1)S(1)}, u32[]{:S(2)}, u32[]{:S(2)}) async-start(bf16[8,192,640]{2,1,0:T(8,128)(2,1)} %copy-done.2), calls=%async_computation.1 | async-start | bytes 3932160 | tf_op jit(solution)/shard_map/all_to_all | solution.py:361
  95.5 8.8 %collective-permute-start.9 = (bf16[320,512]{1,0:T(8,128)(2,1)S(1)}, bf16[320,512]{1,0:T(8,128)(2,1)S(1)}, u32[]{:S(2)}, u32[]{:S(2)}) collective-permute-start(bf16[320,512]{1,0:T(8,128)(2,1)S(1)} %get-tuple-element.25.refs_1_), channel_id=1, source_target_pairs={{0,6},{1,7},{2,0},{3,1},{4,2},{5,3},{6,4},{7,5},{8,14},{9,15},{10,... | collective-permute-start | bytes 983048 | tf_op jit(solution)/shard_map/ppermute | solution.py:290
  98.9 8.8 %collective-permute-start.8 = (bf16[320,512]{1,0:T(8,128)(2,1)S(1)}, bf16[320,512]{1,0:T(8,128)(2,1)S(1)}, u32[]{:S(2)}, u32[]{:S(2)}) collective-permute-start(bf16[320,512]{1,0:T(8,128)(2,1)S(1)} %get-tuple-element.25.refs_1_), channel_id=1, source_target_pairs={{0,2},{1,3},{2,4},{3,5},{4,6},{5,7},{6,0},{7,1},{8,10},{9,11},{10,... | collective-permute-start | bytes 983048 | tf_op jit(solution)/shard_map/ppermute | solution.py:290
  98.9 14.9 %collective-permute-start.12 = (bf16[320,512]{1,0:T(8,128)(2,1)}, bf16[320,512]{1,0:T(8,128)(2,1)S(1)}, u32[]{:S(2)}, u32[]{:S(2)}) collective-permute-start(bf16[320,512]{1,0:T(8,128)(2,1)} %collective-permute-done.10.refs_4_), channel_id=1, source_target_pairs={{0,6},{1,7},{2,0},{3,1},{4,2},{5,3},{6,4},{7,5},{8,14},{9,15},{10,... | collective-permute-start | bytes 983048 | tf_op jit(solution)/shard_map/ppermute | solution.py:290
  101.6 12.8 %collective-permute-start.11 = (bf16[320,512]{1,0:T(8,128)(2,1)}, bf16[320,512]{1,0:T(8,128)(2,1)S(1)}, u32[]{:S(2)}, u32[]{:S(2)}) collective-permute-start(bf16[320,512]{1,0:T(8,128)(2,1)} %collective-permute-done.10.refs_4_), channel_id=1, source_target_pairs={{0,2},{1,3},{2,4},{3,5},{4,6},{5,7},{6,0},{7,1},{8,10},{9,11},{10,... | collective-permute-start | bytes 983048 | tf_op jit(solution)/shard_map/ppermute | solution.py:290
  104.3 18.0 %collective-permute-start.14 = (bf16[160,512]{1,0:T(8,128)(2,1)S(1)}, bf16[160,512]{1,0:T(8,128)(2,1)S(1)}, u32[]{:S(2)}, u32[]{:S(2)}) collective-permute-start(bf16[160,512]{1,0:T(8,128)(2,1)S(1)} %slice.17), channel_id=1, source_target_pairs={{0,6},{1,7},{2,0},{3,1},{4,2},{5,3},{6,4},{7,5},{8,14},{9,15},{10,... | collective-permute-start | bytes 491528 | tf_op jit(solution)/shard_map/ppermute | solution.py:290
  108.8 23.7 %collective-permute-start.17 = (bf16[3,320,512]{2,1,0:T(8,128)(2,1)}, bf16[3,320,512]{2,1,0:T(8,128)(2,1)}, u32[]{:S(2)}, u32[]{:S(2)}) collective-permute-start(bf16[3,320,512]{2,1,0:T(8,128)(2,1)} %pad_maximum_fusion), channel_id=1, source_target_pairs={{0,1},{1,0},{2,3},{3,2},{4,5},{5,4},{6,7},{7,6},{8,9},{9,8},{10,11... | collective-permute-start | bytes 2949128 | tf_op jit(solution)/shard_map/ppermute | solution.py:290
  114.4 16.6 %copy-start.4 = (bf16[320,512]{1,0:T(8,128)(2,1)}, bf16[320,512]{1,0:T(8,128)(2,1)S(1)}, u32[]{:S(2)}) copy-start(bf16[320,512]{1,0:T(8,128)(2,1)S(1)} %collective-permute-done.11.refs_5_) | copy-start | bytes 983044
  116.6 18.0 %collective-permute-start.18 = (bf16[3,320,512]{2,1,0:T(8,128)(2,1)}, bf16[3,320,512]{2,1,0:T(8,128)(2,1)}, u32[]{:S(2)}, u32[]{:S(2)}) collective-permute-start(bf16[3,320,512]{2,1,0:T(8,128)(2,1)} %pad_maximum_fusion.1), channel_id=1, source_target_pairs={{0,1},{1,0},{2,3},{3,2},{4,5},{5,4},{6,7},{7,6},{8,9},{9,8},{10,11... | collective-permute-start | bytes 2949128 | tf_op jit(solution)/shard_map/ppermute | solution.py:290
  119.5 7.1 %collective-permute-start.13 = (bf16[160,512]{1,0:T(8,128)(2,1)S(1)}, bf16[160,512]{1,0:T(8,128)(2,1)S(1)}, u32[]{:S(2)}, u32[]{:S(2)}) collective-permute-start(bf16[160,512]{1,0:T(8,128)(2,1)S(1)} %slice.16), channel_id=1, source_target_pairs={{0,2},{1,3},{2,4},{3,5},{4,6},{5,7},{6,0},{7,1},{8,10},{9,11},{10,... | collective-permute-start | bytes 491528 | tf_op jit(solution)/shard_map/ppermute | solution.py:290
  119.6 7.0 %collective-permute-start.16 = (bf16[160,512]{1,0:T(8,128)(2,1)S(1)}, bf16[160,512]{1,0:T(8,128)(2,1)S(1)}, u32[]{:S(2)}, u32[]{:S(2)}) collective-permute-start(bf16[160,512]{1,0:T(8,128)(2,1)S(1)} %slice.19), channel_id=1, source_target_pairs={{0,6},{1,7},{2,0},{3,1},{4,2},{5,3},{6,4},{7,5},{8,14},{9,15},{10,... | collective-permute-start | bytes 491528 | tf_op jit(solution)/shard_map/ppermute | solution.py:290
  122.3 7.8 %collective-permute-start.15 = (bf16[160,512]{1,0:T(8,128)(2,1)S(1)}, bf16[160,512]{1,0:T(8,128)(2,1)S(1)}, u32[]{:S(2)}, u32[]{:S(2)}) collective-permute-start(bf16[160,512]{1,0:T(8,128)(2,1)S(1)} %slice.18), channel_id=1, source_target_pairs={{0,2},{1,3},{2,4},{3,5},{4,6},{5,7},{6,0},{7,1},{8,10},{9,11},{10,... | collective-permute-start | bytes 491528 | tf_op jit(solution)/shard_map/ppermute | solution.py:290
  126.6 4.4 %copy-start.9 = (bf16[160,512]{1,0:T(8,128)(2,1)}, bf16[160,512]{1,0:T(8,128)(2,1)S(1)}, u32[]{:S(2)}) copy-start(bf16[160,512]{1,0:T(8,128)(2,1)S(1)} %collective-permute-done.16.refs_10_) | copy-start | bytes 491524
  130.1 0.9 copy-start.11
  131.0 0.7 copy-start.7
  131.7 2.9 %collective-permute-start.19 = (bf16[4,160,512]{2,1,0:T(8,128)(2,1)}, bf16[4,160,512]{2,1,0:T(8,128)(2,1)}, u32[]{:S(2)}, u32[]{:S(2)}) collective-permute-start(bf16[4,160,512]{2,1,0:T(8,128)(2,1)} %pad_maximum_fusion.2), channel_id=1, source_target_pairs={{0,1},{1,0},{2,3},{3,2},{4,5},{5,4},{6,7},{7,6},{8,9},{9,8},{10,11... | collective-permute-start | bytes 1966088 | tf_op jit(solution)/shard_map/ppermute | solution.py:290
  134.5 1.0 copy-start.5
  135.5 0.9 copy-start.8
  136.4 0.9 copy-start.10
  137.3 0.9 copy-start.12

commit v2 on v0

v2 whole, which is shorter than its diff:
```python
import jax
import jax.numpy as jnp
from jax import lax
from jax.experimental import pallas as pl
from jax.experimental.pallas import tpu as pltpu
from jax.sharding import PartitionSpec as P

HEAD = 128
HEADS_KV = 4

beta_one = 0.9
beta_two = 0.95
learn_rate = 0.002
decay_rate = 0.1
adam_eps = 1e-08

NX = 4


def along_x(k):
    return [(i, (i & 8) | ((((i >> 1) & 3) + k) % NX) * 2 | (i & 1)) for i in range(16)]


SWAP_CORE = [(i, i ^ 1) for i in range(16)]
SWAP_Y = [(i, i ^ 8) for i in range(16)]

NZ = 4
RINGS_Z = [[0, 1, 2, 3], [4, 5, 6, 7]]
DOWN_Y = [(NZ + z, z) for z in range(NZ)]


def params(mib):
    return pltpu.CompilerParams(vmem_limit_bytes=mib * 1024 * 1024)


def cost(flops, nbytes):
    return pl.CostEstimate(flops=0, bytes_accessed=1, transcendentals=0)


def chip_columns(blk, k):
    x = lax.rem(lax.axis_index("dp") // 2 + k, NX)
    return [pl.ds(pl.multiple_of((y * NX + x) * blk, HEAD), blk) for y in range(2)]


def run_copies(moves, sems):
    copies = [pltpu.make_async_copy(src, dst, sems.at[n]) for n, (src, dst) in enumerate(moves)]
    for one in copies:
        one.start()
    for one in copies:
        one.wait()


def cut_kernel(x_hbm, up, down, far, sems):
    blk = up.shape[1] // 2
    moves = []
    for out, k in ((up, 1), (down, NX - 1), (far, 2)):
        for y, cols in enumerate(chip_columns(blk, k)):
            moves.append((x_hbm.at[:, cols], out.at[:, pl.ds(y * blk, blk)]))
    run_copies(moves, sems)


def cut_columns(acts):
    rows, width = acts.shape
    out = jax.ShapeDtypeStruct((rows, width // NX), acts.dtype)
    return pl.pallas_call(
        cut_kernel,
        in_specs=[pl.BlockSpec(memory_space=pl.ANY)],
        out_specs=[pl.BlockSpec(memory_space=pltpu.VMEM)] * 3,
        out_shape=[out] * 3,
        scratch_shapes=[pltpu.SemaphoreType.DMA((6,))],
        compiler_params=params(60),
        cost_estimate=cost(0, 12 * rows * width // NX),
        name="cut_columns",
    )(acts)


def front_kernel(parts, x_hbm, w_hbm, gain_ref, hgain_ref, cot_ref, after_ref, kgs_ref, term_hbm, xv, wv, tv, acc, kgv, in_sems, out_sems):
    rows, width = xv.shape
    blk = width // parts
    spans = [pl.ds(c * blk, blk) for c in range(parts)]
    loads = []
    for c, span in enumerate(spans):
        loads.append(
            (
                pltpu.make_async_copy(x_hbm.at[:, span], xv.at[:, span], in_sems.at[2 * c]),
                pltpu.make_async_copy(w_hbm.at[span], wv.at[span], in_sems.at[2 * c + 1]),
            )
        )
    for pair in loads:
        for one in pair:
            one.start()
    ssq = None
    for c, span in enumerate(spans):
        for one in loads[c]:
            one.wait()
        xf = xv[:, span].astype(jnp.float32)
        scaled = (xf * gain_ref[:, span]).astype(jnp.bfloat16)
        part = jnp.dot(scaled, wv[span, :], preferred_element_type=jnp.float32)
        sq = jnp.sum(xf * xf, axis=-1, keepdims=True)
        if c == 0:
            acc[...] = part
            ssq = sq
        else:
            acc[...] += part
            ssq = ssq + sq
    inv = lax.rsqrt(ssq / width + 1e-06)
    hg = hgain_ref[...]
    dots = jnp.zeros_like(inv)
    for h in range(HEADS_KV):
        cols = slice(h * HEAD, (h + 1) * HEAD)
        raw = acc[:, cols] * inv
        hinv = lax.rsqrt(jnp.mean(raw * raw, axis=-1, keepdims=True) + 1e-06)
        scaled = cot_ref[:, cols].astype(jnp.float32) * hg
        kg = hinv * (scaled - raw * hinv * hinv * jnp.mean(scaled * raw, axis=-1, keepdims=True))
        kgs_ref[:, cols] = (kg * inv).astype(jnp.bfloat16)
        kg = kg.astype(jnp.bfloat16)
        kgv[:, cols] = kg
        dots += jnp.sum(kg.astype(jnp.float32) * raw, axis=-1, keepdims=True)
    coef = inv * inv * dots / width
    stores = []
    for c, span in enumerate(spans):
        back = lax.dot_general(
            kgv[...], wv[span, :], (((1,), (1,)), ((), ())), preferred_element_type=jnp.float32
        )
        term = inv * (gain_ref[:, span] * back) - coef * xv[:, span].astype(jnp.float32)
        tv[c] = term.astype(jnp.bfloat16)
        stores.append(pltpu.make_async_copy(tv.at[c], term_hbm.at[c], out_sems.at[c]))
        stores[c].start()
    for one in stores:
        one.wait()


def front(acts, gain, weight, head_gain, cot, parts, after):
    rows, width = acts.shape
    kv = weight.shape[1]
    blk = width // parts
    anywhere = pl.BlockSpec(memory_space=pl.ANY)
    inside = pl.BlockSpec(memory_space=pltpu.VMEM)
    return pl.pallas_call(
        lambda *refs: front_kernel(parts, *refs),
        in_specs=[anywhere, anywhere, inside, inside, inside, anywhere],
        out_specs=[inside, anywhere],
        out_shape=[
            jax.ShapeDtypeStruct((rows, kv), jnp.bfloat16),
            jax.ShapeDtypeStruct((parts, rows, blk), jnp.bfloat16),
        ],
        scratch_shapes=[
            pltpu.VMEM((rows, width), jnp.bfloat16),
            pltpu.VMEM((width, kv), jnp.bfloat16),
            pltpu.VMEM((parts, rows, blk), jnp.bfloat16),
            pltpu.VMEM((rows, kv), jnp.float32),
            pltpu.VMEM((rows, kv), jnp.bfloat16),
            pltpu.SemaphoreType.DMA((2 * parts,)),
            pltpu.SemaphoreType.DMA((parts,)),
        ],
        compiler_params=params(60),
        cost_estimate=cost(40 * rows * width * kv, 2 * width * (2 * rows + kv)),
        name="front",
    )(acts, weight, gain, head_gain, cot, after)


def total_kernel(z_ref, t_ref, up_ref, after_ref, out_ref):
    total = up_ref[...].astype(jnp.float32)
    for s in range(t_ref.shape[0]):
        total = total + t_ref[s].astype(jnp.float32)
    out_ref[...] = total.astype(jnp.bfloat16)


def half_total(got, upstream, z, after):
    parts, rows, blk = got.shape
    tile = 96
    return pl.pallas_call(
        total_kernel,
        grid_spec=pltpu.PrefetchScalarGridSpec(
            num_scalar_prefetch=1,
            grid=(rows // tile,),
            in_specs=[
                pl.BlockSpec((parts, tile, blk), lambda i, z: (0, i, 0)),
                pl.BlockSpec((tile, blk), lambda i, z: (i, z[0])),
                pl.BlockSpec(memory_space=pl.ANY),
            ],
            out_specs=pl.BlockSpec((tile, blk), lambda i, z: (i, 0)),
        ),
        out_shape=jax.ShapeDtypeStruct((rows, blk), jnp.bfloat16),
        compiler_params=params(16),
        cost_estimate=cost(parts * rows * blk, 2 * parts * rows * blk),
        name="half_total",
    )(z, got, upstream, after)


def suffix_kernel(z_ref, t_ref, up_ref, above_ref, after_ref, out_ref):
    upper = z_ref[1] == 1
    base = jnp.where(upper, up_ref[...].astype(jnp.float32), above_ref[...].astype(jnp.float32))
    total = base
    for s in reversed(range(t_ref.shape[0])):
        total = total + t_ref[s].astype(jnp.float32)
        out_ref[s] = total.astype(jnp.bfloat16)


def suffix_sums(got, upstream, above, z, after):
    parts, rows, blk = got.shape
    tile = 96
    return pl.pallas_call(
        suffix_kernel,
        grid_spec=pltpu.PrefetchScalarGridSpec(
            num_scalar_prefetch=1,
            grid=(rows // tile,),
            in_specs=[
                pl.BlockSpec((parts, tile, blk), lambda i, z: (0, i, 0)),
                pl.BlockSpec((tile, blk), lambda i, z: (i, z[0])),
                pl.BlockSpec((tile, blk), lambda i, z: (i, 0)),
                pl.BlockSpec(memory_space=pl.ANY),
            ],
            out_specs=pl.BlockSpec((parts, tile, blk), lambda i, z: (0, i, 0)),
        ),
        out_shape=jax.ShapeDtypeStruct(got.shape, jnp.bfloat16),
        compiler_params=params(16),
        cost_estimate=cost(parts * rows * blk, 4 * parts * rows * blk),
        name="suffix_sums",
    )(z, got, upstream, above, after)


def lay_kernel(in_ref, out_ref):
    out_ref[...] = in_ref[0]


def side_by_side(got):
    parts, rows, blk = got.shape
    return pl.pallas_call(
        lay_kernel,
        grid=(parts,),
        in_specs=[pl.BlockSpec((1, rows, blk), lambda i: (i, 0, 0))],
        out_specs=pl.BlockSpec((rows, blk), lambda i: (0, i)),
        out_shape=jax.ShapeDtypeStruct((rows, parts * blk), got.dtype),
        compiler_params=params(16),
        cost_estimate=cost(0, 4 * parts * rows * blk),
        name="side_by_side",
    )(got)


def wgrad_kernel(x_hbm, up, down, far, k0, k1, k3, k2, keep_ref, send_ref, av, kv, full, sems):
    rows, wide = up.shape
    blk = wide // 2
    cols = chip_columns(blk, 0)
    moves = [
        (x_hbm.at[:, cols[0]], av.at[pl.ds(0, rows), pl.ds(0, blk)]),
        (x_hbm.at[:, cols[1]], av.at[pl.ds(0, rows), pl.ds(blk, blk)]),
        (up, av.at[pl.ds(rows, rows)]),
        (down, av.at[pl.ds(2 * rows, rows)]),
        (far, av.at[pl.ds(3 * rows, rows)]),
        (k0, kv.at[pl.ds(0, rows)]),
        (k1, kv.at[pl.ds(rows, rows)]),
        (k3, kv.at[pl.ds(2 * rows, rows)]),
        (k2, kv.at[pl.ds(3 * rows, rows)]),
    ]
    run_copies(moves, sems)
    half = keep_ref.shape[1]
    core = lax.rem(lax.axis_index("dp"), 2)
    own = pl.multiple_of(core * half, half)
    other = pl.multiple_of((1 - core) * half, half)
    for y in range(2):
        full[...] = lax.dot_general(
            av[:, y * blk : (y + 1) * blk], kv[...], (((0,), (0,)), ((), ())), preferred_element_type=jnp.float32
        )
        keep_ref[y] = full[pl.ds(own, half), :]
        send_ref[y] = full[pl.ds(other, half), :].astype(jnp.bfloat16)


def wgrad(acts, got, kgs, got_kgs):
    rows, width = acts.shape
    blk = width // (2 * NX)
    kv = kgs.shape[1]
    half = blk // 2
    anywhere = pl.BlockSpec(memory_space=pl.ANY)
    inside = pl.BlockSpec(memory_space=pltpu.VMEM)
    return pl.pallas_call(
        wgrad_kernel,
        in_specs=[anywhere] * 8,
        out_specs=[inside, inside],
        scratch_shapes=[
            pltpu.VMEM((4 * rows, 2 * blk), jnp.bfloat16),
            pltpu.VMEM((4 * rows, kv), jnp.bfloat16),
            pltpu.VMEM((blk, kv), jnp.float32),
            pltpu.SemaphoreType.DMA((9,)),
        ],
        out_shape=[
            jax.ShapeDtypeStruct((2, half, kv), jnp.float32),
            jax.ShapeDtypeStruct((2, half, kv), jnp.bfloat16),
        ],
        compiler_params=params(58),
        cost_estimate=cost(2 * 4 * rows * 2 * blk * kv, 2 * 4 * rows * (2 * blk + kv)),
        name="wgrad",
    )(acts, *got, kgs, *got_kgs)


def merge_kernel(keep, got, here_ref, there_ref):
    y = lax.axis_index("dp") // 8
    here_ref[...] = keep[y] + got[y].astype(jnp.float32)
    there_ref[...] = (keep[1 - y] + got[1 - y].astype(jnp.float32)).astype(jnp.bfloat16)


def merge(keep, got):
    two, half, kv = keep.shape
    inside = pl.BlockSpec(memory_space=pltpu.VMEM)
    return pl.pallas_call(
        merge_kernel,
        in_specs=[inside, inside],
        out_shape=[
            jax.ShapeDtypeStruct((half, kv), jnp.float32),
            jax.ShapeDtypeStruct((half, kv), jnp.bfloat16),
        ],
        compiler_params=params(16),
        cost_estimate=cost(2 * half * kv, 18 * half * kv),
        name="merge",
    )(keep, got)


def adam_kernel(here, got, gain, master, first, second, o_master, o_first, o_second, o_weight):
    grad = gain[...] * (here[...] + got[...].astype(jnp.float32))
    new_first = beta_one * first[0] + (1.0 - beta_one) * grad
    new_second = beta_two * second[0] + (1.0 - beta_two) * grad * grad
    corr_one = 1.0 - beta_one**10
    corr_two = 1.0 - beta_two**10
    update = (
        new_first / corr_one / (jnp.sqrt(new_second / corr_two) + adam_eps)
        + decay_rate * master[0]
    )
    new_master = master[0] - learn_rate * update
    o_master[0] = new_master
    o_first[0] = new_first
    o_second[0] = new_second
    o_weight[...] = new_master.astype(jnp.bfloat16)


def adam(here, got, gain, master, first, second):
    half, kv = here.shape
    tile = half // 2
    flat = pl.BlockSpec((tile, kv), lambda i: (i, 0))
    deep = pl.BlockSpec((1, tile, kv), lambda i: (0, i, 0))
    out = jax.ShapeDtypeStruct(master.shape, jnp.float32)
    return pl.pallas_call(
        adam_kernel,
        grid=(2,),
        in_specs=[flat, flat, pl.BlockSpec((tile, 1), lambda i: (i, 0)), deep, deep, deep],
        out_specs=[deep, deep, deep, flat],
        out_shape=[out, out, out, jax.ShapeDtypeStruct((half, kv), jnp.bfloat16)],
        compiler_params=params(60),
        cost_estimate=cost(20 * half * kv, 32 * half * kv),
        name="adam",
    )(here, got, gain, master, first, second)


def place(plan, bases, blocks, rows, kv, whole, after):
    prior = ([] if whole is None else [whole]) + list(after)
    count = len(blocks)

    def kernel(base_ref, *refs):
        ins, out, sems = refs[:count], refs[-2], refs[-1]
        moves = []
        for which, index, n, slot, shift in plan:
            src = ins[which].at[pl.ds(index, n)]
            at = pl.multiple_of(base_ref[slot] + shift, 32)
            moves.append((src, out.at[pl.ds(at, n)]))
        run_copies(moves, sems)

    return pl.pallas_call(
        kernel,
        in_specs=[pl.BlockSpec(memory_space=pltpu.SMEM)]
        + [pl.BlockSpec(memory_space=pltpu.VMEM)] * count
        + [pl.BlockSpec(memory_space=pl.ANY)] * len(prior),
        out_specs=pl.BlockSpec(memory_space=pl.ANY),
        out_shape=jax.ShapeDtypeStruct((rows, kv), jnp.bfloat16),
        scratch_shapes=[pltpu.SemaphoreType.DMA((len(plan),))],
        input_output_aliases={} if whole is None else {1 + count: 0},
        compiler_params=params(16),
        cost_estimate=cost(0, 4 * kv * sum(p[2] for p in plan)),
        name="place",
    )(bases, *blocks, *prior)


def stack_kernel(*refs):
    moves, at = [], 0
    for ref in refs[:-2]:
        rows = ref.shape[0]
        moves.append((ref, refs[-2].at[pl.ds(at, rows)]))
        at += rows
    run_copies(moves, refs[-1])


def stacked(blocks):
    rows = sum(b.shape[0] for b in blocks)
    return pl.pallas_call(
        stack_kernel,
        in_specs=[pl.BlockSpec(memory_space=pl.ANY)] * len(blocks),
        out_specs=pl.BlockSpec(memory_space=pltpu.VMEM),
        out_shape=jax.ShapeDtypeStruct((rows, blocks[0].shape[1]), blocks[0].dtype),
        scratch_shapes=[pltpu.SemaphoreType.DMA((len(blocks),))],
        compiler_params=params(16),
        cost_estimate=cost(0, 4 * rows * blocks[0].shape[1]),
        name="stacked",
    )(*blocks)


def gather_rows(own, y, x, core, last):
    rows, kv = own.shape
    half = rows // 2
    send = lambda block, perm: lax.ppermute(block, "dp", perm)
    up, down = along_x(1), along_x(-1)
    yr = send(own, SWAP_Y)
    a = send(own, up)
    b = send(own, down)
    a2 = send(yr, up)
    b2 = send(yr, down)
    f = send(a[:half], up)
    g = send(b[half:], down)
    f2 = send(a2[:half], up)
    g2 = send(b2[half:], down)
    order = (0, -1, 1, 2)
    table = []
    for dy in range(2):
        for dx in order:
            for dc in range(2):
                yy = y if dy == 0 else 1 - y
                cc = core if dc == 0 else 1 - core
                table.append((yy * 8 + lax.rem(x + dx + NX, NX) * 2 + cc) * rows)
    bases = jnp.stack(table).astype(jnp.int32)

    def plan_of(entries, dc):
        return [
            (n, block.shape[0], (dy * 4 + order.index(dx)) * 2 + dc, shift)
            for n, (block, dy, dx, shift) in enumerate(entries)
        ]

    def put(entries, swapped, whole, after=()):
        blocks = [e[0] for e in entries]
        plan = [(n, 0, r, slot, shift) for n, r, slot, shift in plan_of(entries, 0)]
        at = 0
        for n, r, slot, shift in plan_of(entries, 1):
            if len(swapped) == 1:
                plan.append((len(blocks), at, r, slot, shift))
                at += r
            else:
                plan.append((len(blocks) + n, 0, r, slot, shift))
        return place(plan, bases, blocks + swapped, 16 * rows, kv, whole, after)

    near = [(own, 0, 0, 0), (a, 0, -1, 0), (b, 0, 1, 0), (yr, 1, 0, 0)]
    whole = put(near, [send(stacked([e[0] for e in near]), SWAP_CORE)], None)
    middle = [(a2, 1, -1, 0), (b2, 1, 1, 0), (f, 0, 2, 0), (g, 0, 2, half)]
    whole = put(middle, [send(e[0], SWAP_CORE) for e in middle], whole, (last,))
    f2, g2, whole = lax.optimization_barrier((f2, g2, whole))
    swapped = send(jnp.concatenate([f2, g2]), SWAP_CORE)
    return put([(f2, 1, 2, 0), (g2, 1, 2, half)], [swapped], whole)


def body(
    activations,
    norm_gain,
    key_weight,
    key_gain,
    key_cotangent,
    upstream,
    master,
    first_moment,
    second_moment,
):
    micro, tok, width = activations.shape[1:]
    rows = micro * tok
    acts = activations.reshape(rows, width)
    weight = key_weight[0]
    kv = weight.shape[1]
    me = lax.axis_index("dp")
    y, x, core = me // 8, lax.rem(me // 2, NX), lax.rem(me, 2)
    section = lax.axis_index("section")
    zpos = jnp.stack([lax.rem(section, NZ), section // NZ]).astype(jnp.int32)
    upstream = upstream.reshape(rows, width)

    cut = cut_columns(acts)
    got = [lax.ppermute(one, "dp", along_x(k)) for one, k in zip(cut, (1, -1, 2))]
    kgs, term = front(acts, norm_gain, weight, key_gain, key_cotangent.reshape(rows, kv), NZ, cut[0])
    got_kgs = [lax.ppermute(kgs, "dp", along_x(1)), lax.ppermute(kgs, "dp", along_x(-1))]
    kgs_late, *got = lax.optimization_barrier((kgs, *got))
    term, got[0], got[1], got[2], *got_kgs = lax.optimization_barrier((term, *got, *got_kgs))
    got_kgs.append(lax.ppermute(kgs_late, "dp", along_x(2)))
    theirs = lax.all_to_all(term, "section", 0, 0, axis_index_groups=RINGS_Z)

    keep, away = wgrad(acts, got, kgs, got_kgs)
    here, there = merge(keep, lax.ppermute(away, "dp", SWAP_CORE))
    ours = half_total(theirs, upstream, zpos, here)

    above = lax.ppermute(ours, "section", DOWN_Y)
    sums = suffix_sums(theirs, upstream, above, zpos, here)
    mine = lax.all_to_all(sums, "section", 0, 0, axis_index_groups=RINGS_Z)
    input_grad = side_by_side(mine).reshape(activations.shape)

    own_rows = here.shape[0]
    gain_rows = lax.dynamic_slice(norm_gain[0], (me * own_rows,), (own_rows,))[:, None]
    new_master, new_first, new_second, own = adam(
        here, lax.ppermute(there, "dp", SWAP_Y), gain_rows, master, first_moment, second_moment
    )
    new_weight = gather_rows(own, y, x, core, input_grad)
    return (input_grad, new_weight[None], new_master, new_first, new_second)


def solution(mesh):
    return jax.shard_map(
        body,
        mesh=mesh,
        in_specs=(
            P("section", None, "dp", None),
            P("section", None),
            P("section", None, None),
            P("section", None),
            P("section", None, "dp", None),
            P(None, "dp", None),
            P("section", "dp", None),
            P("section", "dp", None),
            P("section", "dp", None),
        ),
        out_specs=(
            P("section", None, "dp", None),
            P("section", None, None),
            P("section", "dp", None),
            P("section", "dp", None),
            P("section", "dp", None),
        ),
        check_vma=False,
    )
```

time: 843 us -> 132 us (0.16)
  the two profiles are of different devices: /device:TPU:114 before, /device:TPU:1 now
where the time goes in v2:
time: 132 us; the launch traced here: 131 us
  starting transfers between devices  43.4 us (33%)
  waiting for transfers between devices  35.7 us (27%)
  Pallas kernels  32.7 us (25%)
  local copies, waits for them, and re-layouts  17.1 us (13%)
    ppermute x15, starting transfers between devices, gather_rows(): send = lambda block, perm: lax.ppermute(block, 'dp', perm)  20 us
    unnamed x44, local copies, waits for them, and re-layouts  13.1 us
    ppermute x3, waiting for transfers between devices, body(): lax.ppermute(one, 'dp', along_x(k))  9.99 us
    ppermute x15, waiting for transfers between devices, gather_rows(): send = lambda block, perm: lax.ppermute(block, 'dp', perm)  8.63 us
    pallas_call x1, Pallas kernels, front(): pl.pallas_call(lambda *refs: front_kernel(parts, *refs), in_specs=[anywhe...  8.09 us
    pallas_call x3, Pallas kernels, place(): pl.pallas_call(kernel, in_specs=[pl.BlockSpec(memory_space=pltpu.SMEM)] +...  6.96 us
    ppermute x1, waiting for transfers between devices, body(): got_kgs.append(lax.ppermute(kgs_late, 'dp', along_x(2)))  6.32 us
    ppermute x3, starting transfers between devices, body(): lax.ppermute(one, 'dp', along_x(k))  5.11 us
  transfers between devices with their start and end apart: 26, of which 9 were waited for; matrix products, arithmetic and copies ran while one was open for 3% of the time, Pallas kernels for 22%

profile of v2, /device:TPU:1, one launch (start us, length us, event | category | flops | bytes accessed | tf_op | source)
XLA Modules:
  0.0 130.9 jit_solution(4917647806308925324)
XLA Ops:
  0.6 2.6 %cut_columns.1 = (bf16[192,1280]{1,0:T(8,128)(2,1)}, bf16[192,1280]{1,0:T(8,128)(2,1)}, bf16[192,1280]{1,0:T(8,128)(2,1)}) custom-call(bf16[192,5120]{1,0:T(8,128)(2,1)} %bitcast.31), custom_call_target="tpu_custom_call" | custom-call | bytes 1 | tf_op jit(solution)/shard_map/cut_columns/pallas_call | solution.py:65
  3.3 2.1 %collective-permute-start = (bf16[192,1280]{1,0:T(8,128)(2,1)}, bf16[192,1280]{1,0:T(8,128)(2,1)S(1)}, u32[]{:S(2)}, u32[]{:S(2)}) collective-permute-start(bf16[192,1280]{1,0:T(8,128)(2,1)} %get-tuple-element.31.refs_5_), channel_id=1, source_target_pairs={{0,2},{1,3},{2,4},{3,5},{4,6},{5,7},{6,0},{7,1},{8,10},{9,11},{10,... | collective-permute-start | bytes 1474568 | tf_op jit(solution)/shard_map/ppermute | solution.py:478
  5.4 1.3 %collective-permute-start.1 = (bf16[192,1280]{1,0:T(8,128)(2,1)}, bf16[192,1280]{1,0:T(8,128)(2,1)S(1)}, u32[]{:S(2)}, u32[]{:S(2)}) collective-permute-start(bf16[192,1280]{1,0:T(8,128)(2,1)} %get-tuple-element.34), channel_id=1, source_target_pairs={{0,6},{1,7},{2,0},{3,1},{4,2},{5,3},{6,4},{7,5},{8,14},{9,15},{10,... | collective-permute-start | bytes 1474568 | tf_op jit(solution)/shard_map/ppermute | solution.py:478
  6.7 1.6 %collective-permute-start.2 = (bf16[192,1280]{1,0:T(8,128)(2,1)}, bf16[192,1280]{1,0:T(8,128)(2,1)S(1)}, u32[]{:S(2)}, u32[]{:S(2)}) collective-permute-start(bf16[192,1280]{1,0:T(8,128)(2,1)} %get-tuple-element.35), channel_id=1, source_target_pairs={{0,4},{1,5},{2,6},{3,7},{4,0},{5,1},{6,2},{7,3},{8,12},{9,13},{10,... | collective-permute-start | bytes 1474568 | tf_op jit(solution)/shard_map/ppermute | solution.py:478
  8.4 8.1 %front.1 = (bf16[192,512]{1,0:T(8,128)(2,1)}, bf16[4,192,1280]{2,1,0:T(8,128)(2,1)}) custom-call(bf16[192,5120]{1,0:T(8,128)(2,1)} %bitcast.32, bf16[5120,512]{1,0:T(8,128)(2,1)} %bitcast.34, f32[1,5120]{1,0:T(1,128)} %refs_2_.1, f32[1,128]{1,0:T(1,128)} %refs_3_.1, bf16[192,512]{1,0:T(8,128)(2,1)} %bitcast.35, bf16[192,1280]{1,0:T(8,128)(2,1)} %get-tuple-element.31.refs_5_), custom_call_target="tpu_custom_call" | custom-call | bytes 1 | tf_op jit(solution)/shard_map/front/pallas_call | solution.py:139
  16.9 2.4 %collective-permute-start.4 = (bf16[192,512]{1,0:T(8,128)(2,1)}, bf16[192,512]{1,0:T(8,128)(2,1)S(1)}, u32[]{:S(2)}, u32[]{:S(2)}) collective-permute-start(bf16[192,512]{1,0:T(8,128)(2,1)} %get-tuple-element.45.k0), channel_id=1, source_target_pairs={{0,6},{1,7},{2,0},{3,1},{4,2},{5,3},{6,4},{7,5},{8,14},{9,15},{10,... | collective-permute-start | bytes 589832 | tf_op jit(solution)/shard_map/ppermute | solution.py:480
  19.3 10.0 %collective-permute-done.2.far = bf16[192,1280]{1,0:T(8,128)(2,1)S(1)} collective-permute-done((bf16[192,1280]{1,0:T(8,128)(2,1)}, bf16[192,1280]{1,0:T(8,128)(2,1)S(1)}, u32[]{:S(2)}, u32[]{:S(2)}) %collective-permute-start.2) | collective-permute-done | bytes 491552 | tf_op jit(solution)/shard_map/ppermute | solution.py:478
  29.2 4.9 %collective-permute-done.3.k1 = bf16[192,512]{1,0:T(8,128)(2,1)S(1)} collective-permute-done((bf16[192,512]{1,0:T(8,128)(2,1)}, bf16[192,512]{1,0:T(8,128)(2,1)S(1)}, u32[]{:S(2)}, u32[]{:S(2)}) %collective-permute-start.3) | collective-permute-done | bytes 196640 | tf_op jit(solution)/shard_map/ppermute | solution.py:480
  35.6 5.0 %all-to-all-start = ((bf16[4,192,1280]{2,1,0:T(8,128)(2,1)}), bf16[4,192,1280]{2,1,0:T(8,128)(2,1)S(1)}, u32[]{:S(2)}, u32[]{:S(2)}) async-start(bf16[4,192,1280]{2,1,0:T(8,128)(2,1)} %get-tuple-element.39), calls=%async_computation | async-start | bytes 3932160 | tf_op jit(solution)/shard_map/all_to_all | solution.py:484
  41.3 6.3 %collective-permute-done.5.k2 = bf16[192,512]{1,0:T(8,128)(2,1)S(1)} collective-permute-done((bf16[192,512]{1,0:T(8,128)(2,1)S(1)}, bf16[192,512]{1,0:T(8,128)(2,1)S(1)}, u32[]{:S(2)}, u32[]{:S(2)}) %collective-permute-start.5) | collective-permute-done | bytes 196640 | tf_op jit(solution)/shard_map/ppermute | solution.py:483
  48.3 4.7 %wgrad.1 = (f32[2,320,512]{2,1,0:T(8,128)}, bf16[2,320,512]{2,1,0:T(8,128)(2,1)}) custom-call(bf16[192,5120]{1,0:T(8,128)(2,1)} %bitcast.33, bf16[192,1280]{1,0:T(8,128)(2,1)} %copy-done.14, bf16[192,1280]{1,0:T(8,128)(2,1)} %copy-done.15, bf16[192,1280]{1,0:T(8,128)(2,1)} %copy-done.16, bf16[192,512]{1,0:T(8,128)(2,1)} %get-tuple-element.45.k0, ...), custom_call_target="tpu_custom_call" | custom-call | bytes 1 | tf_op jit(solution)/shard_map/wgrad/pallas_call | solution.py:276
  52.9 1.9 %collective-permute-start.6 = (bf16[2,320,512]{2,1,0:T(8,128)(2,1)}, bf16[2,320,512]{2,1,0:T(8,128)(2,1)S(1)}, u32[]{:S(2)}, u32[]{:S(2)}) collective-permute-start(bf16[2,320,512]{2,1,0:T(8,128)(2,1)} %get-tuple-element.47), channel_id=1, source_target_pairs={{0,1},{1,0},{2,3},{3,2},{4,5},{5,4},{6,7},{7,6},{8,9},{9,8},{10,11... | collective-permute-start | bytes 1966088 | tf_op jit(solution)/shard_map/ppermute | solution.py:487
  54.8 1.9 %collective-permute-done.6.got = bf16[2,320,512]{2,1,0:T(8,128)(2,1)S(1)} collective-permute-done((bf16[2,320,512]{2,1,0:T(8,128)(2,1)}, bf16[2,320,512]{2,1,0:T(8,128)(2,1)S(1)}, u32[]{:S(2)}, u32[]{:S(2)}) %collective-permute-start.6) | collective-permute-done | bytes 655392 | tf_op jit(solution)/shard_map/ppermute | solution.py:487
  56.8 1.3 %copy-done.7 = f32[2,320,512]{2,1,0:T(8,128)S(1)} copy-done((f32[2,320,512]{2,1,0:T(8,128)S(1)}, f32[2,320,512]{2,1,0:T(8,128)}, u32[]{:S(2)}) %copy-start.7) | copy-done | bytes 1310744
  58.2 3.0 %collective-permute-start.8 = (bf16[320,512]{1,0:T(8,128)(2,1)S(1)}, bf16[320,512]{1,0:T(8,128)(2,1)S(1)}, u32[]{:S(2)}, u32[]{:S(2)}) collective-permute-start(bf16[320,512]{1,0:T(8,128)(2,1)S(1)} %get-tuple-element.49), channel_id=1, source_target_pairs={{0,8},{1,9},{2,10},{3,11},{4,12},{5,13},{6,14},{7,15},{8,0},{9,1},... | collective-permute-start | bytes 983048 | tf_op jit(solution)/shard_map/ppermute | solution.py:498
  61.3 3.4 %all-to-all-done.t_ref = bf16[4,192,1280]{2,1,0:T(8,128)(2,1)S(1)} async-done(((bf16[4,192,1280]{2,1,0:T(8,128)(2,1)}), bf16[4,192,1280]{2,1,0:T(8,128)(2,1)S(1)}, u32[]{:S(2)}, u32[]{:S(2)}) %all-to-all-start) | async-done | bytes 1966112 | tf_op jit(solution)/shard_map/all_to_all | solution.py:484
  64.6 1.5 %copy-done.1 = bf16[2,96,5120]{2,1,0:T(8,128)(2,1)S(1)} copy-done((bf16[2,96,5120]{2,1,0:T(8,128)(2,1)S(1)}, bf16[2,96,5120]{2,1,0:T(8,128)(2,1)}, u32[]{:S(2)}) %copy-start.1) | copy-done | bytes 1966104
  66.2 1.8 %half_total.1 = bf16[192,1280]{1,0:T(8,128)(2,1)} custom-call(s32[2]{0:T(128)S(1)} %pad_add_fusion.z_ref, bf16[4,192,1280]{2,1,0:T(8,128)(2,1)S(1)} %all-to-all-done.t_ref, bf16[192,5120]{1,0:T(8,128)(2,1)S(1)} %bitcast.26, f32[320,512]{1,0:T(8,128)S(1)} %get-tuple-element.48.after_ref.here), custom_call_target="tpu_custom_call" | custom-call | bytes 1 | tf_op jit(solution)/shard_map/half_total/pallas_call | solution.py:172
  68.0 1.3 collective-permute-start.7
  69.3 0.8 dynamic-slice_bitcast_fusion
  70.1 0.8 copy.16.gain
  71.7 3.2 %adam.1 = (f32[1,320,512]{2,1,0:T(8,128)}, f32[1,320,512]{2,1,0:T(8,128)}, f32[1,320,512]{2,1,0:T(8,128)}, bf16[320,512]{1,0:T(8,128)(2,1)}) custom-call(f32[320,512]{1,0:T(8,128)} %copy-done.4, bf16[320,512]{1,0:T(8,128)(2,1)} %copy-done.17, f32[320,1]{1,0:T(8,128)} %copy.16.gain, f32[1,320,512]{2,1,0:T(8,128)} %master.1, f32[1,320,512]{2,1,0:T(8,128)} %first.1, ...), custom_call_target="tpu_custom_call" | custom-call | bytes 1 | tf_op jit(solution)/shard_map/adam/pallas_call | solution.py:341
  74.9 2.7 %collective-permute-start.16 = (bf16[320,512]{1,0:T(8,128)(2,1)}, bf16[320,512]{1,0:T(8,128)(2,1)S(1)}, u32[]{:S(2)}, u32[]{:S(2)}) collective-permute-start(bf16[320,512]{1,0:T(8,128)(2,1)} %get-tuple-element.50.refs_0_), channel_id=1, source_target_pairs={{0,6},{1,7},{2,0},{3,1},{4,2},{5,3},{6,4},{7,5},{8,14},{9,15},{10,... | collective-permute-start | bytes 983048 | tf_op jit(solution)/shard_map/ppermute | solution.py:407
  77.6 2.9 %collective-permute-start.9 = (bf16[320,512]{1,0:T(8,128)(2,1)}, bf16[320,512]{1,0:T(8,128)(2,1)}, u32[]{:S(2)}, u32[]{:S(2)}) collective-permute-start(bf16[320,512]{1,0:T(8,128)(2,1)} %get-tuple-element.50.refs_0_), channel_id=1, source_target_pairs={{0,8},{1,9},{2,10},{3,11},{4,12},{5,13},{6,14},{7,15},{8,0},{9,1},... | collective-permute-start | bytes 983048 | tf_op jit(solution)/shard_map/ppermute | solution.py:407
  81.1 1.5 %copy-done.2 = bf16[2,96,5120]{2,1,0:T(8,128)(2,1)S(1)} copy-done((bf16[2,96,5120]{2,1,0:T(8,128)(2,1)S(1)}, bf16[2,96,5120]{2,1,0:T(8,128)(2,1)}, u32[]{:S(2)}) %copy-start.2) | copy-done | bytes 1966104
  82.6 2.2 %suffix_sums.1 = bf16[4,192,1280]{2,1,0:T(8,128)(2,1)S(1)} custom-call(s32[2]{0:T(128)S(1)} %pad_add_fusion.z_ref, bf16[4,192,1280]{2,1,0:T(8,128)(2,1)S(1)} %all-to-all-done.t_ref, bf16[192,5120]{1,0:T(8,128)(2,1)S(1)} %bitcast.27, bf16[192,1280]{1,0:T(8,128)(2,1)} %collective-permute-done.7.above_ref, f32[320,512]{1,0:T(8,128)S(1)} %copy-done.5), custom_call_target="tpu_custom_call" | custom-call | bytes 1 | tf_op jit(solution)/shard_map/suffix_sums/pallas_call | solution.py:203
  84.8 1.3 copy-done
  86.1 3.7 %all-to-all-start.1 = ((bf16[4,192,1280]{2,1,0:T(8,128)(2,1)}), bf16[4,192,1280]{2,1,0:T(8,128)(2,1)S(1)}, u32[]{:S(2)}, u32[]{:S(2)}) async-start(bf16[4,192,1280]{2,1,0:T(8,128)(2,1)} %copy-done), calls=%async_computation.1 | async-start | bytes 3932160 | tf_op jit(solution)/shard_map/all_to_all | solution.py:492
  89.8 1.3 %stacked.1 = bf16[1280,512]{1,0:T(8,128)(2,1)S(1)} custom-call(bf16[320,512]{1,0:T(8,128)(2,1)S(1)} %copy-done.6, bf16[320,512]{1,0:T(8,128)(2,1)S(1)} %collective-permute-done.14.refs_1_, bf16[320,512]{1,0:T(8,128)(2,1)S(1)} %collective-permute-done.16.refs_2_, bf16[320,512]{1,0:T(8,128)(2,1)} %collective-permute-done.9.refs_3_), custom_call_target="tpu_custom_call" | custom-call | bytes 1 | tf_op jit(solution)/shard_map/stacked/pallas_call | solution.py:392
  91.2 2.8 %collective-permute-start.22 = (bf16[1280,512]{1,0:T(8,128)(2,1)S(1)}, bf16[1280,512]{1,0:T(8,128)(2,1)S(1)}, u32[]{:S(2)}, u32[]{:S(2)}) collective-permute-start(bf16[1280,512]{1,0:T(8,128)(2,1)S(1)} %stacked.1), channel_id=1, source_target_pairs={{0,1},{1,0},{2,3},{3,2},{4,5},{5,4},{6,7},{7,6},{8,9},{9,8},{10,11... | collective-permute-start | bytes 3932168 | tf_op jit(solution)/shard_map/ppermute | solution.py:407
  94.0 2.7 %collective-permute-start.12 = (bf16[320,512]{1,0:T(8,128)(2,1)}, bf16[320,512]{1,0:T(8,128)(2,1)}, u32[]{:S(2)}, u32[]{:S(2)}) collective-permute-start(bf16[320,512]{1,0:T(8,128)(2,1)} %collective-permute-done.9.refs_3_), channel_id=1, source_target_pairs={{0,6},{1,7},{2,0},{3,1},{4,2},{5,3},{6,4},{7,5},{8,14},{9,15},{10,... | collective-permute-start | bytes 983048 | tf_op jit(solution)/shard_map/ppermute | solution.py:407
  96.8 2.7 %collective-permute-start.17 = (bf16[160,512]{1,0:T(8,128)(2,1)S(1)}, bf16[160,512]{1,0:T(8,128)(2,1)}, u32[]{:S(2)}, u32[]{:S(2)}) collective-permute-start(bf16[160,512]{1,0:T(8,128)(2,1)S(1)} %slice.19), channel_id=1, source_target_pairs={{0,6},{1,7},{2,0},{3,1},{4,2},{5,3},{6,4},{7,5},{8,14},{9,15},{10,... | collective-permute-start | bytes 491528 | tf_op jit(solution)/shard_map/ppermute | solution.py:407
  99.5 5.2 %collective-permute-done.10.refs_0_ = bf16[320,512]{1,0:T(8,128)(2,1)S(1)} collective-permute-done((bf16[320,512]{1,0:T(8,128)(2,1)}, bf16[320,512]{1,0:T(8,128)(2,1)S(1)}, u32[]{:S(2)}, u32[]{:S(2)}) %collective-permute-start.10) | collective-permute-done | bytes 327712 | tf_op jit(solution)/shard_map/ppermute | solution.py:407
  104.7 1.3 %collective-permute-start.18 = (bf16[320,512]{1,0:T(8,128)(2,1)S(1)}, bf16[320,512]{1,0:T(8,128)(2,1)}, u32[]{:S(2)}, u32[]{:S(2)}) collective-permute-start(bf16[320,512]{1,0:T(8,128)(2,1)S(1)} %collective-permute-done.10.refs_0_), channel_id=1, source_target_pairs={{0,1},{1,0},{2,3},{3,2},{4,5},{5,4},{6,7},{7,6},{8,9},{9,8},{10,11... | collective-permute-start | bytes 983048 | tf_op jit(solution)/shard_map/ppermute | solution.py:407
  106.0 2.2 %collective-permute-done.15.refs_2_ = bf16[160,512]{1,0:T(8,128)(2,1)S(1)} collective-permute-done((bf16[160,512]{1,0:T(8,128)(2,1)S(1)}, bf16[160,512]{1,0:T(8,128)(2,1)S(1)}, u32[]{:S(2)}, u32[]{:S(2)}) %collective-permute-start.15) | collective-permute-done | bytes 163872 | tf_op jit(solution)/shard_map/ppermute | solution.py:407
  108.2 0.9 collective-permute-start.20
  109.8 1.6 %slice.17 = bf16[160,512]{1,0:T(8,128)(2,1)} slice(bf16[320,512]{1,0:T(8,128)(2,1)} %collective-permute-done.12.refs_1_), slice={[160:320], [0:512]} | slice | bytes 327680 | tf_op jit(solution)/shard_map/slice | solution.py:417
  112.1 1.0 copy-done.8
  113.2 2.7 %collective-permute-start.13 = (bf16[160,512]{1,0:T(8,128)(2,1)}, bf16[160,512]{1,0:T(8,128)(2,1)}, u32[]{:S(2)}, u32[]{:S(2)}) collective-permute-start(bf16[160,512]{1,0:T(8,128)(2,1)} %slice.17), channel_id=1, source_target_pairs={{0,6},{1,7},{2,0},{3,1},{4,2},{5,3},{6,4},{7,5},{8,14},{9,15},{10,... | collective-permute-start | bytes 491528 | tf_op jit(solution)/shard_map/ppermute | solution.py:407
  116.0 1.3 copy-done.9
  117.3 2.5 %place.3.refs_8_ = bf16[5120,512]{1,0:T(8,128)(2,1)} custom-call(s32[16]{0:T(128)S(1)} %stack.79.base_ref, bf16[320,512]{1,0:T(8,128)(2,1)S(1)} %copy-done.6, bf16[320,512]{1,0:T(8,128)(2,1)S(1)} %collective-permute-done.14.refs_1_, bf16[320,512]{1,0:T(8,128)(2,1)S(1)} %collective-permute-done.16.refs_2_, bf16[320,512]{1,0:T(8,128)(2,1)} %collective-permute-done.9.refs_3_, ...), custom_call_target="tpu_custom_call" | custom-call | bytes 1 | tf_op jit(solution)/shard_map/place/pallas_call | solution.py:366
  119.8 1.8 %side_by_side.1 = bf16[192,5120]{1,0:T(8,128)(2,1)} custom-call(bf16[4,192,1280]{2,1,0:T(8,128)(2,1)S(1)} %all-to-all-done.1.in_ref), custom_call_target="tpu_custom_call" | custom-call | bytes 1 | tf_op jit(solution)/shard_map/side_by_side/pallas_call | solution.py:229
  121.7 1.5 %copy-done.3 = bf16[192,5120]{1,0:T(8,128)(2,1)S(1)} copy-done((bf16[192,5120]{1,0:T(8,128)(2,1)S(1)}, bf16[192,5120]{1,0:T(8,128)(2,1)}, u32[]{:S(2)}) %copy-start.3) | copy-done | bytes 1966104
  123.2 2.6 %place.4.refs_3_ = bf16[5120,512]{1,0:T(8,128)(2,1)} custom-call(s32[16]{0:T(128)S(1)} %stack.79.base_ref, bf16[320,512]{1,0:T(8,128)(2,1)S(1)} %collective-permute-done.10.refs_0_, bf16[320,512]{1,0:T(8,128)(2,1)} %collective-permute-done.12.refs_1_, bf16[160,512]{1,0:T(8,128)(2,1)S(1)} %copy-done.11, ...), custom_call_target="tpu_custom_call", output_to_operand_aliasing={{}: (9, {})} | custom-call | bytes 1 | tf_op jit(solution)/shard_map/place/pallas_call | solution.py:366
  125.9 0.9 pad_maximum_fusion
  126.8 1.0 collective-permute-start.23
  127.9 1.3 collective-permute-done.23.refs_2_
  129.1 1.8 %place.5 = bf16[5120,512]{1,0:T(8,128)(2,1)} custom-call(s32[16]{0:T(128)S(1)} %stack.79.base_ref, bf16[160,512]{1,0:T(8,128)(2,1)S(1)} %collective-permute-done.11.refs_0_, bf16[160,512]{1,0:T(8,128)(2,1)} %collective-permute-done.13.refs_1_, bf16[320,512]{1,0:T(8,128)(2,1)S(1)} %collective-permute-done.23.refs_2_, ...), custom_call_target="tpu_custom_call", output_to_operand_aliasing={{}: (4, {})} | custom-call | bytes 1 | tf_op jit(solution)/shard_map/place/pallas_call | solution.py:366
  (69 shorter events, 6.3 us)
Async XLA Ops:
  3.3 16.0 %collective-permute-start = (bf16[192,1280]{1,0:T(8,128)(2,1)}, bf16[192,1280]{1,0:T(8,128)(2,1)S(1)}, u32[]{:S(2)}, u32[]{:S(2)}) collective-permute-start(bf16[192,1280]{1,0:T(8,128)(2,1)} %get-tuple-element.31.refs_5_), channel_id=1, source_target_pairs={{0,2},{1,3},{2,4},{3,5},{4,6},{5,7},{6,0},{7,1},{8,10},{9,11},{10,... | collective-permute-start | bytes 1474568 | tf_op jit(solution)/shard_map/ppermute | solution.py:478
  5.4 13.9 %collective-permute-start.1 = (bf16[192,1280]{1,0:T(8,128)(2,1)}, bf16[192,1280]{1,0:T(8,128)(2,1)S(1)}, u32[]{:S(2)}, u32[]{:S(2)}) collective-permute-start(bf16[192,1280]{1,0:T(8,128)(2,1)} %get-tuple-element.34), channel_id=1, source_target_pairs={{0,6},{1,7},{2,0},{3,1},{4,2},{5,3},{6,4},{7,5},{8,14},{9,15},{10,... | collective-permute-start | bytes 1474568 | tf_op jit(solution)/shard_map/ppermute | solution.py:478
  6.7 22.5 %collective-permute-start.2 = (bf16[192,1280]{1,0:T(8,128)(2,1)}, bf16[192,1280]{1,0:T(8,128)(2,1)S(1)}, u32[]{:S(2)}, u32[]{:S(2)}) collective-permute-start(bf16[192,1280]{1,0:T(8,128)(2,1)} %get-tuple-element.35), channel_id=1, source_target_pairs={{0,4},{1,5},{2,6},{3,7},{4,0},{5,1},{6,2},{7,3},{8,12},{9,13},{10,... | collective-permute-start | bytes 1474568 | tf_op jit(solution)/shard_map/ppermute | solution.py:478
  16.5 17.7 %collective-permute-start.3 = (bf16[192,512]{1,0:T(8,128)(2,1)}, bf16[192,512]{1,0:T(8,128)(2,1)S(1)}, u32[]{:S(2)}, u32[]{:S(2)}) collective-permute-start(bf16[192,512]{1,0:T(8,128)(2,1)} %get-tuple-element.45.k0), channel_id=1, source_target_pairs={{0,2},{1,3},{2,4},{3,5},{4,6},{5,7},{6,0},{7,1},{8,10},{9,11},{10,... | collective-permute-start | bytes 589832 | tf_op jit(solution)/shard_map/ppermute | solution.py:480
  16.9 17.3 %collective-permute-start.4 = (bf16[192,512]{1,0:T(8,128)(2,1)}, bf16[192,512]{1,0:T(8,128)(2,1)S(1)}, u32[]{:S(2)}, u32[]{:S(2)}) collective-permute-start(bf16[192,512]{1,0:T(8,128)(2,1)} %get-tuple-element.45.k0), channel_id=1, source_target_pairs={{0,6},{1,7},{2,0},{3,1},{4,2},{5,3},{6,4},{7,5},{8,14},{9,15},{10,... | collective-permute-start | bytes 589832 | tf_op jit(solution)/shard_map/ppermute | solution.py:480
  19.2 16.3 %copy-start.14 = (bf16[192,1280]{1,0:T(8,128)(2,1)}, bf16[192,1280]{1,0:T(8,128)(2,1)S(1)}, u32[]{:S(2)}) copy-start(bf16[192,1280]{1,0:T(8,128)(2,1)S(1)} %collective-permute-done.up) | copy-start | bytes 1474564
  19.2 16.3 %copy-start.15 = (bf16[192,1280]{1,0:T(8,128)(2,1)}, bf16[192,1280]{1,0:T(8,128)(2,1)S(1)}, u32[]{:S(2)}) copy-start(bf16[192,1280]{1,0:T(8,128)(2,1)S(1)} %collective-permute-done.1.down) | copy-start | bytes 1474564
  29.2 5.6 %copy-start.16 = (bf16[192,1280]{1,0:T(8,128)(2,1)}, bf16[192,1280]{1,0:T(8,128)(2,1)S(1)}, u32[]{:S(2)}) copy-start(bf16[192,1280]{1,0:T(8,128)(2,1)S(1)} %collective-permute-done.2.far) | copy-start | bytes 1474564
  34.2 0.7 copy-start.19
  34.9 0.7 copy-start.20
  34.9 5.7 %copy-start.18 = (bf16[192,512]{1,0:T(8,128)(2,1)S(1)}, bf16[192,512]{1,0:T(8,128)(2,1)}, u32[]{:S(2)}) copy-start(bf16[192,512]{1,0:T(8,128)(2,1)} %get-tuple-element.45.k0) | copy-start | bytes 589828
  35.6 29.1 %all-to-all-start = ((bf16[4,192,1280]{2,1,0:T(8,128)(2,1)}), bf16[4,192,1280]{2,1,0:T(8,128)(2,1)S(1)}, u32[]{:S(2)}, u32[]{:S(2)}) async-start(bf16[4,192,1280]{2,1,0:T(8,128)(2,1)} %get-tuple-element.39), calls=%async_computation | async-start | bytes 3932160 | tf_op jit(solution)/shard_map/all_to_all | solution.py:484
  40.6 7.0 %collective-permute-start.5 = (bf16[192,512]{1,0:T(8,128)(2,1)S(1)}, bf16[192,512]{1,0:T(8,128)(2,1)S(1)}, u32[]{:S(2)}, u32[]{:S(2)}) collective-permute-start(bf16[192,512]{1,0:T(8,128)(2,1)S(1)} %copy-done.18), channel_id=1, source_target_pairs={{0,4},{1,5},{2,6},{3,7},{4,0},{5,1},{6,2},{7,3},{8,12},{9,13},{10,... | collective-permute-start | bytes 589832 | tf_op jit(solution)/shard_map/ppermute | solution.py:483
  47.6 0.7 copy-start.21
  52.9 3.8 %collective-permute-start.6 = (bf16[2,320,512]{2,1,0:T(8,128)(2,1)}, bf16[2,320,512]{2,1,0:T(8,128)(2,1)S(1)}, u32[]{:S(2)}, u32[]{:S(2)}) collective-permute-start(bf16[2,320,512]{2,1,0:T(8,128)(2,1)} %get-tuple-element.47), channel_id=1, source_target_pairs={{0,1},{1,0},{2,3},{3,2},{4,5},{5,4},{6,7},{7,6},{8,9},{9,8},{10,11... | collective-permute-start | bytes 1966088 | tf_op jit(solution)/shard_map/ppermute | solution.py:487
  56.8 1.3 %copy-start.7 = (f32[2,320,512]{2,1,0:T(8,128)S(1)}, f32[2,320,512]{2,1,0:T(8,128)}, u32[]{:S(2)}) copy-start(f32[2,320,512]{2,1,0:T(8,128)} %get-tuple-element.46.keep) | copy-start | bytes 3932164
  58.2 9.8 %copy-start.4 = (f32[320,512]{1,0:T(8,128)}, f32[320,512]{1,0:T(8,128)S(1)}, u32[]{:S(2)}) copy-start(f32[320,512]{1,0:T(8,128)S(1)} %get-tuple-element.48.after_ref.here) | copy-start | bytes 1966084
  58.2 12.7 %collective-permute-start.8 = (bf16[320,512]{1,0:T(8,128)(2,1)S(1)}, bf16[320,512]{1,0:T(8,128)(2,1)S(1)}, u32[]{:S(2)}, u32[]{:S(2)}) collective-permute-start(bf16[320,512]{1,0:T(8,128)(2,1)S(1)} %get-tuple-element.49), channel_id=1, source_target_pairs={{0,8},{1,9},{2,10},{3,11},{4,12},{5,13},{6,14},{7,15},{8,0},{9,1},... | collective-permute-start | bytes 983048 | tf_op jit(solution)/shard_map/ppermute | solution.py:498
  64.6 1.5 %copy-start.1 = (bf16[2,96,5120]{2,1,0:T(8,128)(2,1)S(1)}, bf16[2,96,5120]{2,1,0:T(8,128)(2,1)}, u32[]{:S(2)}) copy-start(bf16[2,96,5120]{2,1,0:T(8,128)(2,1)} %param.14) | copy-start | bytes 5898244
  68.0 13.1 %collective-permute-start.7 = (bf16[192,1280]{1,0:T(8,128)(2,1)}, bf16[192,1280]{1,0:T(8,128)(2,1)}, u32[]{:S(2)}, u32[]{:S(2)}) collective-permute-start(bf16[192,1280]{1,0:T(8,128)(2,1)} %half_total.1), channel_id=1, source_target_pairs={{64,0},{80,16},{96,32},{112,48},{65,1},{81,17},{97,33},{113,49},{6... | collective-permute-start | bytes 1474568 | tf_op jit(solution)/shard_map/ppermute | solution.py:490
  69.2 11.8 %copy-start.5 = (f32[320,512]{1,0:T(8,128)S(1)}, f32[320,512]{1,0:T(8,128)}, u32[]{:S(2)}) copy-start(f32[320,512]{1,0:T(8,128)} %copy-done.4) | copy-start | bytes 1966084
  70.9 0.7 copy-start.17
  74.9 14.9 %collective-permute-start.14 = (bf16[320,512]{1,0:T(8,128)(2,1)}, bf16[320,512]{1,0:T(8,128)(2,1)S(1)}, u32[]{:S(2)}, u32[]{:S(2)}) collective-permute-start(bf16[320,512]{1,0:T(8,128)(2,1)} %get-tuple-element.50.refs_0_), channel_id=1, source_target_pairs={{0,2},{1,3},{2,4},{3,5},{4,6},{5,7},{6,0},{7,1},{8,10},{9,11},{10,... | collective-permute-start | bytes 983048 | tf_op jit(solution)/shard_map/ppermute | solution.py:407
  74.9 14.9 %collective-permute-start.16 = (bf16[320,512]{1,0:T(8,128)(2,1)}, bf16[320,512]{1,0:T(8,128)(2,1)S(1)}, u32[]{:S(2)}, u32[]{:S(2)}) collective-permute-start(bf16[320,512]{1,0:T(8,128)(2,1)} %get-tuple-element.50.refs_0_), channel_id=1, source_target_pairs={{0,6},{1,7},{2,0},{3,1},{4,2},{5,3},{6,4},{7,5},{8,14},{9,15},{10,... | collective-permute-start | bytes 983048 | tf_op jit(solution)/shard_map/ppermute | solution.py:407
  77.6 12.3 %collective-permute-start.9 = (bf16[320,512]{1,0:T(8,128)(2,1)}, bf16[320,512]{1,0:T(8,128)(2,1)}, u32[]{:S(2)}, u32[]{:S(2)}) collective-permute-start(bf16[320,512]{1,0:T(8,128)(2,1)} %get-tuple-element.50.refs_0_), channel_id=1, source_target_pairs={{0,8},{1,9},{2,10},{3,11},{4,12},{5,13},{6,14},{7,15},{8,0},{9,1},... | collective-permute-start | bytes 983048 | tf_op jit(solution)/shard_map/ppermute | solution.py:407
  81.1 1.5 %copy-start.2 = (bf16[2,96,5120]{2,1,0:T(8,128)(2,1)S(1)}, bf16[2,96,5120]{2,1,0:T(8,128)(2,1)}, u32[]{:S(2)}) copy-start(bf16[2,96,5120]{2,1,0:T(8,128)(2,1)} %param.14) | copy-start | bytes 5898244
  84.8 1.3 copy-start
  86.1 3.8 %copy-start.6 = (bf16[320,512]{1,0:T(8,128)(2,1)S(1)}, bf16[320,512]{1,0:T(8,128)(2,1)}, u32[]{:S(2)}) copy-start(bf16[320,512]{1,0:T(8,128)(2,1)} %get-tuple-element.50.refs_0_) | copy-start | bytes 983044
  86.1 33.8 %all-to-all-start.1 = ((bf16[4,192,1280]{2,1,0:T(8,128)(2,1)}), bf16[4,192,1280]{2,1,0:T(8,128)(2,1)S(1)}, u32[]{:S(2)}, u32[]{:S(2)}) async-start(bf16[4,192,1280]{2,1,0:T(8,128)(2,1)} %copy-done), calls=%async_computation.1 | async-start | bytes 3932160 | tf_op jit(solution)/shard_map/all_to_all | solution.py:492
  91.2 20.9 %collective-permute-start.22 = (bf16[1280,512]{1,0:T(8,128)(2,1)S(1)}, bf16[1280,512]{1,0:T(8,128)(2,1)S(1)}, u32[]{:S(2)}, u32[]{:S(2)}) collective-permute-start(bf16[1280,512]{1,0:T(8,128)(2,1)S(1)} %stacked.1), channel_id=1, source_target_pairs={{0,1},{1,0},{2,3},{3,2},{4,5},{5,4},{6,7},{7,6},{8,9},{9,8},{10,11... | collective-permute-start | bytes 3932168 | tf_op jit(solution)/shard_map/ppermute | solution.py:407
  94.0 10.7 %collective-permute-start.10 = (bf16[320,512]{1,0:T(8,128)(2,1)}, bf16[320,512]{1,0:T(8,128)(2,1)S(1)}, u32[]{:S(2)}, u32[]{:S(2)}) collective-permute-start(bf16[320,512]{1,0:T(8,128)(2,1)} %collective-permute-done.9.refs_3_), channel_id=1, source_target_pairs={{0,2},{1,3},{2,4},{3,5},{4,6},{5,7},{6,0},{7,1},{8,10},{9,11},{10,... | collective-permute-start | bytes 983048 | tf_op jit(solution)/shard_map/ppermute | solution.py:407
  94.0 12.0 %collective-permute-start.12 = (bf16[320,512]{1,0:T(8,128)(2,1)}, bf16[320,512]{1,0:T(8,128)(2,1)}, u32[]{:S(2)}, u32[]{:S(2)}) collective-permute-start(bf16[320,512]{1,0:T(8,128)(2,1)} %collective-permute-done.9.refs_3_), channel_id=1, source_target_pairs={{0,6},{1,7},{2,0},{3,1},{4,2},{5,3},{6,4},{7,5},{8,14},{9,15},{10,... | collective-permute-start | bytes 983048 | tf_op jit(solution)/shard_map/ppermute | solution.py:407
  96.7 11.5 %collective-permute-start.15 = (bf16[160,512]{1,0:T(8,128)(2,1)S(1)}, bf16[160,512]{1,0:T(8,128)(2,1)S(1)}, u32[]{:S(2)}, u32[]{:S(2)}) collective-permute-start(bf16[160,512]{1,0:T(8,128)(2,1)S(1)} %slice.18), channel_id=1, source_target_pairs={{0,2},{1,3},{2,4},{3,5},{4,6},{5,7},{6,0},{7,1},{8,10},{9,11},{10,... | collective-permute-start | bytes 491528 | tf_op jit(solution)/shard_map/ppermute | solution.py:407
  96.8 12.3 %collective-permute-start.17 = (bf16[160,512]{1,0:T(8,128)(2,1)S(1)}, bf16[160,512]{1,0:T(8,128)(2,1)}, u32[]{:S(2)}, u32[]{:S(2)}) collective-permute-start(bf16[160,512]{1,0:T(8,128)(2,1)S(1)} %slice.19), channel_id=1, source_target_pairs={{0,6},{1,7},{2,0},{3,1},{4,2},{5,3},{6,4},{7,5},{8,14},{9,15},{10,... | collective-permute-start | bytes 491528 | tf_op jit(solution)/shard_map/ppermute | solution.py:407
  104.7 17.0 %collective-permute-start.18 = (bf16[320,512]{1,0:T(8,128)(2,1)S(1)}, bf16[320,512]{1,0:T(8,128)(2,1)}, u32[]{:S(2)}, u32[]{:S(2)}) collective-permute-start(bf16[320,512]{1,0:T(8,128)(2,1)S(1)} %collective-permute-done.10.refs_0_), channel_id=1, source_target_pairs={{0,1},{1,0},{2,3},{3,2},{4,5},{5,4},{6,7},{7,6},{8,9},{9,8},{10,11... | collective-permute-start | bytes 983048 | tf_op jit(solution)/shard_map/ppermute | solution.py:407
  106.0 15.6 %collective-permute-start.19 = (bf16[320,512]{1,0:T(8,128)(2,1)}, bf16[320,512]{1,0:T(8,128)(2,1)}, u32[]{:S(2)}, u32[]{:S(2)}) collective-permute-start(bf16[320,512]{1,0:T(8,128)(2,1)} %collective-permute-done.12.refs_1_), channel_id=1, source_target_pairs={{0,1},{1,0},{2,3},{3,2},{4,5},{5,4},{6,7},{7,6},{8,9},{9,8},{10,11... | collective-permute-start | bytes 983048 | tf_op jit(solution)/shard_map/ppermute | solution.py:407
  108.2 3.9 %copy-start.10 = (bf16[160,512]{1,0:T(8,128)(2,1)}, bf16[160,512]{1,0:T(8,128)(2,1)S(1)}, u32[]{:S(2)}) copy-start(bf16[160,512]{1,0:T(8,128)(2,1)S(1)} %collective-permute-done.15.refs_2_) | copy-start | bytes 491524
  108.2 3.2 %collective-permute-start.20 = (bf16[160,512]{1,0:T(8,128)(2,1)S(1)}, bf16[160,512]{1,0:T(8,128)(2,1)S(1)}, u32[]{:S(2)}, u32[]{:S(2)}) collective-permute-start(bf16[160,512]{1,0:T(8,128)(2,1)S(1)} %collective-permute-done.15.refs_2_), channel_id=1, source_target_pairs={{0,1},{1,0},{2,3},{3,2},{4,5},{5,4},{6,7},{7,6},{8,9},{9,8},{10,11... | collective-permute-start | bytes 491528 | tf_op jit(solution)/shard_map/ppermute | solution.py:407
  109.1 12.6 %collective-permute-start.21 = (bf16[160,512]{1,0:T(8,128)(2,1)}, bf16[160,512]{1,0:T(8,128)(2,1)}, u32[]{:S(2)}, u32[]{:S(2)}) collective-permute-start(bf16[160,512]{1,0:T(8,128)(2,1)} %collective-permute-done.17.refs_3_), channel_id=1, source_target_pairs={{0,1},{1,0},{2,3},{3,2},{4,5},{5,4},{6,7},{7,6},{8,9},{9,8},{10,11... | collective-permute-start | bytes 491528 | tf_op jit(solution)/shard_map/ppermute | solution.py:407
  111.4 0.7 copy-start.12
  112.1 13.8 %collective-permute-start.11 = (bf16[160,512]{1,0:T(8,128)(2,1)}, bf16[160,512]{1,0:T(8,128)(2,1)S(1)}, u32[]{:S(2)}, u32[]{:S(2)}) collective-permute-start(bf16[160,512]{1,0:T(8,128)(2,1)} %slice.16), channel_id=1, source_target_pairs={{0,2},{1,3},{2,4},{3,5},{4,6},{5,7},{6,0},{7,1},{8,10},{9,11},{10,... | collective-permute-start | bytes 491528 | tf_op jit(solution)/shard_map/ppermute | solution.py:407
  112.1 1.1 copy-start.8
  113.2 12.7 %collective-permute-start.13 = (bf16[160,512]{1,0:T(8,128)(2,1)}, bf16[160,512]{1,0:T(8,128)(2,1)}, u32[]{:S(2)}, u32[]{:S(2)}) collective-permute-start(bf16[160,512]{1,0:T(8,128)(2,1)} %slice.17), channel_id=1, source_target_pairs={{0,6},{1,7},{2,0},{3,1},{4,2},{5,3},{6,4},{7,5},{8,14},{9,15},{10,... | collective-permute-start | bytes 491528 | tf_op jit(solution)/shard_map/ppermute | solution.py:407
  115.9 1.3 %copy-start.9 = (bf16[1280,512]{1,0:T(8,128)(2,1)S(1)}, bf16[1280,512]{1,0:T(8,128)(2,1)}, u32[]{:S(2)}) copy-start(bf16[1280,512]{1,0:T(8,128)(2,1)} %copy-done.8) | copy-start | bytes 3932164
  119.8 1.9 %copy-start.11 = (bf16[160,512]{1,0:T(8,128)(2,1)S(1)}, bf16[160,512]{1,0:T(8,128)(2,1)}, u32[]{:S(2)}) copy-start(bf16[160,512]{1,0:T(8,128)(2,1)} %copy-done.10) | copy-start | bytes 491524
  119.8 1.9 %copy-start.13 = (bf16[160,512]{1,0:T(8,128)(2,1)S(1)}, bf16[160,512]{1,0:T(8,128)(2,1)}, u32[]{:S(2)}) copy-start(bf16[160,512]{1,0:T(8,128)(2,1)} %copy-done.12) | copy-start | bytes 491524
  121.7 1.5 %copy-start.3 = (bf16[192,5120]{1,0:T(8,128)(2,1)S(1)}, bf16[192,5120]{1,0:T(8,128)(2,1)}, u32[]{:S(2)}) copy-start(bf16[192,5120]{1,0:T(8,128)(2,1)} %side_by_side.1) | copy-start | bytes 5898244
  126.8 2.3 %collective-permute-start.23 = (bf16[320,512]{1,0:T(8,128)(2,1)S(1)}, bf16[320,512]{1,0:T(8,128)(2,1)S(1)}, u32[]{:S(2)}, u32[]{:S(2)}) collective-permute-start(bf16[320,512]{1,0:T(8,128)(2,1)S(1)} %pad_maximum_fusion), channel_id=1, source_target_pairs={{0,1},{1,0},{2,3},{3,2},{4,5},{5,4},{6,7},{7,6},{8,9},{9,8},{10,11... | collective-permute-start | bytes 983048 | tf_op jit(solution)/shard_map/ppermute | solution.py:407

commit v3 on v2

--- a/solution.py
+++ b/solution.py
@@ -15,6 +15,7 @@
 adam_eps = 1e-08
 
 NX = 4
+FRONT_CHUNKS = 4
 
 
 def along_x(k):
@@ -23,10 +24,6 @@
 
 SWAP_CORE = [(i, i ^ 1) for i in range(16)]
 SWAP_Y = [(i, i ^ 8) for i in range(16)]
-
-NZ = 4
-RINGS_Z = [[0, 1, 2, 3], [4, 5, 6, 7]]
-DOWN_Y = [(NZ + z, z) for z in range(NZ)]
 
 
 def params(mib):
@@ -76,8 +73,8 @@
 
 def front_kernel(parts, x_hbm, w_hbm, gain_ref, hgain_ref, cot_ref, after_ref, kgs_ref, term_hbm, xv, wv, tv, acc, kgv, in_sems, out_sems):
     rows, width = xv.shape
-    blk = width // parts
-    spans = [pl.ds(c * blk, blk) for c in range(parts)]
+    step = width // FRONT_CHUNKS
+    spans = [pl.ds(c * step, step) for c in range(FRONT_CHUNKS)]
     loads = []
     for c, span in enumerate(spans):
         loads.append(
@@ -118,7 +115,9 @@
         dots += jnp.sum(kg.astype(jnp.float32) * raw, axis=-1, keepdims=True)
     coef = inv * inv * dots / width
     stores = []
-    for c, span in enumerate(spans):
+    blk = width // parts
+    for c in range(parts):
+        span = pl.ds(c * blk, blk)
         back = lax.dot_general(
             kgv[...], wv[span, :], (((1,), (1,)), ((), ())), preferred_element_type=jnp.float32
         )
@@ -150,7 +149,7 @@
             pltpu.VMEM((parts, rows, blk), jnp.bfloat16),
             pltpu.VMEM((rows, kv), jnp.float32),
             pltpu.VMEM((rows, kv), jnp.bfloat16),
-            pltpu.SemaphoreType.DMA((2 * parts,)),
+            pltpu.SemaphoreType.DMA((2 * FRONT_CHUNKS,)),
             pltpu.SemaphoreType.DMA((parts,)),
         ],
         compiler_params=params(60),
@@ -159,65 +158,63 @@
     )(acts, weight, gain, head_gain, cot, after)
 
 
-def total_kernel(z_ref, t_ref, up_ref, after_ref, out_ref):
-    total = up_ref[...].astype(jnp.float32)
-    for s in range(t_ref.shape[0]):
-        total = total + t_ref[s].astype(jnp.float32)
-    out_ref[...] = total.astype(jnp.bfloat16)
-
-
-def half_total(got, upstream, z, after):
+def row_chunks(rows, count):
+    step = rows // count
+    return [pl.ds(c * step, step) for c in range(count)]
+
+
+def suffix_kernel(chunks, t_hbm, up_hbm, after_ref, out_hbm, tv, uv, ov, in_sems, out_sems):
+    parts, rows, blk = tv.shape
+    cols = pl.ds(pl.multiple_of(lax.axis_index("section") * blk, HEAD), blk)
+    spans = row_chunks(rows, chunks)
+    loads, stores = [], []
+    for c, span in enumerate(spans):
+        loads.append(
+            (
+                pltpu.make_async_copy(t_hbm.at[:, span], tv.at[:, span], in_sems.at[2 * c]),
+                pltpu.make_async_copy(up_hbm.at[span, cols], uv.at[span], in_sems.at[2 * c + 1]),
+            )
+        )
+        for one in loads[c]:
+            one.start()
+    for c, span in enumerate(spans):
+        for one in loads[c]:
+            one.wait()
+        total = uv[span, :].astype(jnp.float32)
+        for s in reversed(range(parts)):
+            total = total + tv[s, span, :].astype(jnp.float32)
+            ov[s, span, :] = total.astype(jnp.bfloat16)
+        stores.append(pltpu.make_async_copy(ov.at[:, span], out_hbm.at[:, span], out_sems.at[c]))
+        stores[c].start()
+    for one in stores:
+        one.wait()
+
+
+def row_chunks(rows, count):
+    step = rows // count
+    return [pl.ds(c * step, step) for c in range(count)]
+
+
+def suffix_sums(got, upstream, after):
     parts, rows, blk = got.shape
-    tile = 96
-    return pl.pallas_call(
-        total_kernel,
-        grid_spec=pltpu.PrefetchScalarGridSpec(
-            num_scalar_prefetch=1,
-            grid=(rows // tile,),
-            in_specs=[
-                pl.BlockSpec((parts, tile, blk), lambda i, z: (0, i, 0)),
-                pl.BlockSpec((tile, blk), lambda i, z: (i, z[0])),
-                pl.BlockSpec(memory_space=pl.ANY),
-            ],
-            out_specs=pl.BlockSpec((tile, blk), lambda i, z: (i, 0)),
-        ),
-        out_shape=jax.ShapeDtypeStruct((rows, blk), jnp.bfloat16),
-        compiler_params=params(16),
-        cost_estimate=cost(parts * rows * blk, 2 * parts * rows * blk),
-        name="half_total",
-    )(z, got, upstream, after)
-
-
-def suffix_kernel(z_ref, t_ref, up_ref, above_ref, after_ref, out_ref):
-    upper = z_ref[1] == 1
-    base = jnp.where(upper, up_ref[...].astype(jnp.float32), above_ref[...].astype(jnp.float32))
-    total = base
-    for s in reversed(range(t_ref.shape[0])):
-        total = total + t_ref[s].astype(jnp.float32)
-        out_ref[s] = total.astype(jnp.bfloat16)
-
-
-def suffix_sums(got, upstream, above, z, after):
-    parts, rows, blk = got.shape
-    tile = 96
-    return pl.pallas_call(
-        suffix_kernel,
-        grid_spec=pltpu.PrefetchScalarGridSpec(
-            num_scalar_prefetch=1,
-            grid=(rows // tile,),
-            in_specs=[
-                pl.BlockSpec((parts, tile, blk), lambda i, z: (0, i, 0)),
-                pl.BlockSpec((tile, blk), lambda i, z: (i, z[0])),
-                pl.BlockSpec((tile, blk), lambda i, z: (i, 0)),
-                pl.BlockSpec(memory_space=pl.ANY),
-            ],
-            out_specs=pl.BlockSpec((parts, tile, blk), lambda i, z: (0, i, 0)),
-        ),
+    chunks = 4
+    anywhere = pl.BlockSpec(memory_space=pl.ANY)
+    return pl.pallas_call(
+        lambda *refs: suffix_kernel(chunks, *refs),
+        in_specs=[anywhere] * 3,
+        out_specs=anywhere,
         out_shape=jax.ShapeDtypeStruct(got.shape, jnp.bfloat16),
-        compiler_params=params(16),
+        scratch_shapes=[
+            pltpu.VMEM(got.shape, jnp.bfloat16),
+            pltpu.VMEM((rows, blk), jnp.bfloat16),
+            pltpu.VMEM(got.shape, jnp.bfloat16),
+            pltpu.SemaphoreType.DMA((2 * chunks,)),
+            pltpu.SemaphoreType.DMA((chunks,)),
+        ],
+        compiler_params=params(60),
         cost_estimate=cost(parts * rows * blk, 4 * parts * rows * blk),
         name="suffix_sums",
-    )(z, got, upstream, above, after)
+    )(got, upstream, after)
 
 
 def lay_kernel(in_ref, out_ref):
@@ -238,32 +235,44 @@
     )(got)
 
 
-def wgrad_kernel(x_hbm, up, down, far, k0, k1, k3, k2, keep_ref, send_ref, av, kv, full, sems):
+def wgrad_kernel(x_hbm, up, down, far, k0, k1, k3, k2, keep_hbm, send_hbm, av, kv, full, low, in_sems, out_sems):
     rows, wide = up.shape
     blk = wide // 2
+    half = blk // 2
+    loads = []
+    for n, k in enumerate((k0, k1, k3, k2)):
+        loads.append(pltpu.make_async_copy(k, kv.at[pl.ds(n * rows, rows)], in_sems.at[n]))
+        loads[n].start()
     cols = chip_columns(blk, 0)
-    moves = [
-        (x_hbm.at[:, cols[0]], av.at[pl.ds(0, rows), pl.ds(0, blk)]),
-        (x_hbm.at[:, cols[1]], av.at[pl.ds(0, rows), pl.ds(blk, blk)]),
-        (up, av.at[pl.ds(rows, rows)]),
-        (down, av.at[pl.ds(2 * rows, rows)]),
-        (far, av.at[pl.ds(3 * rows, rows)]),
-        (k0, kv.at[pl.ds(0, rows)]),
-        (k1, kv.at[pl.ds(rows, rows)]),
-        (k3, kv.at[pl.ds(2 * rows, rows)]),
-        (k2, kv.at[pl.ds(3 * rows, rows)]),
-    ]
-    run_copies(moves, sems)
-    half = keep_ref.shape[1]
+    parts = []
+    for y in range(2):
+        span = pl.ds(y * blk, blk)
+        srcs = (x_hbm.at[:, cols[y]], up.at[:, span], down.at[:, span], far.at[:, span])
+        group = []
+        for n, src in enumerate(srcs):
+            dst = av.at[pl.ds(n * rows, rows), span]
+            group.append(pltpu.make_async_copy(src, dst, in_sems.at[4 + 4 * y + n]))
+            group[n].start()
+        parts.append(group)
+    for one in loads:
+        one.wait()
     core = lax.rem(lax.axis_index("dp"), 2)
     own = pl.multiple_of(core * half, half)
     other = pl.multiple_of((1 - core) * half, half)
+    stores = []
     for y in range(2):
-        full[...] = lax.dot_general(
+        for one in parts[y]:
+            one.wait()
+        full[y] = lax.dot_general(
             av[:, y * blk : (y + 1) * blk], kv[...], (((0,), (0,)), ((), ())), preferred_element_type=jnp.float32
         )
-        keep_ref[y] = full[pl.ds(own, half), :]
-        send_ref[y] = full[pl.ds(other, half), :].astype(jnp.bfloat16)
+        low[y] = full[y, pl.ds(other, half), :].astype(jnp.bfloat16)
+        stores.append(pltpu.make_async_copy(full.at[y, pl.ds(own, half)], keep_hbm.at[y], out_sems.at[2 * y]))
+        stores.append(pltpu.make_async_copy(low.at[y], send_hbm.at[y], out_sems.at[2 * y + 1]))
+        stores[2 * y].start()
+        stores[2 * y + 1].start()
+    for one in stores:
+        one.wait()
 
 
 def wgrad(acts, got, kgs, got_kgs):
@@ -272,16 +281,17 @@
     kv = kgs.shape[1]
     half = blk // 2
     anywhere = pl.BlockSpec(memory_space=pl.ANY)
-    inside = pl.BlockSpec(memory_space=pltpu.VMEM)
     return pl.pallas_call(
         wgrad_kernel,
         in_specs=[anywhere] * 8,
-        out_specs=[inside, inside],
+        out_specs=[anywhere, anywhere],
         scratch_shapes=[
             pltpu.VMEM((4 * rows, 2 * blk), jnp.bfloat16),
             pltpu.VMEM((4 * rows, kv), jnp.bfloat16),
-            pltpu.VMEM((blk, kv), jnp.float32),
-            pltpu.SemaphoreType.DMA((9,)),
+            pltpu.VMEM((2, blk, kv), jnp.float32),
+            pltpu.VMEM((2, half, kv), jnp.bfloat16),
+            pltpu.SemaphoreType.DMA((12,)),
+            pltpu.SemaphoreType.DMA((4,)),
         ],
         out_shape=[
             jax.ShapeDtypeStruct((2, half, kv), jnp.float32),
@@ -350,17 +360,17 @@
     )(here, got, gain, master, first, second)
 
 
-def place(plan, bases, blocks, rows, kv, whole, after):
-    prior = ([] if whole is None else [whole]) + list(after)
+def place(plan, bases, blocks, rows, kv, whole):
+    prior = [] if whole is None else [whole]
     count = len(blocks)
+    block = rows // 16
 
     def kernel(base_ref, *refs):
         ins, out, sems = refs[:count], refs[-2], refs[-1]
         moves = []
-        for which, index, n, slot, shift in plan:
-            src = ins[which].at[pl.ds(index, n)]
-            at = pl.multiple_of(base_ref[slot] + shift, 32)
-            moves.append((src, out.at[pl.ds(at, n)]))
+        for which, index, slot in plan:
+            at = pl.multiple_of(base_ref[slot], 32)
+            moves.append((ins[which].at[pl.ds(index, block)], out.at[pl.ds(at, block)]))
         run_copies(moves, sems)
 
     return pl.pallas_call(
@@ -373,7 +383,7 @@
         scratch_shapes=[pltpu.SemaphoreType.DMA((len(plan),))],
         input_output_aliases={} if whole is None else {1 + count: 0},
         compiler_params=params(16),
-        cost_estimate=cost(0, 4 * kv * sum(p[2] for p in plan)),
+        cost_estimate=cost(0, 4 * kv * len(plan) * block),
         name="place",
     )(bases, *blocks, *prior)
 
@@ -401,9 +411,8 @@
     )(*blocks)
 
 
-def gather_rows(own, y, x, core, last):
+def gather_rows(own, y, x, core):
     rows, kv = own.shape
-    half = rows // 2
     send = lambda block, perm: lax.ppermute(block, "dp", perm)
     up, down = along_x(1), along_x(-1)
     yr = send(own, SWAP_Y)
@@ -411,10 +420,8 @@
     b = send(own, down)
     a2 = send(yr, up)
     b2 = send(yr, down)
-    f = send(a[:half], up)
-    g = send(b[half:], down)
-    f2 = send(a2[:half], up)
-    g2 = send(b2[half:], down)
+    e = send(own, along_x(2))
+    e2 = send(yr, along_x(2))
     order = (0, -1, 1, 2)
     table = []
     for dy in range(2):
@@ -425,31 +432,25 @@
                 table.append((yy * 8 + lax.rem(x + dx + NX, NX) * 2 + cc) * rows)
     bases = jnp.stack(table).astype(jnp.int32)
 
-    def plan_of(entries, dc):
-        return [
-            (n, block.shape[0], (dy * 4 + order.index(dx)) * 2 + dc, shift)
-            for n, (block, dy, dx, shift) in enumerate(entries)
-        ]
-
-    def put(entries, swapped, whole, after=()):
-        blocks = [e[0] for e in entries]
-        plan = [(n, 0, r, slot, shift) for n, r, slot, shift in plan_of(entries, 0)]
-        at = 0
-        for n, r, slot, shift in plan_of(entries, 1):
+    def put(entries, swapped, whole):
+        blocks = [one[0] for one in entries]
+        plan = []
+        for n, (block, dy, dx) in enumerate(entries):
+            slot = (dy * 4 + order.index(dx)) * 2
+            plan.append((n, 0, slot))
             if len(swapped) == 1:
-                plan.append((len(blocks), at, r, slot, shift))
-                at += r
+                plan.append((len(blocks), n * rows, slot + 1))
             else:
-                plan.append((len(blocks) + n, 0, r, slot, shift))
-        return place(plan, bases, blocks + swapped, 16 * rows, kv, whole, after)
-
-    near = [(own, 0, 0, 0), (a, 0, -1, 0), (b, 0, 1, 0), (yr, 1, 0, 0)]
-    whole = put(near, [send(stacked([e[0] for e in near]), SWAP_CORE)], None)
-    middle = [(a2, 1, -1, 0), (b2, 1, 1, 0), (f, 0, 2, 0), (g, 0, 2, half)]
-    whole = put(middle, [send(e[0], SWAP_CORE) for e in middle], whole, (last,))
-    f2, g2, whole = lax.optimization_barrier((f2, g2, whole))
-    swapped = send(jnp.concatenate([f2, g2]), SWAP_CORE)
-    return put([(f2, 1, 2, 0), (g2, 1, 2, half)], [swapped], whole)
+                plan.append((len(blocks) + n, 0, slot + 1))
+        return place(plan, bases, blocks + swapped, 16 * rows, kv, whole)
+
+    near = [(own, 0, 0), (a, 0, -1), (b, 0, 1), (yr, 1, 0)]
+    whole = put(near, [send(stacked([one[0] for one in near]), SWAP_CORE)], None)
+    a2, e2 = lax.optimization_barrier((a2, e2))
+    middle = [(a2, 1, -1), (b2, 1, 1), (e, 0, 2)]
+    whole = put(middle, [send(one[0], SWAP_CORE) for one in middle], whole)
+    e2, whole = lax.optimization_barrier((e2, whole))
+    return put([(e2, 1, 2)], [send(e2, SWAP_CORE)], whole)
 
 
 def body(
@@ -463,6 +464,7 @@
     first_moment,
     second_moment,
 ):
+    sections = lax.axis_size("section")
     micro, tok, width = activations.shape[1:]
     rows = micro * tok
     acts = activations.reshape(rows, width)
@@ -470,26 +472,20 @@
     kv = weight.shape[1]
     me = lax.axis_index("dp")
     y, x, core = me // 8, lax.rem(me // 2, NX), lax.rem(me, 2)
-    section = lax.axis_index("section")
-    zpos = jnp.stack([lax.rem(section, NZ), section // NZ]).astype(jnp.int32)
     upstream = upstream.reshape(rows, width)
 
     cut = cut_columns(acts)
     got = [lax.ppermute(one, "dp", along_x(k)) for one, k in zip(cut, (1, -1, 2))]
-    kgs, term = front(acts, norm_gain, weight, key_gain, key_cotangent.reshape(rows, kv), NZ, cut[0])
+    kgs, term = front(acts, norm_gain, weight, key_gain, key_cotangent.reshape(rows, kv), sections, cut[0])
     got_kgs = [lax.ppermute(kgs, "dp", along_x(1)), lax.ppermute(kgs, "dp", along_x(-1))]
     kgs_late, *got = lax.optimization_barrier((kgs, *got))
-    term, got[0], got[1], got[2], *got_kgs = lax.optimization_barrier((term, *got, *got_kgs))
     got_kgs.append(lax.ppermute(kgs_late, "dp", along_x(2)))
-    theirs = lax.all_to_all(term, "section", 0, 0, axis_index_groups=RINGS_Z)
+    theirs = lax.all_to_all(term, "section", 0, 0)
 
     keep, away = wgrad(acts, got, kgs, got_kgs)
     here, there = merge(keep, lax.ppermute(away, "dp", SWAP_CORE))
-    ours = half_total(theirs, upstream, zpos, here)
-
-    above = lax.ppermute(ours, "section", DOWN_Y)
-    sums = suffix_sums(theirs, upstream, above, zpos, here)
-    mine = lax.all_to_all(sums, "section", 0, 0, axis_index_groups=RINGS_Z)
+    sums = suffix_sums(theirs, upstream, here)
+    mine = lax.all_to_all(sums, "section", 0, 0)
     input_grad = side_by_side(mine).reshape(activations.shape)
 
     own_rows = here.shape[0]
@@ -497,7 +493,7 @@
     new_master, new_first, new_second, own = adam(
         here, lax.ppermute(there, "dp", SWAP_Y), gain_rows, master, first_moment, second_moment
     )
-    new_weight = gather_rows(own, y, x, core, input_grad)
+    new_weight = gather_rows(own, y, x, core)
     return (input_grad, new_weight[None], new_master, new_first, new_second)
 
 

time: 132 us -> 118 us (0.89)
  local copies, waits for them, and re-layouts: 17.1 us -> 5.24 us
  waiting for transfers between devices: 35.7 us -> 41.3 us
  starting transfers between devices: 43.4 us -> 37.9 us
    ppermute x15 -> x12, waiting for transfers between devices: 8.63 us -> 18.3 us  [gather_rows(): send = lambda block, perm: lax.ppermute(block, 'dp', perm)]
    unnamed x44 -> x26, local copies, waits for them, and re-layouts: 13.1 us -> 3.59 us
    ppermute x1, waiting for transfers between devices: 0.01 us -> 5.95 us  [body(): lax.ppermute(there, 'dp', SWAP_Y)]
    ppermute x15 -> x12, starting transfers between devices: 20 us -> 15 us  [gather_rows(): send = lambda block, perm: lax.ppermute(block, 'dp', perm)]
    all_to_all x2, waiting for transfers between devices: 3.35 us -> 0.01 us  [the longest x1 0.01 us: body(): theirs = lax.all_to_all(term, 'section', 0, 0)]
    ppermute x1, waiting for transfers between devices: 6.32 us -> 3.45 us  [body(): got_kgs.append(lax.ppermute(kgs_late, 'dp', along_x(2)))]
    all_to_all x2, starting transfers between devices: 8.76 us -> 11.5 us  [the longest x1 6.19 us: body(): theirs = lax.all_to_all(term, 'section', 0, 0)]
    slice x4 -> x0, local copies, waits for them, and re-layouts: 2.27 us -> none  [the longest x1 1.58 us: gather_rows(): g2 = send(b2[half:], down)]
  transfers between devices with their start and end apart: 26 -> 22, of which waited for: 9 -> 8; matrix products, arithmetic and copies ran while one was open for 3% -> 1% of each run, Pallas kernels for 22% -> 24%
where the time goes in v3:
time: 118 us; the launch traced here: 117 us
  waiting for transfers between devices  41.3 us (35%)
  starting transfers between devices  37.9 us (32%)
  Pallas kernels  32.1 us (27%)
  local copies, waits for them, and re-layouts  5.24 us (4%)
    ppermute x12, waiting for transfers between devices, gather_rows(): send = lambda block, perm: lax.ppermute(block, 'dp', perm)  18.3 us
    ppermute x12, starting transfers between devices, gather_rows(): send = lambda block, perm: lax.ppermute(block, 'dp', perm)  15 us
    pallas_call x1, Pallas kernels, front(): pl.pallas_call(lambda *refs: front_kernel(parts, *refs), in_specs=[anywhe...  8.02 us
    ppermute x3, waiting for transfers between devices, body(): lax.ppermute(one, 'dp', along_x(k))  7.97 us
    pallas_call x3, Pallas kernels, place(): pl.pallas_call(kernel, in_specs=[pl.BlockSpec(memory_space=pltpu.SMEM)] +...  7.11 us
    all_to_all x1, starting transfers between devices, body(): theirs = lax.all_to_all(term, 'section', 0, 0)  6.19 us
    ppermute x1, waiting for transfers between devices, body(): lax.ppermute(there, 'dp', SWAP_Y)  5.95 us
    all_to_all x1, starting transfers between devices, body(): mine = lax.all_to_all(sums, 'section', 0, 0)  5.29 us
  transfers between devices with their start and end apart: 22, of which 8 were waited for; matrix products, arithmetic and copies ran while one was open for 1% of the time, Pallas kernels for 24%

profile of v3, /device:TPU:1, one launch (start us, length us, event | category | flops | bytes accessed | tf_op | source)
XLA Modules:
  0.0 117.4 jit_solution(3430314385745567284)
XLA Ops:
  0.6 2.6 %cut_columns.1 = (bf16[192,1280]{1,0:T(8,128)(2,1)}, bf16[192,1280]{1,0:T(8,128)(2,1)}, bf16[192,1280]{1,0:T(8,128)(2,1)}) custom-call(bf16[192,5120]{1,0:T(8,128)(2,1)} %bitcast.25), custom_call_target="tpu_custom_call" | custom-call | bytes 1 | tf_op jit(solution)/shard_map/cut_columns/pallas_call | solution.py:62
  3.3 3.4 %collective-permute-start.1 = (bf16[192,1280]{1,0:T(8,128)(2,1)}, bf16[192,1280]{1,0:T(8,128)(2,1)S(1)}, u32[]{:S(2)}, u32[]{:S(2)}) collective-permute-start(bf16[192,1280]{1,0:T(8,128)(2,1)} %get-tuple-element.29), channel_id=1, source_target_pairs={{0,6},{1,7},{2,0},{3,1},{4,2},{5,3},{6,4},{7,5},{8,14},{9,15},{10,... | collective-permute-start | bytes 1474568 | tf_op jit(solution)/shard_map/ppermute | solution.py:478
  6.7 0.5 collective-permute-start.2
  7.2 0.6 collective-permute-start
  7.8 8.0 %front.1 = (bf16[192,512]{1,0:T(8,128)(2,1)}, bf16[8,192,640]{2,1,0:T(8,128)(2,1)}) custom-call(bf16[192,5120]{1,0:T(8,128)(2,1)} %bitcast.26, bf16[5120,512]{1,0:T(8,128)(2,1)} %bitcast.28, f32[1,5120]{1,0:T(1,128)} %refs_2_.1, f32[1,128]{1,0:T(1,128)} %refs_3_.1, bf16[192,512]{1,0:T(8,128)(2,1)} %bitcast.31, bf16[192,1280]{1,0:T(8,128)(2,1)} %get-tuple-element.26.refs_5_), custom_call_target="tpu_custom_call" | custom-call | bytes 1 | tf_op jit(solution)/shard_map/front/pallas_call | solution.py:138
  15.8 6.2 %all-to-all-start = ((bf16[8,192,640]{2,1,0:T(8,128)(2,1)}), bf16[8,192,640]{2,1,0:T(8,128)(2,1)}, u32[]{:S(2)}, u32[]{:S(2)}) async-start(bf16[8,192,640]{2,1,0:T(8,128)(2,1)} %get-tuple-element.27), calls=%async_computation | async-start | bytes 3932160 | tf_op jit(solution)/shard_map/all_to_all | solution.py:483
  22.0 2.1 %collective-permute-start.4 = (bf16[192,512]{1,0:T(8,128)(2,1)S(1)}, bf16[192,512]{1,0:T(8,128)(2,1)S(1)}, u32[]{:S(2)}, u32[]{:S(2)}) collective-permute-start(bf16[192,512]{1,0:T(8,128)(2,1)S(1)} %copy-done.9), channel_id=1, source_target_pairs={{0,6},{1,7},{2,0},{3,1},{4,2},{5,3},{6,4},{7,5},{8,14},{9,15},{10,... | collective-permute-start | bytes 589832 | tf_op jit(solution)/shard_map/ppermute | solution.py:480
  24.2 0.0 copy-start.6
  24.2 8.0 %collective-permute-done.up = bf16[192,1280]{1,0:T(8,128)(2,1)S(1)} collective-permute-done((bf16[192,1280]{1,0:T(8,128)(2,1)}, bf16[192,1280]{1,0:T(8,128)(2,1)S(1)}, u32[]{:S(2)}, u32[]{:S(2)}) %collective-permute-start) | collective-permute-done | bytes 491552 | tf_op jit(solution)/shard_map/ppermute | solution.py:478
  32.2 0.5 collective-permute-start.5
  32.7 3.7 %collective-permute-done.3.k1 = bf16[192,512]{1,0:T(8,128)(2,1)S(1)} collective-permute-done((bf16[192,512]{1,0:T(8,128)(2,1)S(1)}, bf16[192,512]{1,0:T(8,128)(2,1)S(1)}, u32[]{:S(2)}, u32[]{:S(2)}) %collective-permute-start.3) | collective-permute-done | bytes 196640 | tf_op jit(solution)/shard_map/ppermute | solution.py:480
  36.4 3.5 %collective-permute-done.5.k2 = bf16[192,512]{1,0:T(8,128)(2,1)S(1)} collective-permute-done((bf16[192,512]{1,0:T(8,128)(2,1)S(1)}, bf16[192,512]{1,0:T(8,128)(2,1)S(1)}, u32[]{:S(2)}, u32[]{:S(2)}) %collective-permute-start.5) | collective-permute-done | bytes 196640 | tf_op jit(solution)/shard_map/ppermute | solution.py:482
  39.9 0.7 copy-done.12
  40.5 4.1 %wgrad.1 = (f32[2,320,512]{2,1,0:T(8,128)}, bf16[2,320,512]{2,1,0:T(8,128)(2,1)}) custom-call(bf16[192,5120]{1,0:T(8,128)(2,1)} %bitcast.27, bf16[192,1280]{1,0:T(8,128)(2,1)} %copy-done.7, bf16[192,1280]{1,0:T(8,128)(2,1)} %copy-done.5, bf16[192,1280]{1,0:T(8,128)(2,1)} %copy-done.6, bf16[192,512]{1,0:T(8,128)(2,1)} %get-tuple-element.34.k0, ...), custom_call_target="tpu_custom_call" | custom-call | bytes 1 | tf_op jit(solution)/shard_map/wgrad/pallas_call | solution.py:284
  44.6 1.4 %collective-permute-start.6 = (bf16[2,320,512]{2,1,0:T(8,128)(2,1)}, bf16[2,320,512]{2,1,0:T(8,128)(2,1)S(1)}, u32[]{:S(2)}, u32[]{:S(2)}) collective-permute-start(bf16[2,320,512]{2,1,0:T(8,128)(2,1)} %get-tuple-element.36), channel_id=1, source_target_pairs={{0,1},{1,0},{2,3},{3,2},{4,5},{5,4},{6,7},{7,6},{8,9},{9,8},{10,11... | collective-permute-start | bytes 1966088 | tf_op jit(solution)/shard_map/ppermute | solution.py:486
  46.0 1.9 %collective-permute-done.6.got = bf16[2,320,512]{2,1,0:T(8,128)(2,1)S(1)} collective-permute-done((bf16[2,320,512]{2,1,0:T(8,128)(2,1)}, bf16[2,320,512]{2,1,0:T(8,128)(2,1)S(1)}, u32[]{:S(2)}, u32[]{:S(2)}) %collective-permute-start.6) | collective-permute-done | bytes 655392 | tf_op jit(solution)/shard_map/ppermute | solution.py:486
  47.9 1.3 %copy-done.2 = f32[2,320,512]{2,1,0:T(8,128)S(1)} copy-done((f32[2,320,512]{2,1,0:T(8,128)S(1)}, f32[2,320,512]{2,1,0:T(8,128)}, u32[]{:S(2)}) %copy-start.2) | copy-done | bytes 1310744
  49.2 0.1 merge.1
  49.4 0.0 copy-start
  49.4 0.8 copy-done
  50.2 2.9 %collective-permute-start.7 = (bf16[320,512]{1,0:T(8,128)(2,1)S(1)}, bf16[320,512]{1,0:T(8,128)(2,1)S(1)}, u32[]{:S(2)}, u32[]{:S(2)}) collective-permute-start(bf16[320,512]{1,0:T(8,128)(2,1)S(1)} %get-tuple-element.38), channel_id=1, source_target_pairs={{0,8},{1,9},{2,10},{3,11},{4,12},{5,13},{6,14},{7,15},{8,0},{9,1},... | collective-permute-start | bytes 983048 | tf_op jit(solution)/shard_map/ppermute | solution.py:494
  53.1 0.8 dynamic-slice_bitcast_fusion
  53.9 0.8 copy.16.gain
  54.7 6.0 %collective-permute-done.7.got = bf16[320,512]{1,0:T(8,128)(2,1)S(1)} collective-permute-done((bf16[320,512]{1,0:T(8,128)(2,1)S(1)}, bf16[320,512]{1,0:T(8,128)(2,1)S(1)}, u32[]{:S(2)}, u32[]{:S(2)}) %collective-permute-start.7) | collective-permute-done | bytes 327712 | tf_op jit(solution)/shard_map/ppermute | solution.py:494
  60.6 0.7 copy-done.8
  61.4 3.2 %adam.1 = (f32[1,320,512]{2,1,0:T(8,128)}, f32[1,320,512]{2,1,0:T(8,128)}, f32[1,320,512]{2,1,0:T(8,128)}, bf16[320,512]{1,0:T(8,128)(2,1)}) custom-call(f32[320,512]{1,0:T(8,128)} %copy-done, bf16[320,512]{1,0:T(8,128)(2,1)} %copy-done.8, f32[320,1]{1,0:T(8,128)} %copy.16.gain, f32[1,320,512]{2,1,0:T(8,128)} %master.1, f32[1,320,512]{2,1,0:T(8,128)} %first.1, ...), custom_call_target="tpu_custom_call" | custom-call | bytes 1 | tf_op jit(solution)/shard_map/adam/pallas_call | solution.py:351
  64.6 0.5 collective-permute-start.17
  65.1 1.0 collective-permute-start.16
  66.1 2.9 %collective-permute-start.8 = (bf16[320,512]{1,0:T(8,128)(2,1)}, bf16[320,512]{1,0:T(8,128)(2,1)S(1)}, u32[]{:S(2)}, u32[]{:S(2)}) collective-permute-start(bf16[320,512]{1,0:T(8,128)(2,1)} %get-tuple-element.39.refs_0_), channel_id=1, source_target_pairs={{0,8},{1,9},{2,10},{3,11},{4,12},{5,13},{6,14},{7,15},{8,0},{9,1},... | collective-permute-start | bytes 983048 | tf_op jit(solution)/shard_map/ppermute | solution.py:416
  69.0 2.5 %suffix_sums.1 = bf16[8,192,640]{2,1,0:T(8,128)(2,1)} custom-call(bf16[8,192,640]{2,1,0:T(8,128)(2,1)} %all-to-all-done.refs_0_, bf16[192,5120]{1,0:T(8,128)(2,1)} %bitcast.29, f32[320,512]{1,0:T(8,128)} %copy-done), custom_call_target="tpu_custom_call" | custom-call | bytes 1 | tf_op jit(solution)/shard_map/suffix_sums/pallas_call | solution.py:202
  71.5 5.3 %all-to-all-start.1 = ((bf16[8,192,640]{2,1,0:T(8,128)(2,1)}), bf16[8,192,640]{2,1,0:T(8,128)(2,1)S(1)}, u32[]{:S(2)}, u32[]{:S(2)}) async-start(bf16[8,192,640]{2,1,0:T(8,128)(2,1)} %suffix_sums.1), calls=%async_computation.1 | async-start | bytes 3932160 | tf_op jit(solution)/shard_map/all_to_all | solution.py:488
  76.8 1.5 %stacked.1 = bf16[1280,512]{1,0:T(8,128)(2,1)} custom-call(bf16[320,512]{1,0:T(8,128)(2,1)S(1)} %copy-done.1, bf16[320,512]{1,0:T(8,128)(2,1)S(1)} %collective-permute-done.16.refs_1_, bf16[320,512]{1,0:T(8,128)(2,1)S(1)} %collective-permute-done.17.refs_2_, bf16[320,512]{1,0:T(8,128)(2,1)S(1)} %collective-permute-done.8.refs_3_), custom_call_target="tpu_custom_call" | custom-call | bytes 1 | tf_op jit(solution)/shard_map/stacked/pallas_call | solution.py:402
  78.4 2.4 %collective-permute-start.18 = (bf16[1280,512]{1,0:T(8,128)(2,1)}, bf16[1280,512]{1,0:T(8,128)(2,1)}, u32[]{:S(2)}, u32[]{:S(2)}) collective-permute-start(bf16[1280,512]{1,0:T(8,128)(2,1)} %stacked.1), channel_id=1, source_target_pairs={{0,1},{1,0},{2,3},{3,2},{4,5},{5,4},{6,7},{7,6},{8,9},{9,8},{10,11... | collective-permute-start | bytes 3932168 | tf_op jit(solution)/shard_map/ppermute | solution.py:416
  80.8 0.5 collective-permute-start.12
  81.3 2.5 %collective-permute-start.10 = (bf16[320,512]{1,0:T(8,128)(2,1)S(1)}, bf16[320,512]{1,0:T(8,128)(2,1)S(1)}, u32[]{:S(2)}, u32[]{:S(2)}) collective-permute-start(bf16[320,512]{1,0:T(8,128)(2,1)S(1)} %collective-permute-done.8.refs_3_), channel_id=1, source_target_pairs={{0,4},{1,5},{2,6},{3,7},{4,0},{5,1},{6,2},{7,3},{8,12},{9,13},{10,... | collective-permute-start | bytes 983048 | tf_op jit(solution)/shard_map/ppermute | solution.py:416
  83.7 2.7 %collective-permute-start.11 = (bf16[320,512]{1,0:T(8,128)(2,1)S(1)}, bf16[320,512]{1,0:T(8,128)(2,1)}, u32[]{:S(2)}, u32[]{:S(2)}) collective-permute-start(bf16[320,512]{1,0:T(8,128)(2,1)S(1)} %collective-permute-done.8.refs_3_), channel_id=1, source_target_pairs={{0,6},{1,7},{2,0},{3,1},{4,2},{5,3},{6,4},{7,5},{8,14},{9,15},{10,... | collective-permute-start | bytes 983048 | tf_op jit(solution)/shard_map/ppermute | solution.py:416
  86.4 5.3 %collective-permute-done.12.refs_2_ = bf16[320,512]{1,0:T(8,128)(2,1)} collective-permute-done((bf16[320,512]{1,0:T(8,128)(2,1)S(1)}, bf16[320,512]{1,0:T(8,128)(2,1)}, u32[]{:S(2)}, u32[]{:S(2)}) %collective-permute-start.12) | collective-permute-done | bytes 327712 | tf_op jit(solution)/shard_map/ppermute | solution.py:416
  91.7 1.4 %collective-permute-start.15 = (bf16[320,512]{1,0:T(8,128)(2,1)}, bf16[320,512]{1,0:T(8,128)(2,1)}, u32[]{:S(2)}, u32[]{:S(2)}) collective-permute-start(bf16[320,512]{1,0:T(8,128)(2,1)} %collective-permute-done.12.refs_2_), channel_id=1, source_target_pairs={{0,1},{1,0},{2,3},{3,2},{4,5},{5,4},{6,7},{7,6},{8,9},{9,8},{10,11... | collective-permute-start | bytes 983048 | tf_op jit(solution)/shard_map/ppermute | solution.py:416
  93.1 5.5 %collective-permute-done.10.refs_0_ = bf16[320,512]{1,0:T(8,128)(2,1)S(1)} collective-permute-done((bf16[320,512]{1,0:T(8,128)(2,1)S(1)}, bf16[320,512]{1,0:T(8,128)(2,1)S(1)}, u32[]{:S(2)}, u32[]{:S(2)}) %collective-permute-start.10) | collective-permute-done | bytes 327712 | tf_op jit(solution)/shard_map/ppermute | solution.py:416
  98.6 7.5 %collective-permute-done.9.refs_0_ = bf16[320,512]{1,0:T(8,128)(2,1)} collective-permute-done((bf16[320,512]{1,0:T(8,128)(2,1)S(1)}, bf16[320,512]{1,0:T(8,128)(2,1)}, u32[]{:S(2)}, u32[]{:S(2)}) %collective-permute-start.9) | collective-permute-done | bytes 327712 | tf_op jit(solution)/shard_map/ppermute | solution.py:416
  106.1 0.5 collective-permute-start.14
  106.6 0.1 collective-permute-start.13
  106.7 0.1 stack.67.base_ref
  106.8 2.9 %place.3.refs_6_ = bf16[5120,512]{1,0:T(8,128)(2,1)} custom-call(s32[16]{0:T(128)S(1)} %stack.67.base_ref, bf16[320,512]{1,0:T(8,128)(2,1)S(1)} %copy-done.1, bf16[320,512]{1,0:T(8,128)(2,1)S(1)} %collective-permute-done.16.refs_1_, bf16[320,512]{1,0:T(8,128)(2,1)S(1)} %collective-permute-done.17.refs_2_, ...), custom_call_target="tpu_custom_call" | custom-call | bytes 1 | tf_op jit(solution)/shard_map/place/pallas_call | solution.py:376
  109.7 2.8 %place.4.refs_2_ = bf16[5120,512]{1,0:T(8,128)(2,1)} custom-call(s32[16]{0:T(128)S(1)} %stack.67.base_ref, bf16[320,512]{1,0:T(8,128)(2,1)} %collective-permute-done.9.refs_0_, bf16[320,512]{1,0:T(8,128)(2,1)} %collective-permute-done.11.refs_1_, bf16[320,512]{1,0:T(8,128)(2,1)} %collective-permute-done.12.refs_2_, ...), custom_call_target="tpu_custom_call", output_to_operand_aliasing={{}: (7, {})} | custom-call | bytes 1 | tf_op jit(solution)/shard_map/place/pallas_call | solution.py:376
  112.5 0.5 collective-permute-start.19
  113.0 2.9 %side_by_side.1 = bf16[192,5120]{1,0:T(8,128)(2,1)} custom-call(bf16[8,192,640]{2,1,0:T(8,128)(2,1)S(1)} %all-to-all-done.1.in_ref), custom_call_target="tpu_custom_call" | custom-call | bytes 1 | tf_op jit(solution)/shard_map/side_by_side/pallas_call | solution.py:226
  116.0 1.4 %place.5 = bf16[5120,512]{1,0:T(8,128)(2,1)} custom-call(s32[16]{0:T(128)S(1)} %stack.67.base_ref, bf16[320,512]{1,0:T(8,128)(2,1)S(1)} %copy-done.4, bf16[320,512]{1,0:T(8,128)(2,1)S(1)} %collective-permute-done.19.refs_1_, bf16[5120,512]{1,0:T(8,128)(2,1)} %place.4.refs_2_), custom_call_target="tpu_custom_call", output_to_operand_aliasing={{}: (3, {})} | custom-call | bytes 1 | tf_op jit(solution)/shard_map/place/pallas_call | solution.py:376
  (36 shorter events, 0.1 us)
Async XLA Ops:
  3.3 20.9 %collective-permute-start.1 = (bf16[192,1280]{1,0:T(8,128)(2,1)}, bf16[192,1280]{1,0:T(8,128)(2,1)S(1)}, u32[]{:S(2)}, u32[]{:S(2)}) collective-permute-start(bf16[192,1280]{1,0:T(8,128)(2,1)} %get-tuple-element.29), channel_id=1, source_target_pairs={{0,6},{1,7},{2,0},{3,1},{4,2},{5,3},{6,4},{7,5},{8,14},{9,15},{10,... | collective-permute-start | bytes 1474568 | tf_op jit(solution)/shard_map/ppermute | solution.py:478
  6.7 17.5 %collective-permute-start.2 = (bf16[192,1280]{1,0:T(8,128)(2,1)}, bf16[192,1280]{1,0:T(8,128)(2,1)S(1)}, u32[]{:S(2)}, u32[]{:S(2)}) collective-permute-start(bf16[192,1280]{1,0:T(8,128)(2,1)} %get-tuple-element.30), channel_id=1, source_target_pairs={{0,4},{1,5},{2,6},{3,7},{4,0},{5,1},{6,2},{7,3},{8,12},{9,13},{10,... | collective-permute-start | bytes 1474568 | tf_op jit(solution)/shard_map/ppermute | solution.py:478
  7.2 25.0 %collective-permute-start = (bf16[192,1280]{1,0:T(8,128)(2,1)}, bf16[192,1280]{1,0:T(8,128)(2,1)S(1)}, u32[]{:S(2)}, u32[]{:S(2)}) collective-permute-start(bf16[192,1280]{1,0:T(8,128)(2,1)} %get-tuple-element.26.refs_5_), channel_id=1, source_target_pairs={{0,2},{1,3},{2,4},{3,5},{4,6},{5,7},{6,0},{7,1},{8,10},{9,11},{10,... | collective-permute-start | bytes 1474568 | tf_op jit(solution)/shard_map/ppermute | solution.py:478
  15.8 6.2 %copy-start.9 = (bf16[192,512]{1,0:T(8,128)(2,1)S(1)}, bf16[192,512]{1,0:T(8,128)(2,1)}, u32[]{:S(2)}) copy-start(bf16[192,512]{1,0:T(8,128)(2,1)} %get-tuple-element.34.k0) | copy-start | bytes 589828
  15.8 53.2 %all-to-all-start = ((bf16[8,192,640]{2,1,0:T(8,128)(2,1)}), bf16[8,192,640]{2,1,0:T(8,128)(2,1)}, u32[]{:S(2)}, u32[]{:S(2)}) async-start(bf16[8,192,640]{2,1,0:T(8,128)(2,1)} %get-tuple-element.27), calls=%async_computation | async-start | bytes 3932160 | tf_op jit(solution)/shard_map/all_to_all | solution.py:483
  22.0 10.7 %collective-permute-start.4 = (bf16[192,512]{1,0:T(8,128)(2,1)S(1)}, bf16[192,512]{1,0:T(8,128)(2,1)S(1)}, u32[]{:S(2)}, u32[]{:S(2)}) collective-permute-start(bf16[192,512]{1,0:T(8,128)(2,1)S(1)} %copy-done.9), channel_id=1, source_target_pairs={{0,6},{1,7},{2,0},{3,1},{4,2},{5,3},{6,4},{7,5},{8,14},{9,15},{10,... | collective-permute-start | bytes 589832 | tf_op jit(solution)/shard_map/ppermute | solution.py:480
  24.2 12.2 %collective-permute-start.3 = (bf16[192,512]{1,0:T(8,128)(2,1)S(1)}, bf16[192,512]{1,0:T(8,128)(2,1)S(1)}, u32[]{:S(2)}, u32[]{:S(2)}) collective-permute-start(bf16[192,512]{1,0:T(8,128)(2,1)S(1)} %copy-done.9), channel_id=1, source_target_pairs={{0,2},{1,3},{2,4},{3,5},{4,6},{5,7},{6,0},{7,1},{8,10},{9,11},{10,... | collective-permute-start | bytes 589832 | tf_op jit(solution)/shard_map/ppermute | solution.py:480
  24.2 15.7 %copy-start.5 = (bf16[192,1280]{1,0:T(8,128)(2,1)}, bf16[192,1280]{1,0:T(8,128)(2,1)S(1)}, u32[]{:S(2)}) copy-start(bf16[192,1280]{1,0:T(8,128)(2,1)S(1)} %collective-permute-done.1.down) | copy-start | bytes 1474564
  24.2 15.6 %copy-start.6 = (bf16[192,1280]{1,0:T(8,128)(2,1)}, bf16[192,1280]{1,0:T(8,128)(2,1)S(1)}, u32[]{:S(2)}) copy-start(bf16[192,1280]{1,0:T(8,128)(2,1)S(1)} %collective-permute-done.2.far) | copy-start | bytes 1474564
  32.1 7.7 %copy-start.7 = (bf16[192,1280]{1,0:T(8,128)(2,1)}, bf16[192,1280]{1,0:T(8,128)(2,1)S(1)}, u32[]{:S(2)}) copy-start(bf16[192,1280]{1,0:T(8,128)(2,1)S(1)} %collective-permute-done.up) | copy-start | bytes 1474564
  32.2 7.7 %collective-permute-start.5 = (bf16[192,512]{1,0:T(8,128)(2,1)S(1)}, bf16[192,512]{1,0:T(8,128)(2,1)S(1)}, u32[]{:S(2)}, u32[]{:S(2)}) collective-permute-start(bf16[192,512]{1,0:T(8,128)(2,1)S(1)} %copy-done.9), channel_id=1, source_target_pairs={{0,4},{1,5},{2,6},{3,7},{4,0},{5,1},{6,2},{7,3},{8,12},{9,13},{10,... | collective-permute-start | bytes 589832 | tf_op jit(solution)/shard_map/ppermute | solution.py:482
  32.7 7.2 %copy-start.10 = (bf16[192,512]{1,0:T(8,128)(2,1)}, bf16[192,512]{1,0:T(8,128)(2,1)S(1)}, u32[]{:S(2)}) copy-start(bf16[192,512]{1,0:T(8,128)(2,1)S(1)} %collective-permute-done.4.k3) | copy-start | bytes 589828
  36.4 3.5 %copy-start.11 = (bf16[192,512]{1,0:T(8,128)(2,1)}, bf16[192,512]{1,0:T(8,128)(2,1)S(1)}, u32[]{:S(2)}) copy-start(bf16[192,512]{1,0:T(8,128)(2,1)S(1)} %collective-permute-done.3.k1) | copy-start | bytes 589828
  39.8 0.7 copy-start.12
  44.6 3.3 %collective-permute-start.6 = (bf16[2,320,512]{2,1,0:T(8,128)(2,1)}, bf16[2,320,512]{2,1,0:T(8,128)(2,1)S(1)}, u32[]{:S(2)}, u32[]{:S(2)}) collective-permute-start(bf16[2,320,512]{2,1,0:T(8,128)(2,1)} %get-tuple-element.36), channel_id=1, source_target_pairs={{0,1},{1,0},{2,3},{3,2},{4,5},{5,4},{6,7},{7,6},{8,9},{9,8},{10,11... | collective-permute-start | bytes 1966088 | tf_op jit(solution)/shard_map/ppermute | solution.py:486
  47.9 1.3 %copy-start.2 = (f32[2,320,512]{2,1,0:T(8,128)S(1)}, f32[2,320,512]{2,1,0:T(8,128)}, u32[]{:S(2)}) copy-start(f32[2,320,512]{2,1,0:T(8,128)} %get-tuple-element.35.keep) | copy-start | bytes 3932164
  49.4 0.8 copy-start
  50.2 10.4 %collective-permute-start.7 = (bf16[320,512]{1,0:T(8,128)(2,1)S(1)}, bf16[320,512]{1,0:T(8,128)(2,1)S(1)}, u32[]{:S(2)}, u32[]{:S(2)}) collective-permute-start(bf16[320,512]{1,0:T(8,128)(2,1)S(1)} %get-tuple-element.38), channel_id=1, source_target_pairs={{0,8},{1,9},{2,10},{3,11},{4,12},{5,13},{6,14},{7,15},{8,0},{9,1},... | collective-permute-start | bytes 983048 | tf_op jit(solution)/shard_map/ppermute | solution.py:494
  60.6 0.7 copy-start.8
  64.6 12.2 %collective-permute-start.17 = (bf16[320,512]{1,0:T(8,128)(2,1)}, bf16[320,512]{1,0:T(8,128)(2,1)S(1)}, u32[]{:S(2)}, u32[]{:S(2)}) collective-permute-start(bf16[320,512]{1,0:T(8,128)(2,1)} %get-tuple-element.39.refs_0_), channel_id=1, source_target_pairs={{0,6},{1,7},{2,0},{3,1},{4,2},{5,3},{6,4},{7,5},{8,14},{9,15},{10,... | collective-permute-start | bytes 983048 | tf_op jit(solution)/shard_map/ppermute | solution.py:416
  65.1 11.7 %collective-permute-start.16 = (bf16[320,512]{1,0:T(8,128)(2,1)}, bf16[320,512]{1,0:T(8,128)(2,1)S(1)}, u32[]{:S(2)}, u32[]{:S(2)}) collective-permute-start(bf16[320,512]{1,0:T(8,128)(2,1)} %get-tuple-element.39.refs_0_), channel_id=1, source_target_pairs={{0,2},{1,3},{2,4},{3,5},{4,6},{5,7},{6,0},{7,1},{8,10},{9,11},{10,... | collective-permute-start | bytes 983048 | tf_op jit(solution)/shard_map/ppermute | solution.py:416
  66.1 10.8 %collective-permute-start.8 = (bf16[320,512]{1,0:T(8,128)(2,1)}, bf16[320,512]{1,0:T(8,128)(2,1)S(1)}, u32[]{:S(2)}, u32[]{:S(2)}) collective-permute-start(bf16[320,512]{1,0:T(8,128)(2,1)} %get-tuple-element.39.refs_0_), channel_id=1, source_target_pairs={{0,8},{1,9},{2,10},{3,11},{4,12},{5,13},{6,14},{7,15},{8,0},{9,1},... | collective-permute-start | bytes 983048 | tf_op jit(solution)/shard_map/ppermute | solution.py:416
  71.5 5.3 %copy-start.1 = (bf16[320,512]{1,0:T(8,128)(2,1)S(1)}, bf16[320,512]{1,0:T(8,128)(2,1)}, u32[]{:S(2)}) copy-start(bf16[320,512]{1,0:T(8,128)(2,1)} %get-tuple-element.39.refs_0_) | copy-start | bytes 983044
  71.5 41.5 %all-to-all-start.1 = ((bf16[8,192,640]{2,1,0:T(8,128)(2,1)}), bf16[8,192,640]{2,1,0:T(8,128)(2,1)S(1)}, u32[]{:S(2)}, u32[]{:S(2)}) async-start(bf16[8,192,640]{2,1,0:T(8,128)(2,1)} %suffix_sums.1), calls=%async_computation.1 | async-start | bytes 3932160 | tf_op jit(solution)/shard_map/all_to_all | solution.py:488
  78.4 28.4 %collective-permute-start.18 = (bf16[1280,512]{1,0:T(8,128)(2,1)}, bf16[1280,512]{1,0:T(8,128)(2,1)}, u32[]{:S(2)}, u32[]{:S(2)}) collective-permute-start(bf16[1280,512]{1,0:T(8,128)(2,1)} %stacked.1), channel_id=1, source_target_pairs={{0,1},{1,0},{2,3},{3,2},{4,5},{5,4},{6,7},{7,6},{8,9},{9,8},{10,11... | collective-permute-start | bytes 3932168 | tf_op jit(solution)/shard_map/ppermute | solution.py:416
  80.8 10.9 %collective-permute-start.12 = (bf16[320,512]{1,0:T(8,128)(2,1)S(1)}, bf16[320,512]{1,0:T(8,128)(2,1)}, u32[]{:S(2)}, u32[]{:S(2)}) collective-permute-start(bf16[320,512]{1,0:T(8,128)(2,1)S(1)} %copy-done.1), channel_id=1, source_target_pairs={{0,4},{1,5},{2,6},{3,7},{4,0},{5,1},{6,2},{7,3},{8,12},{9,13},{10,... | collective-permute-start | bytes 983048 | tf_op jit(solution)/shard_map/ppermute | solution.py:416
  81.3 17.3 %collective-permute-start.10 = (bf16[320,512]{1,0:T(8,128)(2,1)S(1)}, bf16[320,512]{1,0:T(8,128)(2,1)S(1)}, u32[]{:S(2)}, u32[]{:S(2)}) collective-permute-start(bf16[320,512]{1,0:T(8,128)(2,1)S(1)} %collective-permute-done.8.refs_3_), channel_id=1, source_target_pairs={{0,4},{1,5},{2,6},{3,7},{4,0},{5,1},{6,2},{7,3},{8,12},{9,13},{10,... | collective-permute-start | bytes 983048 | tf_op jit(solution)/shard_map/ppermute | solution.py:416
  83.7 22.3 %collective-permute-start.9 = (bf16[320,512]{1,0:T(8,128)(2,1)S(1)}, bf16[320,512]{1,0:T(8,128)(2,1)}, u32[]{:S(2)}, u32[]{:S(2)}) collective-permute-start(bf16[320,512]{1,0:T(8,128)(2,1)S(1)} %collective-permute-done.8.refs_3_), channel_id=1, source_target_pairs={{0,2},{1,3},{2,4},{3,5},{4,6},{5,7},{6,0},{7,1},{8,10},{9,11},{10,... | collective-permute-start | bytes 983048 | tf_op jit(solution)/shard_map/ppermute | solution.py:416
  83.7 22.3 %collective-permute-start.11 = (bf16[320,512]{1,0:T(8,128)(2,1)S(1)}, bf16[320,512]{1,0:T(8,128)(2,1)}, u32[]{:S(2)}, u32[]{:S(2)}) collective-permute-start(bf16[320,512]{1,0:T(8,128)(2,1)S(1)} %collective-permute-done.8.refs_3_), channel_id=1, source_target_pairs={{0,6},{1,7},{2,0},{3,1},{4,2},{5,3},{6,4},{7,5},{8,14},{9,15},{10,... | collective-permute-start | bytes 983048 | tf_op jit(solution)/shard_map/ppermute | solution.py:416
  91.7 18.0 %collective-permute-start.15 = (bf16[320,512]{1,0:T(8,128)(2,1)}, bf16[320,512]{1,0:T(8,128)(2,1)}, u32[]{:S(2)}, u32[]{:S(2)}) collective-permute-start(bf16[320,512]{1,0:T(8,128)(2,1)} %collective-permute-done.12.refs_2_), channel_id=1, source_target_pairs={{0,1},{1,0},{2,3},{3,2},{4,5},{5,4},{6,7},{7,6},{8,9},{9,8},{10,11... | collective-permute-start | bytes 983048 | tf_op jit(solution)/shard_map/ppermute | solution.py:416
  98.6 7.5 %copy-start.3 = (bf16[320,512]{1,0:T(8,128)(2,1)}, bf16[320,512]{1,0:T(8,128)(2,1)S(1)}, u32[]{:S(2)}) copy-start(bf16[320,512]{1,0:T(8,128)(2,1)S(1)} %collective-permute-done.10.refs_0_) | copy-start | bytes 983044
  106.1 3.6 %collective-permute-start.14 = (bf16[320,512]{1,0:T(8,128)(2,1)}, bf16[320,512]{1,0:T(8,128)(2,1)}, u32[]{:S(2)}, u32[]{:S(2)}) collective-permute-start(bf16[320,512]{1,0:T(8,128)(2,1)} %collective-permute-done.11.refs_1_), channel_id=1, source_target_pairs={{0,1},{1,0},{2,3},{3,2},{4,5},{5,4},{6,7},{7,6},{8,9},{9,8},{10,11... | collective-permute-start | bytes 983048 | tf_op jit(solution)/shard_map/ppermute | solution.py:416
  106.6 3.1 %collective-permute-start.13 = (bf16[320,512]{1,0:T(8,128)(2,1)}, bf16[320,512]{1,0:T(8,128)(2,1)}, u32[]{:S(2)}, u32[]{:S(2)}) collective-permute-start(bf16[320,512]{1,0:T(8,128)(2,1)} %collective-permute-done.9.refs_0_), channel_id=1, source_target_pairs={{0,1},{1,0},{2,3},{3,2},{4,5},{5,4},{6,7},{7,6},{8,9},{9,8},{10,11... | collective-permute-start | bytes 983048 | tf_op jit(solution)/shard_map/ppermute | solution.py:416
  109.6 2.9 %copy-start.4 = (bf16[320,512]{1,0:T(8,128)(2,1)S(1)}, bf16[320,512]{1,0:T(8,128)(2,1)}, u32[]{:S(2)}) copy-start(bf16[320,512]{1,0:T(8,128)(2,1)} %copy-done.3) | copy-start | bytes 983044
  112.5 3.4 %collective-permute-start.19 = (bf16[320,512]{1,0:T(8,128)(2,1)S(1)}, bf16[320,512]{1,0:T(8,128)(2,1)S(1)}, u32[]{:S(2)}, u32[]{:S(2)}) collective-permute-start(bf16[320,512]{1,0:T(8,128)(2,1)S(1)} %copy-done.4), channel_id=1, source_target_pairs={{0,1},{1,0},{2,3},{3,2},{4,5},{5,4},{6,7},{7,6},{8,9},{9,8},{10,11... | collective-permute-start | bytes 983048 | tf_op jit(solution)/shard_map/ppermute | solution.py:416

commit v4 on v3

--- a/solution.py
+++ b/solution.py
@@ -218,16 +218,19 @@
 
 
 def lay_kernel(in_ref, out_ref):
-    out_ref[...] = in_ref[0]
+    blk = in_ref.shape[2]
+    for p in range(in_ref.shape[0]):
+        out_ref[:, p * blk : (p + 1) * blk] = in_ref[p]
 
 
 def side_by_side(got):
     parts, rows, blk = got.shape
+    some = parts // 2
     return pl.pallas_call(
         lay_kernel,
-        grid=(parts,),
-        in_specs=[pl.BlockSpec((1, rows, blk), lambda i: (i, 0, 0))],
-        out_specs=pl.BlockSpec((rows, blk), lambda i: (0, i)),
+        grid=(2,),
+        in_specs=[pl.BlockSpec((some, rows, blk), lambda i: (i, 0, 0))],
+        out_specs=pl.BlockSpec((rows, some * blk), lambda i: (0, i)),
         out_shape=jax.ShapeDtypeStruct((rows, parts * blk), got.dtype),
         compiler_params=params(16),
         cost_estimate=cost(0, 4 * parts * rows * blk),
@@ -297,7 +300,7 @@
             jax.ShapeDtypeStruct((2, half, kv), jnp.float32),
             jax.ShapeDtypeStruct((2, half, kv), jnp.bfloat16),
         ],
-        compiler_params=params(58),
+        compiler_params=params(40),
         cost_estimate=cost(2 * 4 * rows * 2 * blk * kv, 2 * 4 * rows * (2 * blk + kv)),
         name="wgrad",
     )(acts, *got, kgs, *got_kgs)
@@ -354,7 +357,7 @@
         in_specs=[flat, flat, pl.BlockSpec((tile, 1), lambda i: (i, 0)), deep, deep, deep],
         out_specs=[deep, deep, deep, flat],
         out_shape=[out, out, out, jax.ShapeDtypeStruct((half, kv), jnp.bfloat16)],
-        compiler_params=params(60),
+        compiler_params=params(16),
         cost_estimate=cost(20 * half * kv, 32 * half * kv),
         name="adam",
     )(here, got, gain, master, first, second)
@@ -388,27 +391,33 @@
     )(bases, *blocks, *prior)
 
 
-def stack_kernel(*refs):
-    moves, at = [], 0
-    for ref in refs[:-2]:
-        rows = ref.shape[0]
-        moves.append((ref, refs[-2].at[pl.ds(at, rows)]))
-        at += rows
-    run_copies(moves, refs[-1])
-
-
-def stacked(blocks):
-    rows = sum(b.shape[0] for b in blocks)
-    return pl.pallas_call(
-        stack_kernel,
-        in_specs=[pl.BlockSpec(memory_space=pl.ANY)] * len(blocks),
-        out_specs=pl.BlockSpec(memory_space=pltpu.VMEM),
-        out_shape=jax.ShapeDtypeStruct((rows, blocks[0].shape[1]), blocks[0].dtype),
-        scratch_shapes=[pltpu.SemaphoreType.DMA((len(blocks),))],
+def spread(slots, bases, blocks, rows):
+    count = len(blocks)
+    block, kv = blocks[0].shape
+
+    def kernel(base_ref, *refs):
+        ins, (stack, whole, sems) = refs[:count], refs[count:]
+        moves = []
+        for n, slot in enumerate(slots):
+            at = pl.multiple_of(base_ref[slot], 32)
+            moves.append((ins[n], stack.at[pl.ds(n * block, block)]))
+            moves.append((ins[n], whole.at[pl.ds(at, block)]))
+        run_copies(moves, sems)
+
+    return pl.pallas_call(
+        kernel,
+        in_specs=[pl.BlockSpec(memory_space=pltpu.SMEM)]
+        + [pl.BlockSpec(memory_space=pltpu.VMEM)] * count,
+        out_specs=[pl.BlockSpec(memory_space=pl.ANY)] * 2,
+        out_shape=[
+            jax.ShapeDtypeStruct((count * block, kv), jnp.bfloat16),
+            jax.ShapeDtypeStruct((rows, kv), jnp.bfloat16),
+        ],
+        scratch_shapes=[pltpu.SemaphoreType.DMA((2 * count,))],
         compiler_params=params(16),
-        cost_estimate=cost(0, 4 * rows * blocks[0].shape[1]),
-        name="stacked",
-    )(*blocks)
+        cost_estimate=cost(0, 6 * count * block * kv),
+        name="spread",
+    )(bases, *blocks)
 
 
 def gather_rows(own, y, x, core):
@@ -432,25 +441,29 @@
                 table.append((yy * 8 + lax.rem(x + dx + NX, NX) * 2 + cc) * rows)
     bases = jnp.stack(table).astype(jnp.int32)
 
-    def put(entries, swapped, whole):
+    def put(entries, whole, others=()):
         blocks = [one[0] for one in entries]
         plan = []
         for n, (block, dy, dx) in enumerate(entries):
-            slot = (dy * 4 + order.index(dx)) * 2
-            plan.append((n, 0, slot))
-            if len(swapped) == 1:
-                plan.append((len(blocks), n * rows, slot + 1))
-            else:
-                plan.append((len(blocks) + n, 0, slot + 1))
-        return place(plan, bases, blocks + swapped, 16 * rows, kv, whole)
+            plan.append((n, 0, (dy * 4 + order.index(dx)) * 2))
+        for group, swapped in others:
+            for n, (block, dy, dx) in enumerate(group):
+                slot = (dy * 4 + order.index(dx)) * 2 + 1
+                one = 0 if len(swapped) == 1 else n
+                plan.append((len(blocks) + one, (n - one) * rows, slot))
+            blocks = blocks + swapped
+        return place(plan, bases, blocks, 16 * rows, kv, whole)
 
     near = [(own, 0, 0), (a, 0, -1), (b, 0, 1), (yr, 1, 0)]
-    whole = put(near, [send(stacked([one[0] for one in near]), SWAP_CORE)], None)
+    slots = [(dy * 4 + order.index(dx)) * 2 for _, dy, dx in near]
+    stack, whole = spread(slots, bases, [one[0] for one in near], 16 * rows)
+    c1 = send(stack, SWAP_CORE)
     a2, e2 = lax.optimization_barrier((a2, e2))
     middle = [(a2, 1, -1), (b2, 1, 1), (e, 0, 2)]
-    whole = put(middle, [send(one[0], SWAP_CORE) for one in middle], whole)
+    swapped = [send(one[0], SWAP_CORE) for one in middle]
+    whole = put(middle, whole, [(near, [c1]), (middle, swapped)])
     e2, whole = lax.optimization_barrier((e2, whole))
-    return put([(e2, 1, 2)], [send(e2, SWAP_CORE)], whole)
+    return put([(e2, 1, 2)], whole, [([(e2, 1, 2)], [send(e2, SWAP_CORE)])])
 
 
 def body(

time: 118 us -> 110 us (0.932)
  Pallas kernels: 32.1 us -> 25.2 us
  local copies, waits for them, and re-layouts: 5.24 us -> 1.94 us
  waiting for transfers between devices: 41.3 us -> 43.6 us
    pallas_call x3 -> x2, Pallas kernels: 7.11 us -> 3.72 us  [place(): pl.pallas_call(kernel, in_specs=[pl.BlockSpec(memory_space=pltpu.SMEM)] +...]
    unnamed x26 -> x12, local copies, waits for them, and re-layouts: 3.59 us -> 0.96 us
    ppermute x12, waiting for transfers between devices: 18.3 us -> 19.9 us  [gather_rows(): send = lambda block, perm: lax.ppermute(block, 'dp', perm)]
    pallas_call x1, Pallas kernels: 3.2 us -> 1.68 us  [adam(): pl.pallas_call(adam_kernel, grid=(2,), in_specs=[flat, flat, pl.BlockSpec...]
    pallas_call x2, Pallas kernels: 4.43 us -> 3.11 us  [the longest x1 1.76 us: spread(): pl.pallas_call(kernel, in_specs=[pl.BlockSpec(memory_space=pltpu.SMEM)] +...]
  transfers between devices with their start and end apart: 22 -> 22, of which waited for: 8 -> 10; matrix products, arithmetic and copies ran while one was open for 1% -> 1% of each run, Pallas kernels for 24% -> 19%
where the time goes in v4:
time: 110 us; the launch traced here: 109 us
  waiting for transfers between devices  43.6 us (40%)
  starting transfers between devices  37.6 us (34%)
  Pallas kernels  25.2 us (23%)
  local copies, waits for them, and re-layouts  1.94 us (2%)
    ppermute x12, waiting for transfers between devices, gather_rows(): send = lambda block, perm: lax.ppermute(block, 'dp', perm)  19.9 us
    ppermute x12, starting transfers between devices, gather_rows(): send = lambda block, perm: lax.ppermute(block, 'dp', perm)  14.8 us
    ppermute x3, waiting for transfers between devices, body(): lax.ppermute(one, 'dp', along_x(k))  8.06 us
    pallas_call x1, Pallas kernels, front(): pl.pallas_call(lambda *refs: front_kernel(parts, *refs), in_specs=[anywhe...  8.01 us
    ppermute x1, waiting for transfers between devices, body(): lax.ppermute(there, 'dp', SWAP_Y)  6.61 us
    all_to_all x1, starting transfers between devices, body(): theirs = lax.all_to_all(term, 'section', 0, 0)  6.19 us
    all_to_all x1, starting transfers between devices, body(): mine = lax.all_to_all(sums, 'section', 0, 0)  5.16 us
    ppermute x3, starting transfers between devices, body(): lax.ppermute(one, 'dp', along_x(k))  4.5 us
  transfers between devices with their start and end apart: 22, of which 10 were waited for; matrix products, arithmetic and copies ran while one was open for 1% of the time, Pallas kernels for 19%

profile of v4, /device:TPU:1, one launch (start us, length us, event | category | flops | bytes accessed | tf_op | source)
XLA Modules:
  0.0 109.2 jit_solution(10864981258968177114)
XLA Ops:
  0.6 2.6 %cut_columns.1 = (bf16[192,1280]{1,0:T(8,128)(2,1)}, bf16[192,1280]{1,0:T(8,128)(2,1)}, bf16[192,1280]{1,0:T(8,128)(2,1)}) custom-call(bf16[192,5120]{1,0:T(8,128)(2,1)} %bitcast.24), custom_call_target="tpu_custom_call" | custom-call | bytes 1 | tf_op jit(solution)/shard_map/cut_columns/pallas_call | solution.py:62
  3.3 3.4 %collective-permute-start.1 = (bf16[192,1280]{1,0:T(8,128)(2,1)}, bf16[192,1280]{1,0:T(8,128)(2,1)S(1)}, u32[]{:S(2)}, u32[]{:S(2)}) collective-permute-start(bf16[192,1280]{1,0:T(8,128)(2,1)} %get-tuple-element.31), channel_id=1, source_target_pairs={{0,6},{1,7},{2,0},{3,1},{4,2},{5,3},{6,4},{7,5},{8,14},{9,15},{10,... | collective-permute-start | bytes 1474568 | tf_op jit(solution)/shard_map/ppermute | solution.py:491
  6.7 0.5 collective-permute-start.2
  7.2 0.6 collective-permute-start
  7.8 8.0 %front.1 = (bf16[192,512]{1,0:T(8,128)(2,1)}, bf16[8,192,640]{2,1,0:T(8,128)(2,1)}) custom-call(bf16[192,5120]{1,0:T(8,128)(2,1)} %bitcast.25, bf16[5120,512]{1,0:T(8,128)(2,1)} %bitcast.28, f32[1,5120]{1,0:T(1,128)} %refs_2_.1, f32[1,128]{1,0:T(1,128)} %refs_3_.1, bf16[192,512]{1,0:T(8,128)(2,1)} %bitcast.31, bf16[192,1280]{1,0:T(8,128)(2,1)} %get-tuple-element.28.refs_5_), custom_call_target="tpu_custom_call" | custom-call | bytes 1 | tf_op jit(solution)/shard_map/front/pallas_call | solution.py:138
  15.8 0.0 copy-start
  15.8 6.2 %all-to-all-start = ((bf16[8,192,640]{2,1,0:T(8,128)(2,1)}), bf16[8,192,640]{2,1,0:T(8,128)(2,1)}, u32[]{:S(2)}, u32[]{:S(2)}) async-start(bf16[8,192,640]{2,1,0:T(8,128)(2,1)} %get-tuple-element.29), calls=%async_computation | async-start | bytes 3932160 | tf_op jit(solution)/shard_map/all_to_all | solution.py:496
  22.0 2.1 %collective-permute-start.4 = (bf16[192,512]{1,0:T(8,128)(2,1)}, bf16[192,512]{1,0:T(8,128)(2,1)S(1)}, u32[]{:S(2)}, u32[]{:S(2)}) collective-permute-start(bf16[192,512]{1,0:T(8,128)(2,1)} %get-tuple-element.36.k0), channel_id=1, source_target_pairs={{0,6},{1,7},{2,0},{3,1},{4,2},{5,3},{6,4},{7,5},{8,14},{9,15},{10,... | collective-permute-start | bytes 589832 | tf_op jit(solution)/shard_map/ppermute | solution.py:493
  24.1 8.1 %collective-permute-done.up = bf16[192,1280]{1,0:T(8,128)(2,1)S(1)} collective-permute-done((bf16[192,1280]{1,0:T(8,128)(2,1)}, bf16[192,1280]{1,0:T(8,128)(2,1)S(1)}, u32[]{:S(2)}, u32[]{:S(2)}) %collective-permute-start) | collective-permute-done | bytes 491552 | tf_op jit(solution)/shard_map/ppermute | solution.py:491
  32.1 0.5 collective-permute-start.5
  32.7 3.7 %collective-permute-done.3.k1 = bf16[192,512]{1,0:T(8,128)(2,1)S(1)} collective-permute-done((bf16[192,512]{1,0:T(8,128)(2,1)}, bf16[192,512]{1,0:T(8,128)(2,1)S(1)}, u32[]{:S(2)}, u32[]{:S(2)}) %collective-permute-start.3) | collective-permute-done | bytes 196640 | tf_op jit(solution)/shard_map/ppermute | solution.py:493
  36.4 3.6 %collective-permute-done.5.k2 = bf16[192,512]{1,0:T(8,128)(2,1)S(1)} collective-permute-done((bf16[192,512]{1,0:T(8,128)(2,1)}, bf16[192,512]{1,0:T(8,128)(2,1)S(1)}, u32[]{:S(2)}, u32[]{:S(2)}) %collective-permute-start.5) | collective-permute-done | bytes 196640 | tf_op jit(solution)/shard_map/ppermute | solution.py:495
  40.0 0.9 copy-done.5
  40.9 3.5 %wgrad.1 = (f32[2,320,512]{2,1,0:T(8,128)S(1)}, bf16[2,320,512]{2,1,0:T(8,128)(2,1)S(1)}) custom-call(bf16[192,5120]{1,0:T(8,128)(2,1)S(1)} %bitcast.26, bf16[192,1280]{1,0:T(8,128)(2,1)S(1)} %collective-permute-done.up, bf16[192,1280]{1,0:T(8,128)(2,1)S(1)} %collective-permute-done.1.down, bf16[192,1280]{1,0:T(8,128)(2,1)S(1)} %collective-permute-done.2.far, ...), custom_call_target="tpu_custom_call" | custom-call | bytes 1 | tf_op jit(solution)/shard_map/wgrad/pallas_call | solution.py:287
  44.4 0.0 copy-start.2
  44.4 0.0 copy-start.3
  44.4 1.4 %collective-permute-start.6 = (bf16[2,320,512]{2,1,0:T(8,128)(2,1)S(1)}, bf16[2,320,512]{2,1,0:T(8,128)(2,1)S(1)}, u32[]{:S(2)}, u32[]{:S(2)}) collective-permute-start(bf16[2,320,512]{2,1,0:T(8,128)(2,1)S(1)} %get-tuple-element.38), channel_id=1, source_target_pairs={{0,1},{1,0},{2,3},{3,2},{4,5},{5,4},{6,7},{7,6},{8,9},{9,8},{10,11... | collective-permute-start | bytes 1966088 | tf_op jit(solution)/shard_map/ppermute | solution.py:499
  45.8 1.7 %collective-permute-done.6.got = bf16[2,320,512]{2,1,0:T(8,128)(2,1)S(1)} collective-permute-done((bf16[2,320,512]{2,1,0:T(8,128)(2,1)S(1)}, bf16[2,320,512]{2,1,0:T(8,128)(2,1)S(1)}, u32[]{:S(2)}, u32[]{:S(2)}) %collective-permute-start.6) | collective-permute-done | bytes 655392 | tf_op jit(solution)/shard_map/ppermute | solution.py:499
  47.5 0.1 merge.1
  47.6 0.0 copy-start.1
  47.6 3.0 %collective-permute-start.7 = (bf16[320,512]{1,0:T(8,128)(2,1)S(1)}, bf16[320,512]{1,0:T(8,128)(2,1)S(1)}, u32[]{:S(2)}, u32[]{:S(2)}) collective-permute-start(bf16[320,512]{1,0:T(8,128)(2,1)S(1)} %get-tuple-element.40), channel_id=1, source_target_pairs={{0,8},{1,9},{2,10},{3,11},{4,12},{5,13},{6,14},{7,15},{8,0},{9,1},... | collective-permute-start | bytes 983048 | tf_op jit(solution)/shard_map/ppermute | solution.py:507
  50.6 0.8 dynamic-slice_bitcast_fusion
  51.4 0.1 copy.16.gain
  51.5 6.6 %collective-permute-done.7.got = bf16[320,512]{1,0:T(8,128)(2,1)S(1)} collective-permute-done((bf16[320,512]{1,0:T(8,128)(2,1)S(1)}, bf16[320,512]{1,0:T(8,128)(2,1)S(1)}, u32[]{:S(2)}, u32[]{:S(2)}) %collective-permute-start.7) | collective-permute-done | bytes 327712 | tf_op jit(solution)/shard_map/ppermute | solution.py:507
  58.2 1.7 %adam.1 = (f32[1,320,512]{2,1,0:T(8,128)}, f32[1,320,512]{2,1,0:T(8,128)}, f32[1,320,512]{2,1,0:T(8,128)}, bf16[320,512]{1,0:T(8,128)(2,1)S(1)}) custom-call(f32[320,512]{1,0:T(8,128)S(1)} %get-tuple-element.39.refs_2_.here, bf16[320,512]{1,0:T(8,128)(2,1)S(1)} %collective-permute-done.7.got, f32[320,1]{1,0:T(8,128)S(1)} %copy.16.gain, ...), custom_call_target="tpu_custom_call" | custom-call | bytes 1 | tf_op jit(solution)/shard_map/adam/pallas_call | solution.py:354
  59.9 0.5 collective-permute-start.14
  60.4 0.9 collective-permute-start.13
  61.3 2.9 %collective-permute-start.8 = (bf16[320,512]{1,0:T(8,128)(2,1)S(1)}, bf16[320,512]{1,0:T(8,128)(2,1)S(1)}, u32[]{:S(2)}, u32[]{:S(2)}) collective-permute-start(bf16[320,512]{1,0:T(8,128)(2,1)S(1)} %get-tuple-element.41.refs_0_), channel_id=1, source_target_pairs={{0,8},{1,9},{2,10},{3,11},{4,12},{5,13},{6,14},{7,15},{8,0},{9,1},... | collective-permute-start | bytes 983048 | tf_op jit(solution)/shard_map/ppermute | solution.py:425
  64.2 2.5 %suffix_sums.1 = bf16[8,192,640]{2,1,0:T(8,128)(2,1)} custom-call(bf16[8,192,640]{2,1,0:T(8,128)(2,1)} %all-to-all-done.refs_0_, bf16[192,5120]{1,0:T(8,128)(2,1)} %bitcast.29, f32[320,512]{1,0:T(8,128)} %copy-done.1), custom_call_target="tpu_custom_call" | custom-call | bytes 1 | tf_op jit(solution)/shard_map/suffix_sums/pallas_call | solution.py:202
  66.8 5.2 %all-to-all-start.1 = ((bf16[8,192,640]{2,1,0:T(8,128)(2,1)}), bf16[8,192,640]{2,1,0:T(8,128)(2,1)S(1)}, u32[]{:S(2)}, u32[]{:S(2)}) async-start(bf16[8,192,640]{2,1,0:T(8,128)(2,1)} %suffix_sums.1), calls=%async_computation.1 | async-start | bytes 3932160 | tf_op jit(solution)/shard_map/all_to_all | solution.py:501
  71.9 0.1 stack.67.base_ref
  72.0 1.8 %spread.1 = (bf16[1280,512]{1,0:T(8,128)(2,1)S(1)}, bf16[5120,512]{1,0:T(8,128)(2,1)}) custom-call(s32[16]{0:T(128)S(1)} %stack.67.base_ref, bf16[320,512]{1,0:T(8,128)(2,1)S(1)} %get-tuple-element.41.refs_0_, bf16[320,512]{1,0:T(8,128)(2,1)S(1)} %collective-permute-done.13.refs_1_, bf16[320,512]{1,0:T(8,128)(2,1)S(1)} %collective-permute-done.14.refs_2_, ...), custom_call_target="tpu_custom_call" | custom-call | bytes 1 | tf_op jit(solution)/shard_map/spread/pallas_call | solution.py:407
  73.8 2.4 %collective-permute-start.15 = (bf16[1280,512]{1,0:T(8,128)(2,1)S(1)}, bf16[1280,512]{1,0:T(8,128)(2,1)S(1)}, u32[]{:S(2)}, u32[]{:S(2)}) collective-permute-start(bf16[1280,512]{1,0:T(8,128)(2,1)S(1)} %get-tuple-element.44), channel_id=1, source_target_pairs={{0,1},{1,0},{2,3},{3,2},{4,5},{5,4},{6,7},{7,6},{8,9},{9,8},{10,11... | collective-permute-start | bytes 3932168 | tf_op jit(solution)/shard_map/ppermute | solution.py:425
  76.2 0.5 collective-permute-start.12
  76.7 2.5 %collective-permute-start.10 = (bf16[320,512]{1,0:T(8,128)(2,1)S(1)}, bf16[320,512]{1,0:T(8,128)(2,1)S(1)}, u32[]{:S(2)}, u32[]{:S(2)}) collective-permute-start(bf16[320,512]{1,0:T(8,128)(2,1)S(1)} %collective-permute-done.8.refs_3_), channel_id=1, source_target_pairs={{0,4},{1,5},{2,6},{3,7},{4,0},{5,1},{6,2},{7,3},{8,12},{9,13},{10,... | collective-permute-start | bytes 983048 | tf_op jit(solution)/shard_map/ppermute | solution.py:425
  79.2 2.7 %collective-permute-start.11 = (bf16[320,512]{1,0:T(8,128)(2,1)S(1)}, bf16[320,512]{1,0:T(8,128)(2,1)S(1)}, u32[]{:S(2)}, u32[]{:S(2)}) collective-permute-start(bf16[320,512]{1,0:T(8,128)(2,1)S(1)} %collective-permute-done.8.refs_3_), channel_id=1, source_target_pairs={{0,6},{1,7},{2,0},{3,1},{4,2},{5,3},{6,4},{7,5},{8,14},{9,15},{10,... | collective-permute-start | bytes 983048 | tf_op jit(solution)/shard_map/ppermute | solution.py:425
  81.9 5.2 %collective-permute-done.12.refs_2_ = bf16[320,512]{1,0:T(8,128)(2,1)S(1)} collective-permute-done((bf16[320,512]{1,0:T(8,128)(2,1)S(1)}, bf16[320,512]{1,0:T(8,128)(2,1)S(1)}, u32[]{:S(2)}, u32[]{:S(2)}) %collective-permute-start.12) | collective-permute-done | bytes 327712 | tf_op jit(solution)/shard_map/ppermute | solution.py:425
  87.0 1.4 %collective-permute-start.18 = (bf16[320,512]{1,0:T(8,128)(2,1)S(1)}, bf16[320,512]{1,0:T(8,128)(2,1)S(1)}, u32[]{:S(2)}, u32[]{:S(2)}) collective-permute-start(bf16[320,512]{1,0:T(8,128)(2,1)S(1)} %collective-permute-done.12.refs_2_), channel_id=1, source_target_pairs={{0,1},{1,0},{2,3},{3,2},{4,5},{5,4},{6,7},{7,6},{8,9},{9,8},{10,11... | collective-permute-start | bytes 983048 | tf_op jit(solution)/shard_map/ppermute | solution.py:425
  88.4 5.6 %collective-permute-done.10.refs_0_ = bf16[320,512]{1,0:T(8,128)(2,1)S(1)} collective-permute-done((bf16[320,512]{1,0:T(8,128)(2,1)S(1)}, bf16[320,512]{1,0:T(8,128)(2,1)S(1)}, u32[]{:S(2)}, u32[]{:S(2)}) %collective-permute-start.10) | collective-permute-done | bytes 327712 | tf_op jit(solution)/shard_map/ppermute | solution.py:425
  94.1 7.4 %collective-permute-done.9.refs_0_ = bf16[320,512]{1,0:T(8,128)(2,1)S(1)} collective-permute-done((bf16[320,512]{1,0:T(8,128)(2,1)S(1)}, bf16[320,512]{1,0:T(8,128)(2,1)S(1)}, u32[]{:S(2)}, u32[]{:S(2)}) %collective-permute-start.9) | collective-permute-done | bytes 327712 | tf_op jit(solution)/shard_map/ppermute | solution.py:425
  101.4 0.5 collective-permute-start.17
  101.9 0.0 collective-permute-start.16
  101.9 1.2 %collective-permute-done.17.refs_5_ = bf16[320,512]{1,0:T(8,128)(2,1)S(1)} collective-permute-done((bf16[320,512]{1,0:T(8,128)(2,1)S(1)}, bf16[320,512]{1,0:T(8,128)(2,1)S(1)}, u32[]{:S(2)}, u32[]{:S(2)}) %collective-permute-start.17) | collective-permute-done | bytes 327712 | tf_op jit(solution)/shard_map/ppermute | solution.py:425
  103.2 0.5 collective-permute-done.16.refs_4_
  103.6 2.3 %place.2.refs_2_ = bf16[5120,512]{1,0:T(8,128)(2,1)} custom-call(s32[16]{0:T(128)S(1)} %stack.67.base_ref, bf16[320,512]{1,0:T(8,128)(2,1)S(1)} %collective-permute-done.9.refs_0_, bf16[320,512]{1,0:T(8,128)(2,1)S(1)} %collective-permute-done.11.refs_1_, bf16[320,512]{1,0:T(8,128)(2,1)S(1)} %collective-permute-done.12.refs_2_, ...), custom_call_target="tpu_custom_call", output_to_operand_aliasing={{}: (8, {})} | custom-call | bytes 1 | tf_op jit(solution)/shard_map/place/pallas_call | solution.py:379
  106.0 0.5 collective-permute-start.19
  106.4 1.3 %side_by_side.1 = bf16[192,5120]{1,0:T(8,128)(2,1)} custom-call(bf16[8,192,640]{2,1,0:T(8,128)(2,1)S(1)} %all-to-all-done.1.in_ref), custom_call_target="tpu_custom_call" | custom-call | bytes 1 | tf_op jit(solution)/shard_map/side_by_side/pallas_call | solution.py:229
  107.8 1.4 %place.3 = bf16[5120,512]{1,0:T(8,128)(2,1)} custom-call(s32[16]{0:T(128)S(1)} %stack.67.base_ref, bf16[320,512]{1,0:T(8,128)(2,1)S(1)} %collective-permute-done.10.refs_0_, bf16[320,512]{1,0:T(8,128)(2,1)S(1)} %collective-permute-done.19.refs_1_, bf16[5120,512]{1,0:T(8,128)(2,1)} %place.2.refs_2_), custom_call_target="tpu_custom_call", output_to_operand_aliasing={{}: (3, {})} | custom-call | bytes 1 | tf_op jit(solution)/shard_map/place/pallas_call | solution.py:379
  (21 shorter events, 0.1 us)
Async XLA Ops:
  3.3 20.8 %collective-permute-start.1 = (bf16[192,1280]{1,0:T(8,128)(2,1)}, bf16[192,1280]{1,0:T(8,128)(2,1)S(1)}, u32[]{:S(2)}, u32[]{:S(2)}) collective-permute-start(bf16[192,1280]{1,0:T(8,128)(2,1)} %get-tuple-element.31), channel_id=1, source_target_pairs={{0,6},{1,7},{2,0},{3,1},{4,2},{5,3},{6,4},{7,5},{8,14},{9,15},{10,... | collective-permute-start | bytes 1474568 | tf_op jit(solution)/shard_map/ppermute | solution.py:491
  6.7 17.4 %collective-permute-start.2 = (bf16[192,1280]{1,0:T(8,128)(2,1)}, bf16[192,1280]{1,0:T(8,128)(2,1)S(1)}, u32[]{:S(2)}, u32[]{:S(2)}) collective-permute-start(bf16[192,1280]{1,0:T(8,128)(2,1)} %get-tuple-element.32), channel_id=1, source_target_pairs={{0,4},{1,5},{2,6},{3,7},{4,0},{5,1},{6,2},{7,3},{8,12},{9,13},{10,... | collective-permute-start | bytes 1474568 | tf_op jit(solution)/shard_map/ppermute | solution.py:491
  7.2 25.0 %collective-permute-start = (bf16[192,1280]{1,0:T(8,128)(2,1)}, bf16[192,1280]{1,0:T(8,128)(2,1)S(1)}, u32[]{:S(2)}, u32[]{:S(2)}) collective-permute-start(bf16[192,1280]{1,0:T(8,128)(2,1)} %get-tuple-element.28.refs_5_), channel_id=1, source_target_pairs={{0,2},{1,3},{2,4},{3,5},{4,6},{5,7},{6,0},{7,1},{8,10},{9,11},{10,... | collective-permute-start | bytes 1474568 | tf_op jit(solution)/shard_map/ppermute | solution.py:491
  15.8 24.2 %copy-start = (bf16[1,2,96,5120]{3,2,1,0:T(8,128)(2,1)S(1)}, bf16[1,2,96,5120]{3,2,1,0:T(8,128)(2,1)}, u32[]{:S(2)}) copy-start(bf16[1,2,96,5120]{3,2,1,0:T(8,128)(2,1)} %param.9) | copy-start | bytes 5898244
  15.8 48.4 %all-to-all-start = ((bf16[8,192,640]{2,1,0:T(8,128)(2,1)}), bf16[8,192,640]{2,1,0:T(8,128)(2,1)}, u32[]{:S(2)}, u32[]{:S(2)}) async-start(bf16[8,192,640]{2,1,0:T(8,128)(2,1)} %get-tuple-element.29), calls=%async_computation | async-start | bytes 3932160 | tf_op jit(solution)/shard_map/all_to_all | solution.py:496
  22.0 10.7 %collective-permute-start.4 = (bf16[192,512]{1,0:T(8,128)(2,1)}, bf16[192,512]{1,0:T(8,128)(2,1)S(1)}, u32[]{:S(2)}, u32[]{:S(2)}) collective-permute-start(bf16[192,512]{1,0:T(8,128)(2,1)} %get-tuple-element.36.k0), channel_id=1, source_target_pairs={{0,6},{1,7},{2,0},{3,1},{4,2},{5,3},{6,4},{7,5},{8,14},{9,15},{10,... | collective-permute-start | bytes 589832 | tf_op jit(solution)/shard_map/ppermute | solution.py:493
  24.1 12.3 %collective-permute-start.3 = (bf16[192,512]{1,0:T(8,128)(2,1)}, bf16[192,512]{1,0:T(8,128)(2,1)S(1)}, u32[]{:S(2)}, u32[]{:S(2)}) collective-permute-start(bf16[192,512]{1,0:T(8,128)(2,1)} %get-tuple-element.36.k0), channel_id=1, source_target_pairs={{0,2},{1,3},{2,4},{3,5},{4,6},{5,7},{6,0},{7,1},{8,10},{9,11},{10,... | collective-permute-start | bytes 589832 | tf_op jit(solution)/shard_map/ppermute | solution.py:493
  32.1 7.8 %collective-permute-start.5 = (bf16[192,512]{1,0:T(8,128)(2,1)}, bf16[192,512]{1,0:T(8,128)(2,1)S(1)}, u32[]{:S(2)}, u32[]{:S(2)}) collective-permute-start(bf16[192,512]{1,0:T(8,128)(2,1)} %get-tuple-element.36.k0), channel_id=1, source_target_pairs={{0,4},{1,5},{2,6},{3,7},{4,0},{5,1},{6,2},{7,3},{8,12},{9,13},{10,... | collective-permute-start | bytes 589832 | tf_op jit(solution)/shard_map/ppermute | solution.py:495
  40.0 0.9 copy-start.5
  44.4 13.8 %copy-start.2 = (f32[1,320,512]{2,1,0:T(8,128)S(1)}, f32[1,320,512]{2,1,0:T(8,128)}, u32[]{:S(2)}) copy-start(f32[1,320,512]{2,1,0:T(8,128)} %master.1) | copy-start | bytes 1966084
  44.4 13.8 %copy-start.3 = (f32[1,320,512]{2,1,0:T(8,128)S(1)}, f32[1,320,512]{2,1,0:T(8,128)}, u32[]{:S(2)}) copy-start(f32[1,320,512]{2,1,0:T(8,128)} %first.1) | copy-start | bytes 1966084
  44.4 13.8 %copy-start.4 = (f32[1,320,512]{2,1,0:T(8,128)S(1)}, f32[1,320,512]{2,1,0:T(8,128)}, u32[]{:S(2)}) copy-start(f32[1,320,512]{2,1,0:T(8,128)} %second.1) | copy-start | bytes 1966084
  44.4 3.1 %collective-permute-start.6 = (bf16[2,320,512]{2,1,0:T(8,128)(2,1)S(1)}, bf16[2,320,512]{2,1,0:T(8,128)(2,1)S(1)}, u32[]{:S(2)}, u32[]{:S(2)}) collective-permute-start(bf16[2,320,512]{2,1,0:T(8,128)(2,1)S(1)} %get-tuple-element.38), channel_id=1, source_target_pairs={{0,1},{1,0},{2,3},{3,2},{4,5},{5,4},{6,7},{7,6},{8,9},{9,8},{10,11... | collective-permute-start | bytes 1966088 | tf_op jit(solution)/shard_map/ppermute | solution.py:499
  47.6 16.6 %copy-start.1 = (f32[320,512]{1,0:T(8,128)}, f32[320,512]{1,0:T(8,128)S(1)}, u32[]{:S(2)}) copy-start(f32[320,512]{1,0:T(8,128)S(1)} %get-tuple-element.39.refs_2_.here) | copy-start | bytes 1966084
  47.6 10.5 %collective-permute-start.7 = (bf16[320,512]{1,0:T(8,128)(2,1)S(1)}, bf16[320,512]{1,0:T(8,128)(2,1)S(1)}, u32[]{:S(2)}, u32[]{:S(2)}) collective-permute-start(bf16[320,512]{1,0:T(8,128)(2,1)S(1)} %get-tuple-element.40), channel_id=1, source_target_pairs={{0,8},{1,9},{2,10},{3,11},{4,12},{5,13},{6,14},{7,15},{8,0},{9,1},... | collective-permute-start | bytes 983048 | tf_op jit(solution)/shard_map/ppermute | solution.py:507
  59.9 12.2 %collective-permute-start.14 = (bf16[320,512]{1,0:T(8,128)(2,1)S(1)}, bf16[320,512]{1,0:T(8,128)(2,1)S(1)}, u32[]{:S(2)}, u32[]{:S(2)}) collective-permute-start(bf16[320,512]{1,0:T(8,128)(2,1)S(1)} %get-tuple-element.41.refs_0_), channel_id=1, source_target_pairs={{0,6},{1,7},{2,0},{3,1},{4,2},{5,3},{6,4},{7,5},{8,14},{9,15},{10,... | collective-permute-start | bytes 983048 | tf_op jit(solution)/shard_map/ppermute | solution.py:425
  60.4 11.6 %collective-permute-start.13 = (bf16[320,512]{1,0:T(8,128)(2,1)S(1)}, bf16[320,512]{1,0:T(8,128)(2,1)S(1)}, u32[]{:S(2)}, u32[]{:S(2)}) collective-permute-start(bf16[320,512]{1,0:T(8,128)(2,1)S(1)} %get-tuple-element.41.refs_0_), channel_id=1, source_target_pairs={{0,2},{1,3},{2,4},{3,5},{4,6},{5,7},{6,0},{7,1},{8,10},{9,11},{10,... | collective-permute-start | bytes 983048 | tf_op jit(solution)/shard_map/ppermute | solution.py:425
  61.3 10.7 %collective-permute-start.8 = (bf16[320,512]{1,0:T(8,128)(2,1)S(1)}, bf16[320,512]{1,0:T(8,128)(2,1)S(1)}, u32[]{:S(2)}, u32[]{:S(2)}) collective-permute-start(bf16[320,512]{1,0:T(8,128)(2,1)S(1)} %get-tuple-element.41.refs_0_), channel_id=1, source_target_pairs={{0,8},{1,9},{2,10},{3,11},{4,12},{5,13},{6,14},{7,15},{8,0},{9,1},... | collective-permute-start | bytes 983048 | tf_op jit(solution)/shard_map/ppermute | solution.py:425
  66.8 39.7 %all-to-all-start.1 = ((bf16[8,192,640]{2,1,0:T(8,128)(2,1)}), bf16[8,192,640]{2,1,0:T(8,128)(2,1)S(1)}, u32[]{:S(2)}, u32[]{:S(2)}) async-start(bf16[8,192,640]{2,1,0:T(8,128)(2,1)} %suffix_sums.1), calls=%async_computation.1 | async-start | bytes 3932160 | tf_op jit(solution)/shard_map/all_to_all | solution.py:501
  73.8 29.8 %collective-permute-start.15 = (bf16[1280,512]{1,0:T(8,128)(2,1)S(1)}, bf16[1280,512]{1,0:T(8,128)(2,1)S(1)}, u32[]{:S(2)}, u32[]{:S(2)}) collective-permute-start(bf16[1280,512]{1,0:T(8,128)(2,1)S(1)} %get-tuple-element.44), channel_id=1, source_target_pairs={{0,1},{1,0},{2,3},{3,2},{4,5},{5,4},{6,7},{7,6},{8,9},{9,8},{10,11... | collective-permute-start | bytes 3932168 | tf_op jit(solution)/shard_map/ppermute | solution.py:425
  76.2 10.8 %collective-permute-start.12 = (bf16[320,512]{1,0:T(8,128)(2,1)S(1)}, bf16[320,512]{1,0:T(8,128)(2,1)S(1)}, u32[]{:S(2)}, u32[]{:S(2)}) collective-permute-start(bf16[320,512]{1,0:T(8,128)(2,1)S(1)} %get-tuple-element.41.refs_0_), channel_id=1, source_target_pairs={{0,4},{1,5},{2,6},{3,7},{4,0},{5,1},{6,2},{7,3},{8,12},{9,13},{10,... | collective-permute-start | bytes 983048 | tf_op jit(solution)/shard_map/ppermute | solution.py:425
  76.7 17.3 %collective-permute-start.10 = (bf16[320,512]{1,0:T(8,128)(2,1)S(1)}, bf16[320,512]{1,0:T(8,128)(2,1)S(1)}, u32[]{:S(2)}, u32[]{:S(2)}) collective-permute-start(bf16[320,512]{1,0:T(8,128)(2,1)S(1)} %collective-permute-done.8.refs_3_), channel_id=1, source_target_pairs={{0,4},{1,5},{2,6},{3,7},{4,0},{5,1},{6,2},{7,3},{8,12},{9,13},{10,... | collective-permute-start | bytes 983048 | tf_op jit(solution)/shard_map/ppermute | solution.py:425
  79.2 22.2 %collective-permute-start.9 = (bf16[320,512]{1,0:T(8,128)(2,1)S(1)}, bf16[320,512]{1,0:T(8,128)(2,1)S(1)}, u32[]{:S(2)}, u32[]{:S(2)}) collective-permute-start(bf16[320,512]{1,0:T(8,128)(2,1)S(1)} %collective-permute-done.8.refs_3_), channel_id=1, source_target_pairs={{0,2},{1,3},{2,4},{3,5},{4,6},{5,7},{6,0},{7,1},{8,10},{9,11},{10,... | collective-permute-start | bytes 983048 | tf_op jit(solution)/shard_map/ppermute | solution.py:425
  79.2 22.2 %collective-permute-start.11 = (bf16[320,512]{1,0:T(8,128)(2,1)S(1)}, bf16[320,512]{1,0:T(8,128)(2,1)S(1)}, u32[]{:S(2)}, u32[]{:S(2)}) collective-permute-start(bf16[320,512]{1,0:T(8,128)(2,1)S(1)} %collective-permute-done.8.refs_3_), channel_id=1, source_target_pairs={{0,6},{1,7},{2,0},{3,1},{4,2},{5,3},{6,4},{7,5},{8,14},{9,15},{10,... | collective-permute-start | bytes 983048 | tf_op jit(solution)/shard_map/ppermute | solution.py:425
  87.0 14.9 %collective-permute-start.18 = (bf16[320,512]{1,0:T(8,128)(2,1)S(1)}, bf16[320,512]{1,0:T(8,128)(2,1)S(1)}, u32[]{:S(2)}, u32[]{:S(2)}) collective-permute-start(bf16[320,512]{1,0:T(8,128)(2,1)S(1)} %collective-permute-done.12.refs_2_), channel_id=1, source_target_pairs={{0,1},{1,0},{2,3},{3,2},{4,5},{5,4},{6,7},{7,6},{8,9},{9,8},{10,11... | collective-permute-start | bytes 983048 | tf_op jit(solution)/shard_map/ppermute | solution.py:425
  101.4 1.8 %collective-permute-start.17 = (bf16[320,512]{1,0:T(8,128)(2,1)S(1)}, bf16[320,512]{1,0:T(8,128)(2,1)S(1)}, u32[]{:S(2)}, u32[]{:S(2)}) collective-permute-start(bf16[320,512]{1,0:T(8,128)(2,1)S(1)} %collective-permute-done.11.refs_1_), channel_id=1, source_target_pairs={{0,1},{1,0},{2,3},{3,2},{4,5},{5,4},{6,7},{7,6},{8,9},{9,8},{10,11... | collective-permute-start | bytes 983048 | tf_op jit(solution)/shard_map/ppermute | solution.py:425
  101.9 1.7 %collective-permute-start.16 = (bf16[320,512]{1,0:T(8,128)(2,1)S(1)}, bf16[320,512]{1,0:T(8,128)(2,1)S(1)}, u32[]{:S(2)}, u32[]{:S(2)}) collective-permute-start(bf16[320,512]{1,0:T(8,128)(2,1)S(1)} %collective-permute-done.9.refs_0_), channel_id=1, source_target_pairs={{0,1},{1,0},{2,3},{3,2},{4,5},{5,4},{6,7},{7,6},{8,9},{9,8},{10,11... | collective-permute-start | bytes 983048 | tf_op jit(solution)/shard_map/ppermute | solution.py:425
  106.0 1.8 %collective-permute-start.19 = (bf16[320,512]{1,0:T(8,128)(2,1)S(1)}, bf16[320,512]{1,0:T(8,128)(2,1)S(1)}, u32[]{:S(2)}, u32[]{:S(2)}) collective-permute-start(bf16[320,512]{1,0:T(8,128)(2,1)S(1)} %collective-permute-done.10.refs_0_), channel_id=1, source_target_pairs={{0,1},{1,0},{2,3},{3,2},{4,5},{5,4},{6,7},{7,6},{8,9},{9,8},{10,11... | collective-permute-start | bytes 983048 | tf_op jit(solution)/shard_map/ppermute | solution.py:425

commit v5 on v4

--- a/solution.py
+++ b/solution.py
@@ -427,10 +427,12 @@
     yr = send(own, SWAP_Y)
     a = send(own, up)
     b = send(own, down)
-    a2 = send(yr, up)
-    b2 = send(yr, down)
     e = send(own, along_x(2))
-    e2 = send(yr, along_x(2))
+    later, a, b = lax.optimization_barrier((yr, a, b))
+    a2 = send(later, up)
+    b2 = send(later, down)
+    latest, e = lax.optimization_barrier((yr, e))
+    e2 = send(latest, along_x(2))
     order = (0, -1, 1, 2)
     table = []
     for dy in range(2):
@@ -454,16 +456,19 @@
             blocks = blocks + swapped
         return place(plan, bases, blocks, 16 * rows, kv, whole)
 
-    near = [(own, 0, 0), (a, 0, -1), (b, 0, 1), (yr, 1, 0)]
+    near = [(own, 0, 0), (a, 0, -1), (b, 0, 1)]
     slots = [(dy * 4 + order.index(dx)) * 2 for _, dy, dx in near]
     stack, whole = spread(slots, bases, [one[0] for one in near], 16 * rows)
+    early = [send(yr, SWAP_CORE), send(e, SWAP_CORE)]
+    a2, stack, early[0] = lax.optimization_barrier((a2, stack, early[0]))
+    e2, early[1] = lax.optimization_barrier((e2, early[1]))
+    middle = [(a2, 1, -1), (b2, 1, 1), (e2, 1, 2)]
+    swapped = [send(one[0], SWAP_CORE) for one in middle]
+    stack, swapped[0], swapped[1], swapped[2] = lax.optimization_barrier((stack, swapped[0], swapped[1], swapped[2]))
     c1 = send(stack, SWAP_CORE)
-    a2, e2 = lax.optimization_barrier((a2, e2))
-    middle = [(a2, 1, -1), (b2, 1, 1), (e, 0, 2)]
-    swapped = [send(one[0], SWAP_CORE) for one in middle]
-    whole = put(middle, whole, [(near, [c1]), (middle, swapped)])
-    e2, whole = lax.optimization_barrier((e2, whole))
-    return put([(e2, 1, 2)], whole, [([(e2, 1, 2)], [send(e2, SWAP_CORE)])])
+    middle += [(yr, 1, 0), (e, 0, 2)]
+    whole = put(middle, whole, [(middle, swapped + early)])
+    return put([], whole, [(near, [c1])])
 
 
 def body(

time: 110 us -> 105 us (0.955)
  waiting for transfers between devices: 43.6 us -> 29.1 us
  local copies, waits for them, and re-layouts: 1.94 us -> 6.3 us
  starting transfers between devices: 37.6 us -> 40.9 us
  Pallas kernels: 25.2 us -> 26.8 us
    ppermute x12 -> x13, waiting for transfers between devices: 19.9 us -> 5.45 us  [gather_rows(): send = lambda block, perm: lax.ppermute(block, 'dp', perm)]
    unnamed x12 -> x24, local copies, waits for them, and re-layouts: 0.96 us -> 5.32 us
    ppermute x12 -> x13, starting transfers between devices: 14.8 us -> 18.1 us  [gather_rows(): send = lambda block, perm: lax.ppermute(block, 'dp', perm)]
  transfers between devices with their start and end apart: 22 -> 23, of which waited for: 10 -> 9; matrix products, arithmetic and copies ran while one was open for 1% -> 1% of each run, Pallas kernels for 19% -> 22%
where the time goes in v5:
time: 105 us; the launch traced here: 104 us
  starting transfers between devices  40.9 us (39%)
  waiting for transfers between devices  29.1 us (28%)
  Pallas kernels  26.8 us (26%)
  local copies, waits for them, and re-layouts  6.3 us (6%)
    ppermute x13, starting transfers between devices, gather_rows(): send = lambda block, perm: lax.ppermute(block, 'dp', perm)  18.1 us
    ppermute x3, waiting for transfers between devices, body(): lax.ppermute(one, 'dp', along_x(k))  8.06 us
    pallas_call x1, Pallas kernels, front(): pl.pallas_call(lambda *refs: front_kernel(parts, *refs), in_specs=[anywhe...  8.01 us
    ppermute x1, waiting for transfers between devices, body(): lax.ppermute(there, 'dp', SWAP_Y)  6.61 us
    all_to_all x1, starting transfers between devices, body(): theirs = lax.all_to_all(term, 'section', 0, 0)  6.19 us
    ppermute x13, waiting for transfers between devices, gather_rows(): send = lambda block, perm: lax.ppermute(block, 'dp', perm)  5.45 us
    unnamed x24, local copies, waits for them, and re-layouts  5.32 us
    all_to_all x1, starting transfers between devices, body(): mine = lax.all_to_all(sums, 'section', 0, 0)  5.16 us
  transfers between devices with their start and end apart: 23, of which 9 were waited for; matrix products, arithmetic and copies ran while one was open for 1% of the time, Pallas kernels for 22%

profile of v5, /device:TPU:1, one launch (start us, length us, event | category | flops | bytes accessed | tf_op | source)
XLA Modules:
  0.0 104.0 jit_solution(940025574363365953)
XLA Ops:
  0.6 2.6 %cut_columns.1 = (bf16[192,1280]{1,0:T(8,128)(2,1)}, bf16[192,1280]{1,0:T(8,128)(2,1)}, bf16[192,1280]{1,0:T(8,128)(2,1)}) custom-call(bf16[192,5120]{1,0:T(8,128)(2,1)} %bitcast.24), custom_call_target="tpu_custom_call" | custom-call | bytes 1 | tf_op jit(solution)/shard_map/cut_columns/pallas_call | solution.py:62
  3.3 3.4 %collective-permute-start.1 = (bf16[192,1280]{1,0:T(8,128)(2,1)}, bf16[192,1280]{1,0:T(8,128)(2,1)S(1)}, u32[]{:S(2)}, u32[]{:S(2)}) collective-permute-start(bf16[192,1280]{1,0:T(8,128)(2,1)} %get-tuple-element.41), channel_id=1, source_target_pairs={{0,6},{1,7},{2,0},{3,1},{4,2},{5,3},{6,4},{7,5},{8,14},{9,15},{10,... | collective-permute-start | bytes 1474568 | tf_op jit(solution)/shard_map/ppermute | solution.py:496
  6.7 0.5 collective-permute-start.2
  7.2 0.6 collective-permute-start
  7.8 8.0 %front.1 = (bf16[192,512]{1,0:T(8,128)(2,1)}, bf16[8,192,640]{2,1,0:T(8,128)(2,1)}) custom-call(bf16[192,5120]{1,0:T(8,128)(2,1)} %bitcast.25, bf16[5120,512]{1,0:T(8,128)(2,1)} %bitcast.28, f32[1,5120]{1,0:T(1,128)} %refs_2_.1, f32[1,128]{1,0:T(1,128)} %refs_3_.1, bf16[192,512]{1,0:T(8,128)(2,1)} %bitcast.31, bf16[192,1280]{1,0:T(8,128)(2,1)} %get-tuple-element.38.refs_5_), custom_call_target="tpu_custom_call" | custom-call | bytes 1 | tf_op jit(solution)/shard_map/front/pallas_call | solution.py:138
  15.8 6.2 %all-to-all-start = ((bf16[8,192,640]{2,1,0:T(8,128)(2,1)}), bf16[8,192,640]{2,1,0:T(8,128)(2,1)}, u32[]{:S(2)}, u32[]{:S(2)}) async-start(bf16[8,192,640]{2,1,0:T(8,128)(2,1)} %get-tuple-element.39), calls=%async_computation | async-start | bytes 3932160 | tf_op jit(solution)/shard_map/all_to_all | solution.py:501
  22.0 2.1 %collective-permute-start.4 = (bf16[192,512]{1,0:T(8,128)(2,1)}, bf16[192,512]{1,0:T(8,128)(2,1)S(1)}, u32[]{:S(2)}, u32[]{:S(2)}) collective-permute-start(bf16[192,512]{1,0:T(8,128)(2,1)} %get-tuple-element.46.k0), channel_id=1, source_target_pairs={{0,6},{1,7},{2,0},{3,1},{4,2},{5,3},{6,4},{7,5},{8,14},{9,15},{10,... | collective-permute-start | bytes 589832 | tf_op jit(solution)/shard_map/ppermute | solution.py:498
  24.1 8.1 %collective-permute-done.up = bf16[192,1280]{1,0:T(8,128)(2,1)S(1)} collective-permute-done((bf16[192,1280]{1,0:T(8,128)(2,1)}, bf16[192,1280]{1,0:T(8,128)(2,1)S(1)}, u32[]{:S(2)}, u32[]{:S(2)}) %collective-permute-start) | collective-permute-done | bytes 491552 | tf_op jit(solution)/shard_map/ppermute | solution.py:496
  32.1 0.5 collective-permute-start.5
  32.7 3.7 %collective-permute-done.3.k1 = bf16[192,512]{1,0:T(8,128)(2,1)S(1)} collective-permute-done((bf16[192,512]{1,0:T(8,128)(2,1)}, bf16[192,512]{1,0:T(8,128)(2,1)S(1)}, u32[]{:S(2)}, u32[]{:S(2)}) %collective-permute-start.3) | collective-permute-done | bytes 196640 | tf_op jit(solution)/shard_map/ppermute | solution.py:498
  36.4 3.6 %collective-permute-done.5.k2 = bf16[192,512]{1,0:T(8,128)(2,1)S(1)} collective-permute-done((bf16[192,512]{1,0:T(8,128)(2,1)}, bf16[192,512]{1,0:T(8,128)(2,1)S(1)}, u32[]{:S(2)}, u32[]{:S(2)}) %collective-permute-start.5) | collective-permute-done | bytes 196640 | tf_op jit(solution)/shard_map/ppermute | solution.py:500
  40.0 0.9 copy-done.11
  40.9 3.5 %wgrad.1 = (f32[2,320,512]{2,1,0:T(8,128)S(1)}, bf16[2,320,512]{2,1,0:T(8,128)(2,1)S(1)}) custom-call(bf16[192,5120]{1,0:T(8,128)(2,1)S(1)} %bitcast.26, bf16[192,1280]{1,0:T(8,128)(2,1)S(1)} %collective-permute-done.up, bf16[192,1280]{1,0:T(8,128)(2,1)S(1)} %collective-permute-done.1.down, bf16[192,1280]{1,0:T(8,128)(2,1)S(1)} %collective-permute-done.2.far, ...), custom_call_target="tpu_custom_call" | custom-call | bytes 1 | tf_op jit(solution)/shard_map/wgrad/pallas_call | solution.py:287
  44.4 1.4 %collective-permute-start.6 = (bf16[2,320,512]{2,1,0:T(8,128)(2,1)S(1)}, bf16[2,320,512]{2,1,0:T(8,128)(2,1)S(1)}, u32[]{:S(2)}, u32[]{:S(2)}) collective-permute-start(bf16[2,320,512]{2,1,0:T(8,128)(2,1)S(1)} %get-tuple-element.48), channel_id=1, source_target_pairs={{0,1},{1,0},{2,3},{3,2},{4,5},{5,4},{6,7},{7,6},{8,9},{9,8},{10,11... | collective-permute-start | bytes 1966088 | tf_op jit(solution)/shard_map/ppermute | solution.py:504
  45.8 1.7 %collective-permute-done.6.got = bf16[2,320,512]{2,1,0:T(8,128)(2,1)S(1)} collective-permute-done((bf16[2,320,512]{2,1,0:T(8,128)(2,1)S(1)}, bf16[2,320,512]{2,1,0:T(8,128)(2,1)S(1)}, u32[]{:S(2)}, u32[]{:S(2)}) %collective-permute-start.6) | collective-permute-done | bytes 655392 | tf_op jit(solution)/shard_map/ppermute | solution.py:504
  47.5 0.1 merge.1
  47.6 3.0 %collective-permute-start.7 = (bf16[320,512]{1,0:T(8,128)(2,1)S(1)}, bf16[320,512]{1,0:T(8,128)(2,1)S(1)}, u32[]{:S(2)}, u32[]{:S(2)}) collective-permute-start(bf16[320,512]{1,0:T(8,128)(2,1)S(1)} %get-tuple-element.50), channel_id=1, source_target_pairs={{0,8},{1,9},{2,10},{3,11},{4,12},{5,13},{6,14},{7,15},{8,0},{9,1},... | collective-permute-start | bytes 983048 | tf_op jit(solution)/shard_map/ppermute | solution.py:512
  50.6 0.8 dynamic-slice_bitcast_fusion
  51.4 0.1 copy.16.gain
  51.5 6.6 %collective-permute-done.7.got = bf16[320,512]{1,0:T(8,128)(2,1)S(1)} collective-permute-done((bf16[320,512]{1,0:T(8,128)(2,1)S(1)}, bf16[320,512]{1,0:T(8,128)(2,1)S(1)}, u32[]{:S(2)}, u32[]{:S(2)}) %collective-permute-start.7) | collective-permute-done | bytes 327712 | tf_op jit(solution)/shard_map/ppermute | solution.py:512
  58.2 1.7 %adam.1 = (f32[1,320,512]{2,1,0:T(8,128)}, f32[1,320,512]{2,1,0:T(8,128)}, f32[1,320,512]{2,1,0:T(8,128)}, bf16[320,512]{1,0:T(8,128)(2,1)}) custom-call(f32[320,512]{1,0:T(8,128)S(1)} %get-tuple-element.49.refs_2_.here, bf16[320,512]{1,0:T(8,128)(2,1)S(1)} %collective-permute-done.7.got, f32[320,1]{1,0:T(8,128)S(1)} %copy.16.gain, ...), custom_call_target="tpu_custom_call" | custom-call | bytes 1 | tf_op jit(solution)/shard_map/adam/pallas_call | solution.py:354
  59.9 0.5 collective-permute-start.16
  60.4 2.9 %collective-permute-start.8 = (bf16[320,512]{1,0:T(8,128)(2,1)}, bf16[320,512]{1,0:T(8,128)(2,1)S(1)}, u32[]{:S(2)}, u32[]{:S(2)}) collective-permute-start(bf16[320,512]{1,0:T(8,128)(2,1)} %get-tuple-element.51.refs_0_), channel_id=1, source_target_pairs={{0,8},{1,9},{2,10},{3,11},{4,12},{5,13},{6,14},{7,15},{8,0},{9,1},... | collective-permute-start | bytes 983048 | tf_op jit(solution)/shard_map/ppermute | solution.py:425
  63.3 1.1 %collective-permute-start.10 = (bf16[320,512]{1,0:T(8,128)(2,1)}, bf16[320,512]{1,0:T(8,128)(2,1)}, u32[]{:S(2)}, u32[]{:S(2)}) collective-permute-start(bf16[320,512]{1,0:T(8,128)(2,1)} %get-tuple-element.51.refs_0_), channel_id=1, source_target_pairs={{0,6},{1,7},{2,0},{3,1},{4,2},{5,3},{6,4},{7,5},{8,14},{9,15},{10,... | collective-permute-start | bytes 983048 | tf_op jit(solution)/shard_map/ppermute | solution.py:425
  64.5 0.3 collective-permute-start.9
  64.8 2.5 %suffix_sums.1 = bf16[8,192,640]{2,1,0:T(8,128)(2,1)} custom-call(bf16[8,192,640]{2,1,0:T(8,128)(2,1)} %all-to-all-done.refs_0_, bf16[192,5120]{1,0:T(8,128)(2,1)} %bitcast.29, f32[320,512]{1,0:T(8,128)} %copy-done.1), custom_call_target="tpu_custom_call" | custom-call | bytes 1 | tf_op jit(solution)/shard_map/suffix_sums/pallas_call | solution.py:202
  67.3 5.2 %all-to-all-start.1 = ((bf16[8,192,640]{2,1,0:T(8,128)(2,1)}), bf16[8,192,640]{2,1,0:T(8,128)(2,1)S(1)}, u32[]{:S(2)}, u32[]{:S(2)}) async-start(bf16[8,192,640]{2,1,0:T(8,128)(2,1)} %suffix_sums.1), calls=%async_computation.1 | async-start | bytes 3932160 | tf_op jit(solution)/shard_map/all_to_all | solution.py:506
  72.5 2.5 %collective-permute-start.17 = (bf16[320,512]{1,0:T(8,128)(2,1)S(1)}, bf16[320,512]{1,0:T(8,128)(2,1)S(1)}, u32[]{:S(2)}, u32[]{:S(2)}) collective-permute-start(bf16[320,512]{1,0:T(8,128)(2,1)S(1)} %collective-permute-done.8.refs_3_), channel_id=1, source_target_pairs={{0,4},{1,5},{2,6},{3,7},{4,0},{5,1},{6,2},{7,3},{8,12},{9,13},{10,... | collective-permute-start | bytes 983048 | tf_op jit(solution)/shard_map/ppermute | solution.py:425
  75.0 2.9 %collective-permute-start.18 = (bf16[320,512]{1,0:T(8,128)(2,1)S(1)}, bf16[320,512]{1,0:T(8,128)(2,1)S(1)}, u32[]{:S(2)}, u32[]{:S(2)}) collective-permute-start(bf16[320,512]{1,0:T(8,128)(2,1)S(1)} %collective-permute-done.16.refs_4_), channel_id=1, source_target_pairs={{0,1},{1,0},{2,3},{3,2},{4,5},{5,4},{6,7},{7,6},{8,9},{9,8},{10,11... | collective-permute-start | bytes 983048 | tf_op jit(solution)/shard_map/ppermute | solution.py:425
  77.9 0.4 collective-permute-done.9.refs_1_
  78.4 2.0 %collective-permute-start.12 = (bf16[320,512]{1,0:T(8,128)(2,1)S(1)}, bf16[320,512]{1,0:T(8,128)(2,1)}, u32[]{:S(2)}, u32[]{:S(2)}) collective-permute-start(bf16[320,512]{1,0:T(8,128)(2,1)S(1)} %collective-permute-done.8.refs_3_), channel_id=1, source_target_pairs={{0,1},{1,0},{2,3},{3,2},{4,5},{5,4},{6,7},{7,6},{8,9},{9,8},{10,11... | collective-permute-start | bytes 983048 | tf_op jit(solution)/shard_map/ppermute | solution.py:425
  80.4 3.0 %collective-permute-start.14 = (bf16[320,512]{1,0:T(8,128)(2,1)S(1)}, bf16[320,512]{1,0:T(8,128)(2,1)}, u32[]{:S(2)}, u32[]{:S(2)}) collective-permute-start(bf16[320,512]{1,0:T(8,128)(2,1)S(1)} %collective-permute-done.8.refs_3_), channel_id=1, source_target_pairs={{0,6},{1,7},{2,0},{3,1},{4,2},{5,3},{6,4},{7,5},{8,14},{9,15},{10,... | collective-permute-start | bytes 983048 | tf_op jit(solution)/shard_map/ppermute | solution.py:425
  83.3 0.1 stack.67.base_ref
  83.4 2.5 %spread.1 = (bf16[960,512]{1,0:T(8,128)(2,1)}, bf16[5120,512]{1,0:T(8,128)(2,1)}) custom-call(s32[16]{0:T(128)S(1)} %stack.67.base_ref, bf16[320,512]{1,0:T(8,128)(2,1)} %get-tuple-element.51.refs_0_, bf16[320,512]{1,0:T(8,128)(2,1)} %collective-permute-done.9.refs_1_, bf16[320,512]{1,0:T(8,128)(2,1)} %collective-permute-done.10.refs_2_), custom_call_target="tpu_custom_call" | custom-call | bytes 1 | tf_op jit(solution)/shard_map/spread/pallas_call | solution.py:407
  85.9 0.7 copy-done.9
  86.7 1.4 %collective-permute-start.19 = (bf16[320,512]{1,0:T(8,128)(2,1)S(1)}, bf16[320,512]{1,0:T(8,128)(2,1)S(1)}, u32[]{:S(2)}, u32[]{:S(2)}) collective-permute-start(bf16[320,512]{1,0:T(8,128)(2,1)S(1)} %collective-permute-done.17.refs_2_), channel_id=1, source_target_pairs={{0,1},{1,0},{2,3},{3,2},{4,5},{5,4},{6,7},{7,6},{8,9},{9,8},{10,11... | collective-permute-start | bytes 983048 | tf_op jit(solution)/shard_map/ppermute | solution.py:425
  88.1 0.7 copy-done.7
  88.8 3.2 %collective-permute-done.11.refs_0_ = bf16[320,512]{1,0:T(8,128)(2,1)} collective-permute-done((bf16[320,512]{1,0:T(8,128)(2,1)S(1)}, bf16[320,512]{1,0:T(8,128)(2,1)}, u32[]{:S(2)}, u32[]{:S(2)}) %collective-permute-start.11) | collective-permute-done | bytes 327712 | tf_op jit(solution)/shard_map/ppermute | solution.py:425
  92.0 0.9 collective-permute-start.15
  93.0 1.4 %collective-permute-done.15.refs_6_ = bf16[320,512]{1,0:T(8,128)(2,1)S(1)} collective-permute-done((bf16[320,512]{1,0:T(8,128)(2,1)}, bf16[320,512]{1,0:T(8,128)(2,1)S(1)}, u32[]{:S(2)}, u32[]{:S(2)}) %collective-permute-start.15) | collective-permute-done | bytes 327712 | tf_op jit(solution)/shard_map/ppermute | solution.py:425
  94.4 0.5 collective-permute-done.13.refs_5_
  94.9 0.4 collective-permute-start.20
  95.2 1.0 copy-done.6
  96.2 1.0 copy-done.8
  97.2 1.0 copy-done.10
  98.2 3.0 %place.2.refs_1_ = bf16[5120,512]{1,0:T(8,128)(2,1)} custom-call(s32[16]{0:T(128)S(1)} %stack.67.base_ref, bf16[320,512]{1,0:T(8,128)(2,1)} %collective-permute-done.11.refs_0_, bf16[320,512]{1,0:T(8,128)(2,1)} %collective-permute-done.14.refs_1_, bf16[320,512]{1,0:T(8,128)(2,1)S(1)} %copy-done.8, ...), custom_call_target="tpu_custom_call", output_to_operand_aliasing={{}: (11, {})} | custom-call | bytes 1 | tf_op jit(solution)/shard_map/place/pallas_call | solution.py:379
  101.1 1.4 %side_by_side.1 = bf16[192,5120]{1,0:T(8,128)(2,1)} custom-call(bf16[8,192,640]{2,1,0:T(8,128)(2,1)S(1)} %all-to-all-done.1.in_ref), custom_call_target="tpu_custom_call" | custom-call | bytes 1 | tf_op jit(solution)/shard_map/side_by_side/pallas_call | solution.py:229
  102.5 1.5 %place.3 = bf16[5120,512]{1,0:T(8,128)(2,1)} custom-call(s32[16]{0:T(128)S(1)} %stack.67.base_ref, bf16[960,512]{1,0:T(8,128)(2,1)S(1)} %collective-permute-done.20.refs_0_, bf16[5120,512]{1,0:T(8,128)(2,1)} %place.2.refs_1_), custom_call_target="tpu_custom_call", output_to_operand_aliasing={{}: (2, {})} | custom-call | bytes 1 | tf_op jit(solution)/shard_map/place/pallas_call | solution.py:379
  (35 shorter events, 0.2 us)
Async XLA Ops:
  3.3 20.8 %collective-permute-start.1 = (bf16[192,1280]{1,0:T(8,128)(2,1)}, bf16[192,1280]{1,0:T(8,128)(2,1)S(1)}, u32[]{:S(2)}, u32[]{:S(2)}) collective-permute-start(bf16[192,1280]{1,0:T(8,128)(2,1)} %get-tuple-element.41), channel_id=1, source_target_pairs={{0,6},{1,7},{2,0},{3,1},{4,2},{5,3},{6,4},{7,5},{8,14},{9,15},{10,... | collective-permute-start | bytes 1474568 | tf_op jit(solution)/shard_map/ppermute | solution.py:496
  6.7 17.4 %collective-permute-start.2 = (bf16[192,1280]{1,0:T(8,128)(2,1)}, bf16[192,1280]{1,0:T(8,128)(2,1)S(1)}, u32[]{:S(2)}, u32[]{:S(2)}) collective-permute-start(bf16[192,1280]{1,0:T(8,128)(2,1)} %get-tuple-element.42), channel_id=1, source_target_pairs={{0,4},{1,5},{2,6},{3,7},{4,0},{5,1},{6,2},{7,3},{8,12},{9,13},{10,... | collective-permute-start | bytes 1474568 | tf_op jit(solution)/shard_map/ppermute | solution.py:496
  7.2 25.0 %collective-permute-start = (bf16[192,1280]{1,0:T(8,128)(2,1)}, bf16[192,1280]{1,0:T(8,128)(2,1)S(1)}, u32[]{:S(2)}, u32[]{:S(2)}) collective-permute-start(bf16[192,1280]{1,0:T(8,128)(2,1)} %get-tuple-element.38.refs_5_), channel_id=1, source_target_pairs={{0,2},{1,3},{2,4},{3,5},{4,6},{5,7},{6,0},{7,1},{8,10},{9,11},{10,... | collective-permute-start | bytes 1474568 | tf_op jit(solution)/shard_map/ppermute | solution.py:496
  15.8 24.2 %copy-start = (bf16[1,2,96,5120]{3,2,1,0:T(8,128)(2,1)S(1)}, bf16[1,2,96,5120]{3,2,1,0:T(8,128)(2,1)}, u32[]{:S(2)}) copy-start(bf16[1,2,96,5120]{3,2,1,0:T(8,128)(2,1)} %param.9) | copy-start | bytes 5898244
  15.8 49.0 %all-to-all-start = ((bf16[8,192,640]{2,1,0:T(8,128)(2,1)}), bf16[8,192,640]{2,1,0:T(8,128)(2,1)}, u32[]{:S(2)}, u32[]{:S(2)}) async-start(bf16[8,192,640]{2,1,0:T(8,128)(2,1)} %get-tuple-element.39), calls=%async_computation | async-start | bytes 3932160 | tf_op jit(solution)/shard_map/all_to_all | solution.py:501
  22.0 10.7 %collective-permute-start.4 = (bf16[192,512]{1,0:T(8,128)(2,1)}, bf16[192,512]{1,0:T(8,128)(2,1)S(1)}, u32[]{:S(2)}, u32[]{:S(2)}) collective-permute-start(bf16[192,512]{1,0:T(8,128)(2,1)} %get-tuple-element.46.k0), channel_id=1, source_target_pairs={{0,6},{1,7},{2,0},{3,1},{4,2},{5,3},{6,4},{7,5},{8,14},{9,15},{10,... | collective-permute-start | bytes 589832 | tf_op jit(solution)/shard_map/ppermute | solution.py:498
  24.1 12.3 %collective-permute-start.3 = (bf16[192,512]{1,0:T(8,128)(2,1)}, bf16[192,512]{1,0:T(8,128)(2,1)S(1)}, u32[]{:S(2)}, u32[]{:S(2)}) collective-permute-start(bf16[192,512]{1,0:T(8,128)(2,1)} %get-tuple-element.46.k0), channel_id=1, source_target_pairs={{0,2},{1,3},{2,4},{3,5},{4,6},{5,7},{6,0},{7,1},{8,10},{9,11},{10,... | collective-permute-start | bytes 589832 | tf_op jit(solution)/shard_map/ppermute | solution.py:498
  32.1 7.8 %collective-permute-start.5 = (bf16[192,512]{1,0:T(8,128)(2,1)}, bf16[192,512]{1,0:T(8,128)(2,1)S(1)}, u32[]{:S(2)}, u32[]{:S(2)}) collective-permute-start(bf16[192,512]{1,0:T(8,128)(2,1)} %get-tuple-element.46.k0), channel_id=1, source_target_pairs={{0,4},{1,5},{2,6},{3,7},{4,0},{5,1},{6,2},{7,3},{8,12},{9,13},{10,... | collective-permute-start | bytes 589832 | tf_op jit(solution)/shard_map/ppermute | solution.py:500
  40.0 0.9 copy-start.11
  44.4 13.8 %copy-start.2 = (f32[1,320,512]{2,1,0:T(8,128)S(1)}, f32[1,320,512]{2,1,0:T(8,128)}, u32[]{:S(2)}) copy-start(f32[1,320,512]{2,1,0:T(8,128)} %master.1) | copy-start | bytes 1966084
  44.4 13.8 %copy-start.3 = (f32[1,320,512]{2,1,0:T(8,128)S(1)}, f32[1,320,512]{2,1,0:T(8,128)}, u32[]{:S(2)}) copy-start(f32[1,320,512]{2,1,0:T(8,128)} %first.1) | copy-start | bytes 1966084
  44.4 13.8 %copy-start.4 = (f32[1,320,512]{2,1,0:T(8,128)S(1)}, f32[1,320,512]{2,1,0:T(8,128)}, u32[]{:S(2)}) copy-start(f32[1,320,512]{2,1,0:T(8,128)} %second.1) | copy-start | bytes 1966084
  44.4 3.1 %collective-permute-start.6 = (bf16[2,320,512]{2,1,0:T(8,128)(2,1)S(1)}, bf16[2,320,512]{2,1,0:T(8,128)(2,1)S(1)}, u32[]{:S(2)}, u32[]{:S(2)}) collective-permute-start(bf16[2,320,512]{2,1,0:T(8,128)(2,1)S(1)} %get-tuple-element.48), channel_id=1, source_target_pairs={{0,1},{1,0},{2,3},{3,2},{4,5},{5,4},{6,7},{7,6},{8,9},{9,8},{10,11... | collective-permute-start | bytes 1966088 | tf_op jit(solution)/shard_map/ppermute | solution.py:504
  47.6 17.2 %copy-start.1 = (f32[320,512]{1,0:T(8,128)}, f32[320,512]{1,0:T(8,128)S(1)}, u32[]{:S(2)}) copy-start(f32[320,512]{1,0:T(8,128)S(1)} %get-tuple-element.49.refs_2_.here) | copy-start | bytes 1966084
  47.6 10.5 %collective-permute-start.7 = (bf16[320,512]{1,0:T(8,128)(2,1)S(1)}, bf16[320,512]{1,0:T(8,128)(2,1)S(1)}, u32[]{:S(2)}, u32[]{:S(2)}) collective-permute-start(bf16[320,512]{1,0:T(8,128)(2,1)S(1)} %get-tuple-element.50), channel_id=1, source_target_pairs={{0,8},{1,9},{2,10},{3,11},{4,12},{5,13},{6,14},{7,15},{8,0},{9,1},... | collective-permute-start | bytes 983048 | tf_op jit(solution)/shard_map/ppermute | solution.py:512
  59.9 12.6 %collective-permute-start.16 = (bf16[320,512]{1,0:T(8,128)(2,1)}, bf16[320,512]{1,0:T(8,128)(2,1)S(1)}, u32[]{:S(2)}, u32[]{:S(2)}) collective-permute-start(bf16[320,512]{1,0:T(8,128)(2,1)} %get-tuple-element.51.refs_0_), channel_id=1, source_target_pairs={{0,4},{1,5},{2,6},{3,7},{4,0},{5,1},{6,2},{7,3},{8,12},{9,13},{10,... | collective-permute-start | bytes 983048 | tf_op jit(solution)/shard_map/ppermute | solution.py:425
  60.4 12.1 %collective-permute-start.8 = (bf16[320,512]{1,0:T(8,128)(2,1)}, bf16[320,512]{1,0:T(8,128)(2,1)S(1)}, u32[]{:S(2)}, u32[]{:S(2)}) collective-permute-start(bf16[320,512]{1,0:T(8,128)(2,1)} %get-tuple-element.51.refs_0_), channel_id=1, source_target_pairs={{0,8},{1,9},{2,10},{3,11},{4,12},{5,13},{6,14},{7,15},{8,0},{9,1},... | collective-permute-start | bytes 983048 | tf_op jit(solution)/shard_map/ppermute | solution.py:425
  63.3 14.6 %collective-permute-start.10 = (bf16[320,512]{1,0:T(8,128)(2,1)}, bf16[320,512]{1,0:T(8,128)(2,1)}, u32[]{:S(2)}, u32[]{:S(2)}) collective-permute-start(bf16[320,512]{1,0:T(8,128)(2,1)} %get-tuple-element.51.refs_0_), channel_id=1, source_target_pairs={{0,6},{1,7},{2,0},{3,1},{4,2},{5,3},{6,4},{7,5},{8,14},{9,15},{10,... | collective-permute-start | bytes 983048 | tf_op jit(solution)/shard_map/ppermute | solution.py:425
  64.5 13.9 %collective-permute-start.9 = (bf16[320,512]{1,0:T(8,128)(2,1)}, bf16[320,512]{1,0:T(8,128)(2,1)}, u32[]{:S(2)}, u32[]{:S(2)}) collective-permute-start(bf16[320,512]{1,0:T(8,128)(2,1)} %get-tuple-element.51.refs_0_), channel_id=1, source_target_pairs={{0,2},{1,3},{2,4},{3,5},{4,6},{5,7},{6,0},{7,1},{8,10},{9,11},{10,... | collective-permute-start | bytes 983048 | tf_op jit(solution)/shard_map/ppermute | solution.py:425
  67.3 33.8 %all-to-all-start.1 = ((bf16[8,192,640]{2,1,0:T(8,128)(2,1)}), bf16[8,192,640]{2,1,0:T(8,128)(2,1)S(1)}, u32[]{:S(2)}, u32[]{:S(2)}) async-start(bf16[8,192,640]{2,1,0:T(8,128)(2,1)} %suffix_sums.1), calls=%async_computation.1 | async-start | bytes 3932160 | tf_op jit(solution)/shard_map/all_to_all | solution.py:506
  72.5 21.9 %copy-start.5 = (bf16[320,512]{1,0:T(8,128)(2,1)}, bf16[320,512]{1,0:T(8,128)(2,1)S(1)}, u32[]{:S(2)}) copy-start(bf16[320,512]{1,0:T(8,128)(2,1)S(1)} %collective-permute-done.8.refs_3_) | copy-start | bytes 983044
  72.5 13.4 %collective-permute-start.17 = (bf16[320,512]{1,0:T(8,128)(2,1)S(1)}, bf16[320,512]{1,0:T(8,128)(2,1)S(1)}, u32[]{:S(2)}, u32[]{:S(2)}) collective-permute-start(bf16[320,512]{1,0:T(8,128)(2,1)S(1)} %collective-permute-done.8.refs_3_), channel_id=1, source_target_pairs={{0,4},{1,5},{2,6},{3,7},{4,0},{5,1},{6,2},{7,3},{8,12},{9,13},{10,... | collective-permute-start | bytes 983048 | tf_op jit(solution)/shard_map/ppermute | solution.py:425
  75.0 10.9 %collective-permute-start.18 = (bf16[320,512]{1,0:T(8,128)(2,1)S(1)}, bf16[320,512]{1,0:T(8,128)(2,1)S(1)}, u32[]{:S(2)}, u32[]{:S(2)}) collective-permute-start(bf16[320,512]{1,0:T(8,128)(2,1)S(1)} %collective-permute-done.16.refs_4_), channel_id=1, source_target_pairs={{0,1},{1,0},{2,3},{3,2},{4,5},{5,4},{6,7},{7,6},{8,9},{9,8},{10,11... | collective-permute-start | bytes 983048 | tf_op jit(solution)/shard_map/ppermute | solution.py:425
  78.3 13.6 %collective-permute-start.11 = (bf16[320,512]{1,0:T(8,128)(2,1)S(1)}, bf16[320,512]{1,0:T(8,128)(2,1)}, u32[]{:S(2)}, u32[]{:S(2)}) collective-permute-start(bf16[320,512]{1,0:T(8,128)(2,1)S(1)} %collective-permute-done.8.refs_3_), channel_id=1, source_target_pairs={{0,2},{1,3},{2,4},{3,5},{4,6},{5,7},{6,0},{7,1},{8,10},{9,11},{10,... | collective-permute-start | bytes 983048 | tf_op jit(solution)/shard_map/ppermute | solution.py:425
  78.4 13.6 %collective-permute-start.12 = (bf16[320,512]{1,0:T(8,128)(2,1)S(1)}, bf16[320,512]{1,0:T(8,128)(2,1)}, u32[]{:S(2)}, u32[]{:S(2)}) collective-permute-start(bf16[320,512]{1,0:T(8,128)(2,1)S(1)} %collective-permute-done.8.refs_3_), channel_id=1, source_target_pairs={{0,1},{1,0},{2,3},{3,2},{4,5},{5,4},{6,7},{7,6},{8,9},{9,8},{10,11... | collective-permute-start | bytes 983048 | tf_op jit(solution)/shard_map/ppermute | solution.py:425
  80.4 11.6 %collective-permute-start.14 = (bf16[320,512]{1,0:T(8,128)(2,1)S(1)}, bf16[320,512]{1,0:T(8,128)(2,1)}, u32[]{:S(2)}, u32[]{:S(2)}) collective-permute-start(bf16[320,512]{1,0:T(8,128)(2,1)S(1)} %collective-permute-done.8.refs_3_), channel_id=1, source_target_pairs={{0,6},{1,7},{2,0},{3,1},{4,2},{5,3},{6,4},{7,5},{8,14},{9,15},{10,... | collective-permute-start | bytes 983048 | tf_op jit(solution)/shard_map/ppermute | solution.py:425
  85.9 0.7 copy-start.9
  86.7 7.7 %collective-permute-start.19 = (bf16[320,512]{1,0:T(8,128)(2,1)S(1)}, bf16[320,512]{1,0:T(8,128)(2,1)S(1)}, u32[]{:S(2)}, u32[]{:S(2)}) collective-permute-start(bf16[320,512]{1,0:T(8,128)(2,1)S(1)} %collective-permute-done.17.refs_2_), channel_id=1, source_target_pairs={{0,1},{1,0},{2,3},{3,2},{4,5},{5,4},{6,7},{7,6},{8,9},{9,8},{10,11... | collective-permute-start | bytes 983048 | tf_op jit(solution)/shard_map/ppermute | solution.py:425
  88.1 0.7 copy-start.7
  92.0 2.4 %collective-permute-start.15 = (bf16[320,512]{1,0:T(8,128)(2,1)}, bf16[320,512]{1,0:T(8,128)(2,1)S(1)}, u32[]{:S(2)}, u32[]{:S(2)}) collective-permute-start(bf16[320,512]{1,0:T(8,128)(2,1)} %collective-permute-done.14.refs_1_), channel_id=1, source_target_pairs={{0,1},{1,0},{2,3},{3,2},{4,5},{5,4},{6,7},{7,6},{8,9},{9,8},{10,11... | collective-permute-start | bytes 983048 | tf_op jit(solution)/shard_map/ppermute | solution.py:425
  92.9 1.9 %collective-permute-start.13 = (bf16[320,512]{1,0:T(8,128)(2,1)}, bf16[320,512]{1,0:T(8,128)(2,1)S(1)}, u32[]{:S(2)}, u32[]{:S(2)}) collective-permute-start(bf16[320,512]{1,0:T(8,128)(2,1)} %collective-permute-done.11.refs_0_), channel_id=1, source_target_pairs={{0,1},{1,0},{2,3},{3,2},{4,5},{5,4},{6,7},{7,6},{8,9},{9,8},{10,11... | collective-permute-start | bytes 983048 | tf_op jit(solution)/shard_map/ppermute | solution.py:425
  94.9 7.6 %collective-permute-start.20 = (bf16[960,512]{1,0:T(8,128)(2,1)}, bf16[960,512]{1,0:T(8,128)(2,1)S(1)}, u32[]{:S(2)}, u32[]{:S(2)}) collective-permute-start(bf16[960,512]{1,0:T(8,128)(2,1)} %get-tuple-element.61), channel_id=1, source_target_pairs={{0,1},{1,0},{2,3},{3,2},{4,5},{5,4},{6,7},{7,6},{8,9},{9,8},{10,11... | collective-permute-start | bytes 2949128 | tf_op jit(solution)/shard_map/ppermute | solution.py:425
  95.2 1.0 copy-start.6
  96.2 1.0 copy-start.8
  97.2 1.0 copy-start.10

commit v6 on v5

--- a/solution.py
+++ b/solution.py
@@ -217,27 +217,6 @@
     )(got, upstream, after)
 
 
-def lay_kernel(in_ref, out_ref):
-    blk = in_ref.shape[2]
-    for p in range(in_ref.shape[0]):
-        out_ref[:, p * blk : (p + 1) * blk] = in_ref[p]
-
-
-def side_by_side(got):
-    parts, rows, blk = got.shape
-    some = parts // 2
-    return pl.pallas_call(
-        lay_kernel,
-        grid=(2,),
-        in_specs=[pl.BlockSpec((some, rows, blk), lambda i: (i, 0, 0))],
-        out_specs=pl.BlockSpec((rows, some * blk), lambda i: (0, i)),
-        out_shape=jax.ShapeDtypeStruct((rows, parts * blk), got.dtype),
-        compiler_params=params(16),
-        cost_estimate=cost(0, 4 * parts * rows * blk),
-        name="side_by_side",
-    )(got)
-
-
 def wgrad_kernel(x_hbm, up, down, far, k0, k1, k3, k2, keep_hbm, send_hbm, av, kv, full, low, in_sems, out_sems):
     rows, wide = up.shape
     blk = wide // 2
@@ -385,10 +364,61 @@
         out_shape=jax.ShapeDtypeStruct((rows, kv), jnp.bfloat16),
         scratch_shapes=[pltpu.SemaphoreType.DMA((len(plan),))],
         input_output_aliases={} if whole is None else {1 + count: 0},
-        compiler_params=params(16),
+        compiler_params=params(60),
         cost_estimate=cost(0, 4 * kv * len(plan) * block),
         name="place",
     )(bases, *blocks, *prior)
+
+
+def finish(slots, bases, late, got, whole):
+    parts, rows, blk = got.shape
+    some = parts // 2
+    count = len(slots)
+    block = late.shape[0] // count
+
+    def kernel(base_ref, late_ref, got_ref, whole_ref, out, wide_ref, sems):
+        copies = []
+        for n, slot in enumerate(slots):
+            at = pl.multiple_of(base_ref[slot], 32)
+            src = late_ref.at[pl.ds(n * block, block)]
+            copies.append(pltpu.make_async_copy(src, out.at[pl.ds(at, block)], sems.at[n]))
+
+        @pl.when(pl.program_id(0) == 0)
+        def _():
+            for one in copies:
+                one.start()
+
+        for p in range(some):
+            wide_ref[:, p * blk : (p + 1) * blk] = got_ref[p]
+
+        @pl.when(pl.program_id(0) == 1)
+        def _():
+            for one in copies:
+                one.wait()
+
+    return pl.pallas_call(
+        kernel,
+        grid=(2,),
+        in_specs=[
+            pl.BlockSpec(memory_space=pltpu.SMEM),
+            pl.BlockSpec(late.shape, lambda i: (0, 0)),
+            pl.BlockSpec((some, rows, blk), lambda i: (i, 0, 0)),
+            pl.BlockSpec(memory_space=pl.ANY),
+        ],
+        out_specs=[
+            pl.BlockSpec(memory_space=pl.ANY),
+            pl.BlockSpec((rows, some * blk), lambda i: (0, i)),
+        ],
+        out_shape=[
+            jax.ShapeDtypeStruct(whole.shape, whole.dtype),
+            jax.ShapeDtypeStruct((rows, parts * blk), got.dtype),
+        ],
+        scratch_shapes=[pltpu.SemaphoreType.DMA((count,))],
+        input_output_aliases={3: 0},
+        compiler_params=params(16),
+        cost_estimate=cost(0, 4 * got.size),
+        name="finish",
+    )(bases, late, got, whole)
 
 
 def spread(slots, bases, blocks, rows):
@@ -420,7 +450,7 @@
     )(bases, *blocks)
 
 
-def gather_rows(own, y, x, core):
+def gather_rows(own, y, x, core, mine):
     rows, kv = own.shape
     send = lambda block, perm: lax.ppermute(block, "dp", perm)
     up, down = along_x(1), along_x(-1)
@@ -468,7 +498,8 @@
     c1 = send(stack, SWAP_CORE)
     middle += [(yr, 1, 0), (e, 0, 2)]
     whole = put(middle, whole, [(middle, swapped + early)])
-    return put([], whole, [(near, [c1])])
+    slots = [slot + 1 for slot in slots]
+    return finish(slots, bases, c1, mine, whole)
 
 
 def body(
@@ -504,15 +535,14 @@
     here, there = merge(keep, lax.ppermute(away, "dp", SWAP_CORE))
     sums = suffix_sums(theirs, upstream, here)
     mine = lax.all_to_all(sums, "section", 0, 0)
-    input_grad = side_by_side(mine).reshape(activations.shape)
 
     own_rows = here.shape[0]
     gain_rows = lax.dynamic_slice(norm_gain[0], (me * own_rows,), (own_rows,))[:, None]
     new_master, new_first, new_second, own = adam(
         here, lax.ppermute(there, "dp", SWAP_Y), gain_rows, master, first_moment, second_moment
     )
-    new_weight = gather_rows(own, y, x, core)
-    return (input_grad, new_weight[None], new_master, new_first, new_second)
+    new_weight, input_grad = gather_rows(own, y, x, core, mine)
+    return (input_grad.reshape(activations.shape), new_weight[None], new_master, new_first, new_second)
 
 
 def solution(mesh):

time: 105 us -> 103 us (0.981)
  local copies, waits for them, and re-layouts: 6.3 us -> 3.67 us
  starting transfers between devices: 40.9 us -> 42.3 us
    unnamed x24 -> x22, local copies, waits for them, and re-layouts: 5.32 us -> 2.69 us
    ppermute x13, starting transfers between devices: 18.1 us -> 19.5 us  [gather_rows(): send = lambda block, perm: lax.ppermute(block, 'dp', perm)]
    pallas_call x1, Pallas kernels: 1.37 us -> 2.45 us  [finish(): pl.pallas_call(kernel, grid=(2,), in_specs=[pl.BlockSpec(memory_space=plt...]
    pallas_call x2 -> x1, Pallas kernels: 4.47 us -> 3.65 us  [place(): pl.pallas_call(kernel, in_specs=[pl.BlockSpec(memory_space=pltpu.SMEM)] +...]
  transfers between devices with their start and end apart: 23 -> 23, of which waited for: 9 -> 7; matrix products, arithmetic and copies ran while one was open for 1% -> 1% of each run, Pallas kernels for 22% -> 21%
where the time goes in v6:
time: 103 us; the launch traced here: 102 us
  starting transfers between devices  42.3 us (41%)
  waiting for transfers between devices  29.2 us (28%)
  Pallas kernels  26.4 us (26%)
  local copies, waits for them, and re-layouts  3.67 us (4%)
    ppermute x13, starting transfers between devices, gather_rows(): send = lambda block, perm: lax.ppermute(block, 'dp', perm)  19.5 us
    ppermute x3, waiting for transfers between devices, body(): lax.ppermute(one, 'dp', along_x(k))  8.06 us
    pallas_call x1, Pallas kernels, front(): pl.pallas_call(lambda *refs: front_kernel(parts, *refs), in_specs=[anywhe...  8.01 us
    ppermute x1, waiting for transfers between devices, body(): lax.ppermute(there, 'dp', SWAP_Y)  6.61 us
    all_to_all x1, starting transfers between devices, body(): theirs = lax.all_to_all(term, 'section', 0, 0)  6.19 us
    ppermute x13, waiting for transfers between devices, gather_rows(): send = lambda block, perm: lax.ppermute(block, 'dp', perm)  5.47 us
    all_to_all x1, starting transfers between devices, body(): mine = lax.all_to_all(sums, 'section', 0, 0)  5.16 us
    ppermute x3, starting transfers between devices, body(): lax.ppermute(one, 'dp', along_x(k))  4.5 us
  transfers between devices with their start and end apart: 23, of which 7 were waited for; matrix products, arithmetic and copies ran while one was open for 1% of the time, Pallas kernels for 21%

profile of v6, /device:TPU:1, one launch (start us, length us, event | category | flops | bytes accessed | tf_op | source)
XLA Modules:
  0.0 102.4 jit_solution(8722488253223850825)
XLA Ops:
  0.6 2.6 %cut_columns.1 = (bf16[192,1280]{1,0:T(8,128)(2,1)}, bf16[192,1280]{1,0:T(8,128)(2,1)}, bf16[192,1280]{1,0:T(8,128)(2,1)}) custom-call(bf16[192,5120]{1,0:T(8,128)(2,1)} %bitcast.24), custom_call_target="tpu_custom_call" | custom-call | bytes 1 | tf_op jit(solution)/shard_map/cut_columns/pallas_call | solution.py:62
  3.3 3.4 %collective-permute-start.1 = (bf16[192,1280]{1,0:T(8,128)(2,1)}, bf16[192,1280]{1,0:T(8,128)(2,1)S(1)}, u32[]{:S(2)}, u32[]{:S(2)}) collective-permute-start(bf16[192,1280]{1,0:T(8,128)(2,1)} %get-tuple-element.42), channel_id=1, source_target_pairs={{0,6},{1,7},{2,0},{3,1},{4,2},{5,3},{6,4},{7,5},{8,14},{9,15},{10,... | collective-permute-start | bytes 1474568 | tf_op jit(solution)/shard_map/ppermute | solution.py:527
  6.7 0.5 collective-permute-start.2
  7.2 0.6 collective-permute-start
  7.8 8.0 %front.1 = (bf16[192,512]{1,0:T(8,128)(2,1)}, bf16[8,192,640]{2,1,0:T(8,128)(2,1)}) custom-call(bf16[192,5120]{1,0:T(8,128)(2,1)} %bitcast.25, bf16[5120,512]{1,0:T(8,128)(2,1)} %bitcast.28, f32[1,5120]{1,0:T(1,128)} %refs_2_.1, f32[1,128]{1,0:T(1,128)} %refs_3_.1, bf16[192,512]{1,0:T(8,128)(2,1)} %bitcast.30, bf16[192,1280]{1,0:T(8,128)(2,1)} %get-tuple-element.40.refs_5_), custom_call_target="tpu_custom_call" | custom-call | bytes 1 | tf_op jit(solution)/shard_map/front/pallas_call | solution.py:138
  15.8 0.0 copy-start
  15.8 6.2 %all-to-all-start = ((bf16[8,192,640]{2,1,0:T(8,128)(2,1)}), bf16[8,192,640]{2,1,0:T(8,128)(2,1)}, u32[]{:S(2)}, u32[]{:S(2)}) async-start(bf16[8,192,640]{2,1,0:T(8,128)(2,1)} %get-tuple-element.63), calls=%async_computation | async-start | bytes 3932160 | tf_op jit(solution)/shard_map/all_to_all | solution.py:532
  22.0 2.1 %collective-permute-start.4 = (bf16[192,512]{1,0:T(8,128)(2,1)}, bf16[192,512]{1,0:T(8,128)(2,1)S(1)}, u32[]{:S(2)}, u32[]{:S(2)}) collective-permute-start(bf16[192,512]{1,0:T(8,128)(2,1)} %get-tuple-element.47.k0), channel_id=1, source_target_pairs={{0,6},{1,7},{2,0},{3,1},{4,2},{5,3},{6,4},{7,5},{8,14},{9,15},{10,... | collective-permute-start | bytes 589832 | tf_op jit(solution)/shard_map/ppermute | solution.py:529
  24.1 8.1 %collective-permute-done.up = bf16[192,1280]{1,0:T(8,128)(2,1)S(1)} collective-permute-done((bf16[192,1280]{1,0:T(8,128)(2,1)}, bf16[192,1280]{1,0:T(8,128)(2,1)S(1)}, u32[]{:S(2)}, u32[]{:S(2)}) %collective-permute-start) | collective-permute-done | bytes 491552 | tf_op jit(solution)/shard_map/ppermute | solution.py:527
  32.1 0.5 collective-permute-start.5
  32.7 3.7 %collective-permute-done.3.k1 = bf16[192,512]{1,0:T(8,128)(2,1)S(1)} collective-permute-done((bf16[192,512]{1,0:T(8,128)(2,1)}, bf16[192,512]{1,0:T(8,128)(2,1)S(1)}, u32[]{:S(2)}, u32[]{:S(2)}) %collective-permute-start.3) | collective-permute-done | bytes 196640 | tf_op jit(solution)/shard_map/ppermute | solution.py:529
  36.4 3.6 %collective-permute-done.5.k2 = bf16[192,512]{1,0:T(8,128)(2,1)S(1)} collective-permute-done((bf16[192,512]{1,0:T(8,128)(2,1)}, bf16[192,512]{1,0:T(8,128)(2,1)S(1)}, u32[]{:S(2)}, u32[]{:S(2)}) %collective-permute-start.5) | collective-permute-done | bytes 196640 | tf_op jit(solution)/shard_map/ppermute | solution.py:531
  40.0 0.9 copy-done.5
  40.9 3.5 %wgrad.1 = (f32[2,320,512]{2,1,0:T(8,128)S(1)}, bf16[2,320,512]{2,1,0:T(8,128)(2,1)S(1)}) custom-call(bf16[192,5120]{1,0:T(8,128)(2,1)S(1)} %bitcast.26, bf16[192,1280]{1,0:T(8,128)(2,1)S(1)} %collective-permute-done.up, bf16[192,1280]{1,0:T(8,128)(2,1)S(1)} %collective-permute-done.1.down, bf16[192,1280]{1,0:T(8,128)(2,1)S(1)} %collective-permute-done.2.far, ...), custom_call_target="tpu_custom_call" | custom-call | bytes 1 | tf_op jit(solution)/shard_map/wgrad/pallas_call | solution.py:266
  44.4 0.0 copy-start.2
  44.4 0.0 copy-start.3
  44.4 1.4 %collective-permute-start.6 = (bf16[2,320,512]{2,1,0:T(8,128)(2,1)S(1)}, bf16[2,320,512]{2,1,0:T(8,128)(2,1)S(1)}, u32[]{:S(2)}, u32[]{:S(2)}) collective-permute-start(bf16[2,320,512]{2,1,0:T(8,128)(2,1)S(1)} %get-tuple-element.49), channel_id=1, source_target_pairs={{0,1},{1,0},{2,3},{3,2},{4,5},{5,4},{6,7},{7,6},{8,9},{9,8},{10,11... | collective-permute-start | bytes 1966088 | tf_op jit(solution)/shard_map/ppermute | solution.py:535
  45.8 1.7 %collective-permute-done.6.got = bf16[2,320,512]{2,1,0:T(8,128)(2,1)S(1)} collective-permute-done((bf16[2,320,512]{2,1,0:T(8,128)(2,1)S(1)}, bf16[2,320,512]{2,1,0:T(8,128)(2,1)S(1)}, u32[]{:S(2)}, u32[]{:S(2)}) %collective-permute-start.6) | collective-permute-done | bytes 655392 | tf_op jit(solution)/shard_map/ppermute | solution.py:535
  47.5 0.1 merge.1
  47.6 3.0 %collective-permute-start.7 = (bf16[320,512]{1,0:T(8,128)(2,1)S(1)}, bf16[320,512]{1,0:T(8,128)(2,1)S(1)}, u32[]{:S(2)}, u32[]{:S(2)}) collective-permute-start(bf16[320,512]{1,0:T(8,128)(2,1)S(1)} %get-tuple-element.51), channel_id=1, source_target_pairs={{0,8},{1,9},{2,10},{3,11},{4,12},{5,13},{6,14},{7,15},{8,0},{9,1},... | collective-permute-start | bytes 983048 | tf_op jit(solution)/shard_map/ppermute | solution.py:542
  50.6 0.8 dynamic-slice_bitcast_fusion
  51.4 0.1 copy.16.gain
  51.5 6.6 %collective-permute-done.7.got = bf16[320,512]{1,0:T(8,128)(2,1)S(1)} collective-permute-done((bf16[320,512]{1,0:T(8,128)(2,1)S(1)}, bf16[320,512]{1,0:T(8,128)(2,1)S(1)}, u32[]{:S(2)}, u32[]{:S(2)}) %collective-permute-start.7) | collective-permute-done | bytes 327712 | tf_op jit(solution)/shard_map/ppermute | solution.py:542
  58.2 1.7 %adam.1 = (f32[1,320,512]{2,1,0:T(8,128)}, f32[1,320,512]{2,1,0:T(8,128)}, f32[1,320,512]{2,1,0:T(8,128)}, bf16[320,512]{1,0:T(8,128)(2,1)S(1)}) custom-call(f32[320,512]{1,0:T(8,128)S(1)} %get-tuple-element.50.here.refs_2_, bf16[320,512]{1,0:T(8,128)(2,1)S(1)} %collective-permute-done.7.got, f32[320,1]{1,0:T(8,128)S(1)} %copy.16.gain, ...), custom_call_target="tpu_custom_call" | custom-call | bytes 1 | tf_op jit(solution)/shard_map/adam/pallas_call | solution.py:333
  59.9 0.5 collective-permute-start.16
  60.4 2.9 %collective-permute-start.8 = (bf16[320,512]{1,0:T(8,128)(2,1)S(1)}, bf16[320,512]{1,0:T(8,128)(2,1)}, u32[]{:S(2)}, u32[]{:S(2)}) collective-permute-start(bf16[320,512]{1,0:T(8,128)(2,1)S(1)} %get-tuple-element.52.refs_0_), channel_id=1, source_target_pairs={{0,8},{1,9},{2,10},{3,11},{4,12},{5,13},{6,14},{7,15},{8,0},{9,1},... | collective-permute-start | bytes 983048 | tf_op jit(solution)/shard_map/ppermute | solution.py:455
  63.3 1.1 %collective-permute-start.10 = (bf16[320,512]{1,0:T(8,128)(2,1)S(1)}, bf16[320,512]{1,0:T(8,128)(2,1)S(1)}, u32[]{:S(2)}, u32[]{:S(2)}) collective-permute-start(bf16[320,512]{1,0:T(8,128)(2,1)S(1)} %get-tuple-element.52.refs_0_), channel_id=1, source_target_pairs={{0,6},{1,7},{2,0},{3,1},{4,2},{5,3},{6,4},{7,5},{8,14},{9,15},{10,... | collective-permute-start | bytes 983048 | tf_op jit(solution)/shard_map/ppermute | solution.py:455
  64.4 0.3 collective-permute-start.9
  64.8 2.5 %suffix_sums.1 = bf16[8,192,640]{2,1,0:T(8,128)(2,1)} custom-call(bf16[8,192,640]{2,1,0:T(8,128)(2,1)} %all-to-all-done.refs_0_, bf16[192,5120]{1,0:T(8,128)(2,1)} %bitcast.29, f32[320,512]{1,0:T(8,128)} %copy-done.1), custom_call_target="tpu_custom_call" | custom-call | bytes 1 | tf_op jit(solution)/shard_map/suffix_sums/pallas_call | solution.py:202
  67.3 5.2 %all-to-all-start.1 = ((bf16[8,192,640]{2,1,0:T(8,128)(2,1)}), bf16[8,192,640]{2,1,0:T(8,128)(2,1)S(1)}, u32[]{:S(2)}, u32[]{:S(2)}) async-start(bf16[8,192,640]{2,1,0:T(8,128)(2,1)} %suffix_sums.1), calls=%async_computation.1 | async-start | bytes 3932160 | tf_op jit(solution)/shard_map/all_to_all | solution.py:537
  72.5 2.5 %collective-permute-start.17 = (bf16[320,512]{1,0:T(8,128)(2,1)}, bf16[320,512]{1,0:T(8,128)(2,1)}, u32[]{:S(2)}, u32[]{:S(2)}) collective-permute-start(bf16[320,512]{1,0:T(8,128)(2,1)} %collective-permute-done.8.refs_3_), channel_id=1, source_target_pairs={{0,4},{1,5},{2,6},{3,7},{4,0},{5,1},{6,2},{7,3},{8,12},{9,13},{10,... | collective-permute-start | bytes 983048 | tf_op jit(solution)/shard_map/ppermute | solution.py:455
  75.0 2.9 %collective-permute-start.18 = (bf16[320,512]{1,0:T(8,128)(2,1)S(1)}, bf16[320,512]{1,0:T(8,128)(2,1)}, u32[]{:S(2)}, u32[]{:S(2)}) collective-permute-start(bf16[320,512]{1,0:T(8,128)(2,1)S(1)} %collective-permute-done.16.refs_4_), channel_id=1, source_target_pairs={{0,1},{1,0},{2,3},{3,2},{4,5},{5,4},{6,7},{7,6},{8,9},{9,8},{10,11... | collective-permute-start | bytes 983048 | tf_op jit(solution)/shard_map/ppermute | solution.py:455
  77.9 0.5 collective-permute-start.11
  78.4 1.2 %collective-permute-start.12 = (bf16[320,512]{1,0:T(8,128)(2,1)}, bf16[320,512]{1,0:T(8,128)(2,1)}, u32[]{:S(2)}, u32[]{:S(2)}) collective-permute-start(bf16[320,512]{1,0:T(8,128)(2,1)} %collective-permute-done.8.refs_3_), channel_id=1, source_target_pairs={{0,1},{1,0},{2,3},{3,2},{4,5},{5,4},{6,7},{7,6},{8,9},{9,8},{10,11... | collective-permute-start | bytes 983048 | tf_op jit(solution)/shard_map/ppermute | solution.py:455
  79.6 3.0 %collective-permute-start.14 = (bf16[320,512]{1,0:T(8,128)(2,1)}, bf16[320,512]{1,0:T(8,128)(2,1)}, u32[]{:S(2)}, u32[]{:S(2)}) collective-permute-start(bf16[320,512]{1,0:T(8,128)(2,1)} %collective-permute-done.8.refs_3_), channel_id=1, source_target_pairs={{0,6},{1,7},{2,0},{3,1},{4,2},{5,3},{6,4},{7,5},{8,14},{9,15},{10,... | collective-permute-start | bytes 983048 | tf_op jit(solution)/shard_map/ppermute | solution.py:455
  82.5 0.1 stack.67.base_ref
  82.6 1.9 %spread.1 = (bf16[960,512]{1,0:T(8,128)(2,1)}, bf16[5120,512]{1,0:T(8,128)(2,1)}) custom-call(s32[16]{0:T(128)S(1)} %stack.67.base_ref, bf16[320,512]{1,0:T(8,128)(2,1)S(1)} %get-tuple-element.52.refs_0_, bf16[320,512]{1,0:T(8,128)(2,1)S(1)} %collective-permute-done.9.refs_1_, bf16[320,512]{1,0:T(8,128)(2,1)S(1)} %collective-permute-done.10.refs_2_), custom_call_target="tpu_custom_call" | custom-call | bytes 1 | tf_op jit(solution)/shard_map/spread/pallas_call | solution.py:437
  84.5 3.1 %collective-permute-start.19 = (bf16[320,512]{1,0:T(8,128)(2,1)}, bf16[320,512]{1,0:T(8,128)(2,1)S(1)}, u32[]{:S(2)}, u32[]{:S(2)}) collective-permute-start(bf16[320,512]{1,0:T(8,128)(2,1)} %collective-permute-done.17.refs_2_), channel_id=1, source_target_pairs={{0,1},{1,0},{2,3},{3,2},{4,5},{5,4},{6,7},{7,6},{8,9},{9,8},{10,11... | collective-permute-start | bytes 983048 | tf_op jit(solution)/shard_map/ppermute | solution.py:455
  87.6 4.1 %collective-permute-done.11.refs_0_ = bf16[320,512]{1,0:T(8,128)(2,1)} collective-permute-done((bf16[320,512]{1,0:T(8,128)(2,1)}, bf16[320,512]{1,0:T(8,128)(2,1)}, u32[]{:S(2)}, u32[]{:S(2)}) %collective-permute-start.11) | collective-permute-done | bytes 327712 | tf_op jit(solution)/shard_map/ppermute | solution.py:455
  91.7 1.0 collective-permute-start.15
  92.7 0.1 collective-permute-start.13
  92.7 1.4 %collective-permute-done.15.refs_6_ = bf16[320,512]{1,0:T(8,128)(2,1)S(1)} collective-permute-done((bf16[320,512]{1,0:T(8,128)(2,1)}, bf16[320,512]{1,0:T(8,128)(2,1)S(1)}, u32[]{:S(2)}, u32[]{:S(2)}) %collective-permute-start.15) | collective-permute-done | bytes 327712 | tf_op jit(solution)/shard_map/ppermute | solution.py:455
  94.1 0.7 copy-done.10
  94.9 0.4 collective-permute-start.20
  95.2 0.3 copy-done.9
  95.6 3.7 %place.1.whole_ref = bf16[5120,512]{1,0:T(8,128)(2,1)} custom-call(s32[16]{0:T(128)} %copy-done.6, bf16[320,512]{1,0:T(8,128)(2,1)} %collective-permute-done.11.refs_0_, bf16[320,512]{1,0:T(8,128)(2,1)} %collective-permute-done.14.refs_1_, bf16[320,512]{1,0:T(8,128)(2,1)} %collective-permute-done.17.refs_2_, ...), custom_call_target="tpu_custom_call", output_to_operand_aliasing={{}: (11, {})} | custom-call | bytes 1 | tf_op jit(solution)/shard_map/place/pallas_call | solution.py:358
  99.3 0.7 copy-done.7
  99.9 2.5 %finish.1 = (bf16[5120,512]{1,0:T(8,128)(2,1)}, bf16[192,5120]{1,0:T(8,128)(2,1)}) custom-call(s32[16]{0:T(128)S(1)} %copy-done.7, bf16[960,512]{1,0:T(8,128)(2,1)S(1)} %collective-permute-done.20.late_ref, bf16[8,192,640]{2,1,0:T(8,128)(2,1)S(1)} %all-to-all-done.1.got_ref, bf16[5120,512]{1,0:T(8,128)(2,1)} %place.1.whole_ref), custom_call_target="tpu_custom_call", output_to_operand_aliasing={{0}: (3, {})} | custom-call | bytes 1 | tf_op jit(solution)/shard_map/finish/pallas_call | solution.py:399
  (32 shorter events, 0.1 us)
Async XLA Ops:
  3.3 20.8 %collective-permute-start.1 = (bf16[192,1280]{1,0:T(8,128)(2,1)}, bf16[192,1280]{1,0:T(8,128)(2,1)S(1)}, u32[]{:S(2)}, u32[]{:S(2)}) collective-permute-start(bf16[192,1280]{1,0:T(8,128)(2,1)} %get-tuple-element.42), channel_id=1, source_target_pairs={{0,6},{1,7},{2,0},{3,1},{4,2},{5,3},{6,4},{7,5},{8,14},{9,15},{10,... | collective-permute-start | bytes 1474568 | tf_op jit(solution)/shard_map/ppermute | solution.py:527
  6.7 17.4 %collective-permute-start.2 = (bf16[192,1280]{1,0:T(8,128)(2,1)}, bf16[192,1280]{1,0:T(8,128)(2,1)S(1)}, u32[]{:S(2)}, u32[]{:S(2)}) collective-permute-start(bf16[192,1280]{1,0:T(8,128)(2,1)} %get-tuple-element.43), channel_id=1, source_target_pairs={{0,4},{1,5},{2,6},{3,7},{4,0},{5,1},{6,2},{7,3},{8,12},{9,13},{10,... | collective-permute-start | bytes 1474568 | tf_op jit(solution)/shard_map/ppermute | solution.py:527
  7.2 25.0 %collective-permute-start = (bf16[192,1280]{1,0:T(8,128)(2,1)}, bf16[192,1280]{1,0:T(8,128)(2,1)S(1)}, u32[]{:S(2)}, u32[]{:S(2)}) collective-permute-start(bf16[192,1280]{1,0:T(8,128)(2,1)} %get-tuple-element.40.refs_5_), channel_id=1, source_target_pairs={{0,2},{1,3},{2,4},{3,5},{4,6},{5,7},{6,0},{7,1},{8,10},{9,11},{10,... | collective-permute-start | bytes 1474568 | tf_op jit(solution)/shard_map/ppermute | solution.py:527
  15.8 24.2 %copy-start = (bf16[1,2,96,5120]{3,2,1,0:T(8,128)(2,1)S(1)}, bf16[1,2,96,5120]{3,2,1,0:T(8,128)(2,1)}, u32[]{:S(2)}) copy-start(bf16[1,2,96,5120]{3,2,1,0:T(8,128)(2,1)} %param.9) | copy-start | bytes 5898244
  15.8 48.9 %all-to-all-start = ((bf16[8,192,640]{2,1,0:T(8,128)(2,1)}), bf16[8,192,640]{2,1,0:T(8,128)(2,1)}, u32[]{:S(2)}, u32[]{:S(2)}) async-start(bf16[8,192,640]{2,1,0:T(8,128)(2,1)} %get-tuple-element.63), calls=%async_computation | async-start | bytes 3932160 | tf_op jit(solution)/shard_map/all_to_all | solution.py:532
  22.0 10.7 %collective-permute-start.4 = (bf16[192,512]{1,0:T(8,128)(2,1)}, bf16[192,512]{1,0:T(8,128)(2,1)S(1)}, u32[]{:S(2)}, u32[]{:S(2)}) collective-permute-start(bf16[192,512]{1,0:T(8,128)(2,1)} %get-tuple-element.47.k0), channel_id=1, source_target_pairs={{0,6},{1,7},{2,0},{3,1},{4,2},{5,3},{6,4},{7,5},{8,14},{9,15},{10,... | collective-permute-start | bytes 589832 | tf_op jit(solution)/shard_map/ppermute | solution.py:529
  24.1 12.3 %collective-permute-start.3 = (bf16[192,512]{1,0:T(8,128)(2,1)}, bf16[192,512]{1,0:T(8,128)(2,1)S(1)}, u32[]{:S(2)}, u32[]{:S(2)}) collective-permute-start(bf16[192,512]{1,0:T(8,128)(2,1)} %get-tuple-element.47.k0), channel_id=1, source_target_pairs={{0,2},{1,3},{2,4},{3,5},{4,6},{5,7},{6,0},{7,1},{8,10},{9,11},{10,... | collective-permute-start | bytes 589832 | tf_op jit(solution)/shard_map/ppermute | solution.py:529
  32.1 7.8 %collective-permute-start.5 = (bf16[192,512]{1,0:T(8,128)(2,1)}, bf16[192,512]{1,0:T(8,128)(2,1)S(1)}, u32[]{:S(2)}, u32[]{:S(2)}) collective-permute-start(bf16[192,512]{1,0:T(8,128)(2,1)} %get-tuple-element.47.k0), channel_id=1, source_target_pairs={{0,4},{1,5},{2,6},{3,7},{4,0},{5,1},{6,2},{7,3},{8,12},{9,13},{10,... | collective-permute-start | bytes 589832 | tf_op jit(solution)/shard_map/ppermute | solution.py:531
  40.0 0.9 copy-start.5
  44.4 13.8 %copy-start.2 = (f32[1,320,512]{2,1,0:T(8,128)S(1)}, f32[1,320,512]{2,1,0:T(8,128)}, u32[]{:S(2)}) copy-start(f32[1,320,512]{2,1,0:T(8,128)} %master.1) | copy-start | bytes 1966084
  44.4 13.8 %copy-start.3 = (f32[1,320,512]{2,1,0:T(8,128)S(1)}, f32[1,320,512]{2,1,0:T(8,128)}, u32[]{:S(2)}) copy-start(f32[1,320,512]{2,1,0:T(8,128)} %first.1) | copy-start | bytes 1966084
  44.4 13.8 %copy-start.4 = (f32[1,320,512]{2,1,0:T(8,128)S(1)}, f32[1,320,512]{2,1,0:T(8,128)}, u32[]{:S(2)}) copy-start(f32[1,320,512]{2,1,0:T(8,128)} %second.1) | copy-start | bytes 1966084
  44.4 3.1 %collective-permute-start.6 = (bf16[2,320,512]{2,1,0:T(8,128)(2,1)S(1)}, bf16[2,320,512]{2,1,0:T(8,128)(2,1)S(1)}, u32[]{:S(2)}, u32[]{:S(2)}) collective-permute-start(bf16[2,320,512]{2,1,0:T(8,128)(2,1)S(1)} %get-tuple-element.49), channel_id=1, source_target_pairs={{0,1},{1,0},{2,3},{3,2},{4,5},{5,4},{6,7},{7,6},{8,9},{9,8},{10,11... | collective-permute-start | bytes 1966088 | tf_op jit(solution)/shard_map/ppermute | solution.py:535
  47.6 17.1 %copy-start.1 = (f32[320,512]{1,0:T(8,128)}, f32[320,512]{1,0:T(8,128)S(1)}, u32[]{:S(2)}) copy-start(f32[320,512]{1,0:T(8,128)S(1)} %get-tuple-element.50.here.refs_2_) | copy-start | bytes 1966084
  47.6 10.5 %collective-permute-start.7 = (bf16[320,512]{1,0:T(8,128)(2,1)S(1)}, bf16[320,512]{1,0:T(8,128)(2,1)S(1)}, u32[]{:S(2)}, u32[]{:S(2)}) collective-permute-start(bf16[320,512]{1,0:T(8,128)(2,1)S(1)} %get-tuple-element.51), channel_id=1, source_target_pairs={{0,8},{1,9},{2,10},{3,11},{4,12},{5,13},{6,14},{7,15},{8,0},{9,1},... | collective-permute-start | bytes 983048 | tf_op jit(solution)/shard_map/ppermute | solution.py:542
  59.9 12.6 %collective-permute-start.16 = (bf16[320,512]{1,0:T(8,128)(2,1)S(1)}, bf16[320,512]{1,0:T(8,128)(2,1)S(1)}, u32[]{:S(2)}, u32[]{:S(2)}) collective-permute-start(bf16[320,512]{1,0:T(8,128)(2,1)S(1)} %get-tuple-element.52.refs_0_), channel_id=1, source_target_pairs={{0,4},{1,5},{2,6},{3,7},{4,0},{5,1},{6,2},{7,3},{8,12},{9,13},{10,... | collective-permute-start | bytes 983048 | tf_op jit(solution)/shard_map/ppermute | solution.py:455
  60.4 12.1 %collective-permute-start.8 = (bf16[320,512]{1,0:T(8,128)(2,1)S(1)}, bf16[320,512]{1,0:T(8,128)(2,1)}, u32[]{:S(2)}, u32[]{:S(2)}) collective-permute-start(bf16[320,512]{1,0:T(8,128)(2,1)S(1)} %get-tuple-element.52.refs_0_), channel_id=1, source_target_pairs={{0,8},{1,9},{2,10},{3,11},{4,12},{5,13},{6,14},{7,15},{8,0},{9,1},... | collective-permute-start | bytes 983048 | tf_op jit(solution)/shard_map/ppermute | solution.py:455
  63.3 14.6 %collective-permute-start.10 = (bf16[320,512]{1,0:T(8,128)(2,1)S(1)}, bf16[320,512]{1,0:T(8,128)(2,1)S(1)}, u32[]{:S(2)}, u32[]{:S(2)}) collective-permute-start(bf16[320,512]{1,0:T(8,128)(2,1)S(1)} %get-tuple-element.52.refs_0_), channel_id=1, source_target_pairs={{0,6},{1,7},{2,0},{3,1},{4,2},{5,3},{6,4},{7,5},{8,14},{9,15},{10,... | collective-permute-start | bytes 983048 | tf_op jit(solution)/shard_map/ppermute | solution.py:455
  64.4 13.5 %collective-permute-start.9 = (bf16[320,512]{1,0:T(8,128)(2,1)S(1)}, bf16[320,512]{1,0:T(8,128)(2,1)S(1)}, u32[]{:S(2)}, u32[]{:S(2)}) collective-permute-start(bf16[320,512]{1,0:T(8,128)(2,1)S(1)} %get-tuple-element.52.refs_0_), channel_id=1, source_target_pairs={{0,2},{1,3},{2,4},{3,5},{4,6},{5,7},{6,0},{7,1},{8,10},{9,11},{10,... | collective-permute-start | bytes 983048 | tf_op jit(solution)/shard_map/ppermute | solution.py:455
  67.3 32.0 %all-to-all-start.1 = ((bf16[8,192,640]{2,1,0:T(8,128)(2,1)}), bf16[8,192,640]{2,1,0:T(8,128)(2,1)S(1)}, u32[]{:S(2)}, u32[]{:S(2)}) async-start(bf16[8,192,640]{2,1,0:T(8,128)(2,1)} %suffix_sums.1), calls=%async_computation.1 | async-start | bytes 3932160 | tf_op jit(solution)/shard_map/all_to_all | solution.py:537
  72.4 22.8 %copy-start.8 = (bf16[320,512]{1,0:T(8,128)(2,1)}, bf16[320,512]{1,0:T(8,128)(2,1)S(1)}, u32[]{:S(2)}) copy-start(bf16[320,512]{1,0:T(8,128)(2,1)S(1)} %collective-permute-done.16.refs_4_) | copy-start | bytes 983044
  72.5 12.0 %collective-permute-start.17 = (bf16[320,512]{1,0:T(8,128)(2,1)}, bf16[320,512]{1,0:T(8,128)(2,1)}, u32[]{:S(2)}, u32[]{:S(2)}) collective-permute-start(bf16[320,512]{1,0:T(8,128)(2,1)} %collective-permute-done.8.refs_3_), channel_id=1, source_target_pairs={{0,4},{1,5},{2,6},{3,7},{4,0},{5,1},{6,2},{7,3},{8,12},{9,13},{10,... | collective-permute-start | bytes 983048 | tf_op jit(solution)/shard_map/ppermute | solution.py:455
  75.0 9.5 %collective-permute-start.18 = (bf16[320,512]{1,0:T(8,128)(2,1)S(1)}, bf16[320,512]{1,0:T(8,128)(2,1)}, u32[]{:S(2)}, u32[]{:S(2)}) collective-permute-start(bf16[320,512]{1,0:T(8,128)(2,1)S(1)} %collective-permute-done.16.refs_4_), channel_id=1, source_target_pairs={{0,1},{1,0},{2,3},{3,2},{4,5},{5,4},{6,7},{7,6},{8,9},{9,8},{10,11... | collective-permute-start | bytes 983048 | tf_op jit(solution)/shard_map/ppermute | solution.py:455
  77.9 13.8 %collective-permute-start.11 = (bf16[320,512]{1,0:T(8,128)(2,1)}, bf16[320,512]{1,0:T(8,128)(2,1)}, u32[]{:S(2)}, u32[]{:S(2)}) collective-permute-start(bf16[320,512]{1,0:T(8,128)(2,1)} %collective-permute-done.8.refs_3_), channel_id=1, source_target_pairs={{0,2},{1,3},{2,4},{3,5},{4,6},{5,7},{6,0},{7,1},{8,10},{9,11},{10,... | collective-permute-start | bytes 983048 | tf_op jit(solution)/shard_map/ppermute | solution.py:455
  78.4 13.3 %collective-permute-start.12 = (bf16[320,512]{1,0:T(8,128)(2,1)}, bf16[320,512]{1,0:T(8,128)(2,1)}, u32[]{:S(2)}, u32[]{:S(2)}) collective-permute-start(bf16[320,512]{1,0:T(8,128)(2,1)} %collective-permute-done.8.refs_3_), channel_id=1, source_target_pairs={{0,1},{1,0},{2,3},{3,2},{4,5},{5,4},{6,7},{7,6},{8,9},{9,8},{10,11... | collective-permute-start | bytes 983048 | tf_op jit(solution)/shard_map/ppermute | solution.py:455
  79.6 12.1 %collective-permute-start.14 = (bf16[320,512]{1,0:T(8,128)(2,1)}, bf16[320,512]{1,0:T(8,128)(2,1)}, u32[]{:S(2)}, u32[]{:S(2)}) collective-permute-start(bf16[320,512]{1,0:T(8,128)(2,1)} %collective-permute-done.8.refs_3_), channel_id=1, source_target_pairs={{0,6},{1,7},{2,0},{3,1},{4,2},{5,3},{6,4},{7,5},{8,14},{9,15},{10,... | collective-permute-start | bytes 983048 | tf_op jit(solution)/shard_map/ppermute | solution.py:455
  82.6 12.6 %copy-start.6 = (s32[16]{0:T(128)}, s32[16]{0:T(128)S(1)}, u32[]{:S(2)}) copy-start(s32[16]{0:T(128)S(1)} %stack.67.base_ref) | copy-start | bytes 196
  84.5 9.6 %collective-permute-start.19 = (bf16[320,512]{1,0:T(8,128)(2,1)}, bf16[320,512]{1,0:T(8,128)(2,1)S(1)}, u32[]{:S(2)}, u32[]{:S(2)}) collective-permute-start(bf16[320,512]{1,0:T(8,128)(2,1)} %collective-permute-done.17.refs_2_), channel_id=1, source_target_pairs={{0,1},{1,0},{2,3},{3,2},{4,5},{5,4},{6,7},{7,6},{8,9},{9,8},{10,11... | collective-permute-start | bytes 983048 | tf_op jit(solution)/shard_map/ppermute | solution.py:455
  91.7 2.4 %collective-permute-start.15 = (bf16[320,512]{1,0:T(8,128)(2,1)}, bf16[320,512]{1,0:T(8,128)(2,1)S(1)}, u32[]{:S(2)}, u32[]{:S(2)}) collective-permute-start(bf16[320,512]{1,0:T(8,128)(2,1)} %collective-permute-done.14.refs_1_), channel_id=1, source_target_pairs={{0,1},{1,0},{2,3},{3,2},{4,5},{5,4},{6,7},{7,6},{8,9},{9,8},{10,11... | collective-permute-start | bytes 983048 | tf_op jit(solution)/shard_map/ppermute | solution.py:455
  92.7 2.2 %collective-permute-start.13 = (bf16[320,512]{1,0:T(8,128)(2,1)}, bf16[320,512]{1,0:T(8,128)(2,1)}, u32[]{:S(2)}, u32[]{:S(2)}) collective-permute-start(bf16[320,512]{1,0:T(8,128)(2,1)} %collective-permute-done.11.refs_0_), channel_id=1, source_target_pairs={{0,1},{1,0},{2,3},{3,2},{4,5},{5,4},{6,7},{7,6},{8,9},{9,8},{10,11... | collective-permute-start | bytes 983048 | tf_op jit(solution)/shard_map/ppermute | solution.py:455
  94.1 0.7 copy-start.10
  94.8 0.7 copy-start.9
  94.9 4.4 %collective-permute-start.20 = (bf16[960,512]{1,0:T(8,128)(2,1)}, bf16[960,512]{1,0:T(8,128)(2,1)S(1)}, u32[]{:S(2)}, u32[]{:S(2)}) collective-permute-start(bf16[960,512]{1,0:T(8,128)(2,1)} %get-tuple-element.62), channel_id=1, source_target_pairs={{0,1},{1,0},{2,3},{3,2},{4,5},{5,4},{6,7},{7,6},{8,9},{9,8},{10,11... | collective-permute-start | bytes 2949128 | tf_op jit(solution)/shard_map/ppermute | solution.py:455
  99.3 0.7 copy-start.7

commit v7 on v6

--- a/solution.py
+++ b/solution.py
@@ -421,7 +421,7 @@
     )(bases, late, got, whole)
 
 
-def spread(slots, bases, blocks, rows):
+def spread(slots, bases, blocks, rows, together):
     count = len(blocks)
     block, kv = blocks[0].shape
 
@@ -430,7 +430,8 @@
         moves = []
         for n, slot in enumerate(slots):
             at = pl.multiple_of(base_ref[slot], 32)
-            moves.append((ins[n], stack.at[pl.ds(n * block, block)]))
+            if n < together:
+                moves.append((ins[n], stack.at[pl.ds(n * block, block)]))
             moves.append((ins[n], whole.at[pl.ds(at, block)]))
         run_copies(moves, sems)
 
@@ -440,7 +441,7 @@
         + [pl.BlockSpec(memory_space=pltpu.VMEM)] * count,
         out_specs=[pl.BlockSpec(memory_space=pl.ANY)] * 2,
         out_shape=[
-            jax.ShapeDtypeStruct((count * block, kv), jnp.bfloat16),
+            jax.ShapeDtypeStruct((together * block, kv), jnp.bfloat16),
             jax.ShapeDtypeStruct((rows, kv), jnp.bfloat16),
         ],
         scratch_shapes=[pltpu.SemaphoreType.DMA((2 * count,))],
@@ -487,8 +488,9 @@
         return place(plan, bases, blocks, 16 * rows, kv, whole)
 
     near = [(own, 0, 0), (a, 0, -1), (b, 0, 1)]
-    slots = [(dy * 4 + order.index(dx)) * 2 for _, dy, dx in near]
-    stack, whole = spread(slots, bases, [one[0] for one in near], 16 * rows)
+    others = [(yr, 1, 0), (e, 0, 2)]
+    slots = [(dy * 4 + order.index(dx)) * 2 for _, dy, dx in near + others]
+    stack, whole = spread(slots, bases, [one[0] for one in near + others], 16 * rows, len(near))
     early = [send(yr, SWAP_CORE), send(e, SWAP_CORE)]
     a2, stack, early[0] = lax.optimization_barrier((a2, stack, early[0]))
     e2, early[1] = lax.optimization_barrier((e2, early[1]))
@@ -496,9 +498,8 @@
     swapped = [send(one[0], SWAP_CORE) for one in middle]
     stack, swapped[0], swapped[1], swapped[2] = lax.optimization_barrier((stack, swapped[0], swapped[1], swapped[2]))
     c1 = send(stack, SWAP_CORE)
-    middle += [(yr, 1, 0), (e, 0, 2)]
-    whole = put(middle, whole, [(middle, swapped + early)])
-    slots = [slot + 1 for slot in slots]
+    whole = put(middle, whole, [(middle, swapped), (others, early)])
+    slots = [slot + 1 for slot in slots[: len(near)]]
     return finish(slots, bases, c1, mine, whole)
 
 

time: 103 us -> 102 us (level)
  local copies, waits for them, and re-layouts: 3.67 us -> 2.58 us
    unnamed x22 -> x20, local copies, waits for them, and re-layouts: 2.69 us -> 1.6 us
  transfers between devices with their start and end apart: 23 -> 23, of which waited for: 7 -> 8; matrix products, arithmetic and copies ran while one was open for 1% -> 1% of each run, Pallas kernels for 21% -> 21%
where the time goes in v7:
time: 102 us; the launch traced here: 101 us
  starting transfers between devices  41.4 us (41%)
  waiting for transfers between devices  30 us (29%)
  Pallas kernels  26.7 us (26%)
  local copies, waits for them, and re-layouts  2.58 us (3%)
    ppermute x13, starting transfers between devices, gather_rows(): send = lambda block, perm: lax.ppermute(block, 'dp', perm)  18.5 us
    ppermute x3, waiting for transfers between devices, body(): lax.ppermute(one, 'dp', along_x(k))  8.06 us
    pallas_call x1, Pallas kernels, front(): pl.pallas_call(lambda *refs: front_kernel(parts, *refs), in_specs=[anywhe...  8.01 us
    ppermute x1, waiting for transfers between devices, body(): lax.ppermute(there, 'dp', SWAP_Y)  6.61 us
    ppermute x13, waiting for transfers between devices, gather_rows(): send = lambda block, perm: lax.ppermute(block, 'dp', perm)  6.33 us
    all_to_all x1, starting transfers between devices, body(): theirs = lax.all_to_all(term, 'section', 0, 0)  6.19 us
    all_to_all x1, starting transfers between devices, body(): mine = lax.all_to_all(sums, 'section', 0, 0)  5.16 us
    ppermute x3, starting transfers between devices, body(): lax.ppermute(one, 'dp', along_x(k))  4.5 us
  transfers between devices with their start and end apart: 23, of which 8 were waited for; matrix products, arithmetic and copies ran while one was open for 1% of the time, Pallas kernels for 21%

profile of v7, /device:TPU:1, one launch (start us, length us, event | category | flops | bytes accessed | tf_op | source)
XLA Modules:
  0.0 101.5 jit_solution(17057065220070008571)
XLA Ops:
  0.6 2.6 %cut_columns.1 = (bf16[192,1280]{1,0:T(8,128)(2,1)}, bf16[192,1280]{1,0:T(8,128)(2,1)}, bf16[192,1280]{1,0:T(8,128)(2,1)}) custom-call(bf16[192,5120]{1,0:T(8,128)(2,1)} %bitcast.24), custom_call_target="tpu_custom_call" | custom-call | bytes 1 | tf_op jit(solution)/shard_map/cut_columns/pallas_call | solution.py:62
  3.3 3.4 %collective-permute-start.1 = (bf16[192,1280]{1,0:T(8,128)(2,1)}, bf16[192,1280]{1,0:T(8,128)(2,1)S(1)}, u32[]{:S(2)}, u32[]{:S(2)}) collective-permute-start(bf16[192,1280]{1,0:T(8,128)(2,1)} %get-tuple-element.42), channel_id=1, source_target_pairs={{0,6},{1,7},{2,0},{3,1},{4,2},{5,3},{6,4},{7,5},{8,14},{9,15},{10,... | collective-permute-start | bytes 1474568 | tf_op jit(solution)/shard_map/ppermute | solution.py:528
  6.7 0.5 collective-permute-start.2
  7.2 0.6 collective-permute-start
  7.8 8.0 %front.1 = (bf16[192,512]{1,0:T(8,128)(2,1)}, bf16[8,192,640]{2,1,0:T(8,128)(2,1)}) custom-call(bf16[192,5120]{1,0:T(8,128)(2,1)} %bitcast.25, bf16[5120,512]{1,0:T(8,128)(2,1)} %bitcast.28, f32[1,5120]{1,0:T(1,128)} %refs_2_.1, f32[1,128]{1,0:T(1,128)} %refs_3_.1, bf16[192,512]{1,0:T(8,128)(2,1)} %bitcast.30, bf16[192,1280]{1,0:T(8,128)(2,1)} %get-tuple-element.40.refs_5_), custom_call_target="tpu_custom_call" | custom-call | bytes 1 | tf_op jit(solution)/shard_map/front/pallas_call | solution.py:138
  15.8 0.0 copy-start
  15.8 6.2 %all-to-all-start = ((bf16[8,192,640]{2,1,0:T(8,128)(2,1)}), bf16[8,192,640]{2,1,0:T(8,128)(2,1)}, u32[]{:S(2)}, u32[]{:S(2)}) async-start(bf16[8,192,640]{2,1,0:T(8,128)(2,1)} %get-tuple-element.63), calls=%async_computation | async-start | bytes 3932160 | tf_op jit(solution)/shard_map/all_to_all | solution.py:533
  22.0 2.1 %collective-permute-start.4 = (bf16[192,512]{1,0:T(8,128)(2,1)}, bf16[192,512]{1,0:T(8,128)(2,1)S(1)}, u32[]{:S(2)}, u32[]{:S(2)}) collective-permute-start(bf16[192,512]{1,0:T(8,128)(2,1)} %get-tuple-element.47.k0), channel_id=1, source_target_pairs={{0,6},{1,7},{2,0},{3,1},{4,2},{5,3},{6,4},{7,5},{8,14},{9,15},{10,... | collective-permute-start | bytes 589832 | tf_op jit(solution)/shard_map/ppermute | solution.py:530
  24.1 8.1 %collective-permute-done.up = bf16[192,1280]{1,0:T(8,128)(2,1)S(1)} collective-permute-done((bf16[192,1280]{1,0:T(8,128)(2,1)}, bf16[192,1280]{1,0:T(8,128)(2,1)S(1)}, u32[]{:S(2)}, u32[]{:S(2)}) %collective-permute-start) | collective-permute-done | bytes 491552 | tf_op jit(solution)/shard_map/ppermute | solution.py:528
  32.1 0.5 collective-permute-start.5
  32.7 3.7 %collective-permute-done.3.k1 = bf16[192,512]{1,0:T(8,128)(2,1)S(1)} collective-permute-done((bf16[192,512]{1,0:T(8,128)(2,1)}, bf16[192,512]{1,0:T(8,128)(2,1)S(1)}, u32[]{:S(2)}, u32[]{:S(2)}) %collective-permute-start.3) | collective-permute-done | bytes 196640 | tf_op jit(solution)/shard_map/ppermute | solution.py:530
  36.4 3.6 %collective-permute-done.5.k2 = bf16[192,512]{1,0:T(8,128)(2,1)S(1)} collective-permute-done((bf16[192,512]{1,0:T(8,128)(2,1)}, bf16[192,512]{1,0:T(8,128)(2,1)S(1)}, u32[]{:S(2)}, u32[]{:S(2)}) %collective-permute-start.5) | collective-permute-done | bytes 196640 | tf_op jit(solution)/shard_map/ppermute | solution.py:532
  40.0 0.9 copy-done.5
  40.9 3.5 %wgrad.1 = (f32[2,320,512]{2,1,0:T(8,128)S(1)}, bf16[2,320,512]{2,1,0:T(8,128)(2,1)S(1)}) custom-call(bf16[192,5120]{1,0:T(8,128)(2,1)S(1)} %bitcast.26, bf16[192,1280]{1,0:T(8,128)(2,1)S(1)} %collective-permute-done.up, bf16[192,1280]{1,0:T(8,128)(2,1)S(1)} %collective-permute-done.1.down, bf16[192,1280]{1,0:T(8,128)(2,1)S(1)} %collective-permute-done.2.far, ...), custom_call_target="tpu_custom_call" | custom-call | bytes 1 | tf_op jit(solution)/shard_map/wgrad/pallas_call | solution.py:266
  44.4 0.0 copy-start.2
  44.4 0.0 copy-start.3
  44.4 1.4 %collective-permute-start.6 = (bf16[2,320,512]{2,1,0:T(8,128)(2,1)S(1)}, bf16[2,320,512]{2,1,0:T(8,128)(2,1)S(1)}, u32[]{:S(2)}, u32[]{:S(2)}) collective-permute-start(bf16[2,320,512]{2,1,0:T(8,128)(2,1)S(1)} %get-tuple-element.49), channel_id=1, source_target_pairs={{0,1},{1,0},{2,3},{3,2},{4,5},{5,4},{6,7},{7,6},{8,9},{9,8},{10,11... | collective-permute-start | bytes 1966088 | tf_op jit(solution)/shard_map/ppermute | solution.py:536
  45.8 1.7 %collective-permute-done.6.got = bf16[2,320,512]{2,1,0:T(8,128)(2,1)S(1)} collective-permute-done((bf16[2,320,512]{2,1,0:T(8,128)(2,1)S(1)}, bf16[2,320,512]{2,1,0:T(8,128)(2,1)S(1)}, u32[]{:S(2)}, u32[]{:S(2)}) %collective-permute-start.6) | collective-permute-done | bytes 655392 | tf_op jit(solution)/shard_map/ppermute | solution.py:536
  47.5 0.1 merge.1
  47.6 3.0 %collective-permute-start.7 = (bf16[320,512]{1,0:T(8,128)(2,1)S(1)}, bf16[320,512]{1,0:T(8,128)(2,1)S(1)}, u32[]{:S(2)}, u32[]{:S(2)}) collective-permute-start(bf16[320,512]{1,0:T(8,128)(2,1)S(1)} %get-tuple-element.51), channel_id=1, source_target_pairs={{0,8},{1,9},{2,10},{3,11},{4,12},{5,13},{6,14},{7,15},{8,0},{9,1},... | collective-permute-start | bytes 983048 | tf_op jit(solution)/shard_map/ppermute | solution.py:543
  50.6 0.8 dynamic-slice_bitcast_fusion
  51.4 0.1 copy.16.gain
  51.5 6.6 %collective-permute-done.7.got = bf16[320,512]{1,0:T(8,128)(2,1)S(1)} collective-permute-done((bf16[320,512]{1,0:T(8,128)(2,1)S(1)}, bf16[320,512]{1,0:T(8,128)(2,1)S(1)}, u32[]{:S(2)}, u32[]{:S(2)}) %collective-permute-start.7) | collective-permute-done | bytes 327712 | tf_op jit(solution)/shard_map/ppermute | solution.py:543
  58.2 1.7 %adam.1 = (f32[1,320,512]{2,1,0:T(8,128)}, f32[1,320,512]{2,1,0:T(8,128)}, f32[1,320,512]{2,1,0:T(8,128)}, bf16[320,512]{1,0:T(8,128)(2,1)S(1)}) custom-call(f32[320,512]{1,0:T(8,128)S(1)} %get-tuple-element.50.here.refs_2_, bf16[320,512]{1,0:T(8,128)(2,1)S(1)} %collective-permute-done.7.got, f32[320,1]{1,0:T(8,128)S(1)} %copy.16.gain, ...), custom_call_target="tpu_custom_call" | custom-call | bytes 1 | tf_op jit(solution)/shard_map/adam/pallas_call | solution.py:333
  59.9 0.5 collective-permute-start.12
  60.4 2.9 %collective-permute-start.8 = (bf16[320,512]{1,0:T(8,128)(2,1)S(1)}, bf16[320,512]{1,0:T(8,128)(2,1)S(1)}, u32[]{:S(2)}, u32[]{:S(2)}) collective-permute-start(bf16[320,512]{1,0:T(8,128)(2,1)S(1)} %get-tuple-element.52.refs_0_), channel_id=1, source_target_pairs={{0,8},{1,9},{2,10},{3,11},{4,12},{5,13},{6,14},{7,15},{8,0},{9,1},... | collective-permute-start | bytes 983048 | tf_op jit(solution)/shard_map/ppermute | solution.py:456
  63.3 1.1 %collective-permute-start.10 = (bf16[320,512]{1,0:T(8,128)(2,1)S(1)}, bf16[320,512]{1,0:T(8,128)(2,1)S(1)}, u32[]{:S(2)}, u32[]{:S(2)}) collective-permute-start(bf16[320,512]{1,0:T(8,128)(2,1)S(1)} %get-tuple-element.52.refs_0_), channel_id=1, source_target_pairs={{0,6},{1,7},{2,0},{3,1},{4,2},{5,3},{6,4},{7,5},{8,14},{9,15},{10,... | collective-permute-start | bytes 983048 | tf_op jit(solution)/shard_map/ppermute | solution.py:456
  64.4 0.3 collective-permute-start.9
  64.8 2.5 %suffix_sums.1 = bf16[8,192,640]{2,1,0:T(8,128)(2,1)} custom-call(bf16[8,192,640]{2,1,0:T(8,128)(2,1)} %all-to-all-done.refs_0_, bf16[192,5120]{1,0:T(8,128)(2,1)} %bitcast.29, f32[320,512]{1,0:T(8,128)} %copy-done.1), custom_call_target="tpu_custom_call" | custom-call | bytes 1 | tf_op jit(solution)/shard_map/suffix_sums/pallas_call | solution.py:202
  67.3 5.2 %all-to-all-start.1 = ((bf16[8,192,640]{2,1,0:T(8,128)(2,1)}), bf16[8,192,640]{2,1,0:T(8,128)(2,1)S(1)}, u32[]{:S(2)}, u32[]{:S(2)}) async-start(bf16[8,192,640]{2,1,0:T(8,128)(2,1)} %suffix_sums.1), calls=%async_computation.1 | async-start | bytes 3932160 | tf_op jit(solution)/shard_map/all_to_all | solution.py:538
  72.5 2.5 %collective-permute-start.17 = (bf16[320,512]{1,0:T(8,128)(2,1)S(1)}, bf16[320,512]{1,0:T(8,128)(2,1)}, u32[]{:S(2)}, u32[]{:S(2)}) collective-permute-start(bf16[320,512]{1,0:T(8,128)(2,1)S(1)} %collective-permute-done.8.refs_3_), channel_id=1, source_target_pairs={{0,4},{1,5},{2,6},{3,7},{4,0},{5,1},{6,2},{7,3},{8,12},{9,13},{10,... | collective-permute-start | bytes 983048 | tf_op jit(solution)/shard_map/ppermute | solution.py:456
  75.0 2.9 %collective-permute-start.18 = (bf16[320,512]{1,0:T(8,128)(2,1)S(1)}, bf16[320,512]{1,0:T(8,128)(2,1)}, u32[]{:S(2)}, u32[]{:S(2)}) collective-permute-start(bf16[320,512]{1,0:T(8,128)(2,1)S(1)} %collective-permute-done.12.refs_4_), channel_id=1, source_target_pairs={{0,1},{1,0},{2,3},{3,2},{4,5},{5,4},{6,7},{7,6},{8,9},{9,8},{10,11... | collective-permute-start | bytes 983048 | tf_op jit(solution)/shard_map/ppermute | solution.py:456
  77.9 0.0 collective-permute-done.9.refs_1_
  77.9 0.5 collective-permute-start.11
  78.4 1.6 %collective-permute-start.13 = (bf16[320,512]{1,0:T(8,128)(2,1)S(1)}, bf16[320,512]{1,0:T(8,128)(2,1)}, u32[]{:S(2)}, u32[]{:S(2)}) collective-permute-start(bf16[320,512]{1,0:T(8,128)(2,1)S(1)} %collective-permute-done.8.refs_3_), channel_id=1, source_target_pairs={{0,1},{1,0},{2,3},{3,2},{4,5},{5,4},{6,7},{7,6},{8,9},{9,8},{10,11... | collective-permute-start | bytes 983048 | tf_op jit(solution)/shard_map/ppermute | solution.py:456
  79.9 3.0 %collective-permute-start.15 = (bf16[320,512]{1,0:T(8,128)(2,1)S(1)}, bf16[320,512]{1,0:T(8,128)(2,1)}, u32[]{:S(2)}, u32[]{:S(2)}) collective-permute-start(bf16[320,512]{1,0:T(8,128)(2,1)S(1)} %collective-permute-done.8.refs_3_), channel_id=1, source_target_pairs={{0,6},{1,7},{2,0},{3,1},{4,2},{5,3},{6,4},{7,5},{8,14},{9,15},{10,... | collective-permute-start | bytes 983048 | tf_op jit(solution)/shard_map/ppermute | solution.py:456
  82.9 0.1 stack.67.base_ref
  83.0 2.5 %spread.1 = (bf16[960,512]{1,0:T(8,128)(2,1)}, bf16[5120,512]{1,0:T(8,128)(2,1)}) custom-call(s32[16]{0:T(128)S(1)} %stack.67.base_ref, bf16[320,512]{1,0:T(8,128)(2,1)S(1)} %get-tuple-element.52.refs_0_, bf16[320,512]{1,0:T(8,128)(2,1)} %collective-permute-done.9.refs_1_, bf16[320,512]{1,0:T(8,128)(2,1)S(1)} %collective-permute-done.10.refs_2_, ...), custom_call_target="tpu_custom_call" | custom-call | bytes 1 | tf_op jit(solution)/shard_map/spread/pallas_call | solution.py:438
  85.5 1.9 %collective-permute-start.19 = (bf16[320,512]{1,0:T(8,128)(2,1)}, bf16[320,512]{1,0:T(8,128)(2,1)S(1)}, u32[]{:S(2)}, u32[]{:S(2)}) collective-permute-start(bf16[320,512]{1,0:T(8,128)(2,1)} %collective-permute-done.17.refs_2_), channel_id=1, source_target_pairs={{0,1},{1,0},{2,3},{3,2},{4,5},{5,4},{6,7},{7,6},{8,9},{9,8},{10,11... | collective-permute-start | bytes 983048 | tf_op jit(solution)/shard_map/ppermute | solution.py:456
  87.4 4.3 %collective-permute-done.11.refs_0_ = bf16[320,512]{1,0:T(8,128)(2,1)} collective-permute-done((bf16[320,512]{1,0:T(8,128)(2,1)S(1)}, bf16[320,512]{1,0:T(8,128)(2,1)}, u32[]{:S(2)}, u32[]{:S(2)}) %collective-permute-start.11) | collective-permute-done | bytes 327712 | tf_op jit(solution)/shard_map/ppermute | solution.py:456
  91.7 0.9 collective-permute-start.16
  92.7 0.1 collective-permute-start.14
  92.7 1.4 %collective-permute-done.16.refs_4_ = bf16[320,512]{1,0:T(8,128)(2,1)S(1)} collective-permute-done((bf16[320,512]{1,0:T(8,128)(2,1)}, bf16[320,512]{1,0:T(8,128)(2,1)S(1)}, u32[]{:S(2)}, u32[]{:S(2)}) %collective-permute-start.16) | collective-permute-done | bytes 327712 | tf_op jit(solution)/shard_map/ppermute | solution.py:456
  94.1 0.6 collective-permute-done.14.refs_3_
  94.7 0.4 collective-permute-start.20
  95.1 3.2 %place.1.whole_ref = bf16[5120,512]{1,0:T(8,128)(2,1)} custom-call(s32[16]{0:T(128)} %copy-done.6, bf16[320,512]{1,0:T(8,128)(2,1)} %collective-permute-done.11.refs_0_, bf16[320,512]{1,0:T(8,128)(2,1)} %collective-permute-done.15.refs_1_, bf16[320,512]{1,0:T(8,128)(2,1)} %collective-permute-done.17.refs_2_, ...), custom_call_target="tpu_custom_call", output_to_operand_aliasing={{}: (9, {})} | custom-call | bytes 1 | tf_op jit(solution)/shard_map/place/pallas_call | solution.py:358
  98.4 0.6 copy-done.7
  99.0 2.5 %finish.1 = (bf16[5120,512]{1,0:T(8,128)(2,1)}, bf16[192,5120]{1,0:T(8,128)(2,1)}) custom-call(s32[16]{0:T(128)S(1)} %copy-done.7, bf16[960,512]{1,0:T(8,128)(2,1)S(1)} %collective-permute-done.20.late_ref, bf16[8,192,640]{2,1,0:T(8,128)(2,1)S(1)} %all-to-all-done.1.got_ref, bf16[5120,512]{1,0:T(8,128)(2,1)} %place.1.whole_ref), custom_call_target="tpu_custom_call", output_to_operand_aliasing={{0}: (3, {})} | custom-call | bytes 1 | tf_op jit(solution)/shard_map/finish/pallas_call | solution.py:399
  (30 shorter events, 0.1 us)
Async XLA Ops:
  3.3 20.8 %collective-permute-start.1 = (bf16[192,1280]{1,0:T(8,128)(2,1)}, bf16[192,1280]{1,0:T(8,128)(2,1)S(1)}, u32[]{:S(2)}, u32[]{:S(2)}) collective-permute-start(bf16[192,1280]{1,0:T(8,128)(2,1)} %get-tuple-element.42), channel_id=1, source_target_pairs={{0,6},{1,7},{2,0},{3,1},{4,2},{5,3},{6,4},{7,5},{8,14},{9,15},{10,... | collective-permute-start | bytes 1474568 | tf_op jit(solution)/shard_map/ppermute | solution.py:528
  6.7 17.4 %collective-permute-start.2 = (bf16[192,1280]{1,0:T(8,128)(2,1)}, bf16[192,1280]{1,0:T(8,128)(2,1)S(1)}, u32[]{:S(2)}, u32[]{:S(2)}) collective-permute-start(bf16[192,1280]{1,0:T(8,128)(2,1)} %get-tuple-element.43), channel_id=1, source_target_pairs={{0,4},{1,5},{2,6},{3,7},{4,0},{5,1},{6,2},{7,3},{8,12},{9,13},{10,... | collective-permute-start | bytes 1474568 | tf_op jit(solution)/shard_map/ppermute | solution.py:528
  7.2 25.0 %collective-permute-start = (bf16[192,1280]{1,0:T(8,128)(2,1)}, bf16[192,1280]{1,0:T(8,128)(2,1)S(1)}, u32[]{:S(2)}, u32[]{:S(2)}) collective-permute-start(bf16[192,1280]{1,0:T(8,128)(2,1)} %get-tuple-element.40.refs_5_), channel_id=1, source_target_pairs={{0,2},{1,3},{2,4},{3,5},{4,6},{5,7},{6,0},{7,1},{8,10},{9,11},{10,... | collective-permute-start | bytes 1474568 | tf_op jit(solution)/shard_map/ppermute | solution.py:528
  15.8 24.2 %copy-start = (bf16[1,2,96,5120]{3,2,1,0:T(8,128)(2,1)S(1)}, bf16[1,2,96,5120]{3,2,1,0:T(8,128)(2,1)}, u32[]{:S(2)}) copy-start(bf16[1,2,96,5120]{3,2,1,0:T(8,128)(2,1)} %param.9) | copy-start | bytes 5898244
  15.8 48.9 %all-to-all-start = ((bf16[8,192,640]{2,1,0:T(8,128)(2,1)}), bf16[8,192,640]{2,1,0:T(8,128)(2,1)}, u32[]{:S(2)}, u32[]{:S(2)}) async-start(bf16[8,192,640]{2,1,0:T(8,128)(2,1)} %get-tuple-element.63), calls=%async_computation | async-start | bytes 3932160 | tf_op jit(solution)/shard_map/all_to_all | solution.py:533
  22.0 10.7 %collective-permute-start.4 = (bf16[192,512]{1,0:T(8,128)(2,1)}, bf16[192,512]{1,0:T(8,128)(2,1)S(1)}, u32[]{:S(2)}, u32[]{:S(2)}) collective-permute-start(bf16[192,512]{1,0:T(8,128)(2,1)} %get-tuple-element.47.k0), channel_id=1, source_target_pairs={{0,6},{1,7},{2,0},{3,1},{4,2},{5,3},{6,4},{7,5},{8,14},{9,15},{10,... | collective-permute-start | bytes 589832 | tf_op jit(solution)/shard_map/ppermute | solution.py:530
  24.1 12.3 %collective-permute-start.3 = (bf16[192,512]{1,0:T(8,128)(2,1)}, bf16[192,512]{1,0:T(8,128)(2,1)S(1)}, u32[]{:S(2)}, u32[]{:S(2)}) collective-permute-start(bf16[192,512]{1,0:T(8,128)(2,1)} %get-tuple-element.47.k0), channel_id=1, source_target_pairs={{0,2},{1,3},{2,4},{3,5},{4,6},{5,7},{6,0},{7,1},{8,10},{9,11},{10,... | collective-permute-start | bytes 589832 | tf_op jit(solution)/shard_map/ppermute | solution.py:530
  32.1 7.8 %collective-permute-start.5 = (bf16[192,512]{1,0:T(8,128)(2,1)}, bf16[192,512]{1,0:T(8,128)(2,1)S(1)}, u32[]{:S(2)}, u32[]{:S(2)}) collective-permute-start(bf16[192,512]{1,0:T(8,128)(2,1)} %get-tuple-element.47.k0), channel_id=1, source_target_pairs={{0,4},{1,5},{2,6},{3,7},{4,0},{5,1},{6,2},{7,3},{8,12},{9,13},{10,... | collective-permute-start | bytes 589832 | tf_op jit(solution)/shard_map/ppermute | solution.py:532
  40.0 0.9 copy-start.5
  44.4 13.8 %copy-start.2 = (f32[1,320,512]{2,1,0:T(8,128)S(1)}, f32[1,320,512]{2,1,0:T(8,128)}, u32[]{:S(2)}) copy-start(f32[1,320,512]{2,1,0:T(8,128)} %master.1) | copy-start | bytes 1966084
  44.4 13.8 %copy-start.3 = (f32[1,320,512]{2,1,0:T(8,128)S(1)}, f32[1,320,512]{2,1,0:T(8,128)}, u32[]{:S(2)}) copy-start(f32[1,320,512]{2,1,0:T(8,128)} %first.1) | copy-start | bytes 1966084
  44.4 13.8 %copy-start.4 = (f32[1,320,512]{2,1,0:T(8,128)S(1)}, f32[1,320,512]{2,1,0:T(8,128)}, u32[]{:S(2)}) copy-start(f32[1,320,512]{2,1,0:T(8,128)} %second.1) | copy-start | bytes 1966084
  44.4 3.1 %collective-permute-start.6 = (bf16[2,320,512]{2,1,0:T(8,128)(2,1)S(1)}, bf16[2,320,512]{2,1,0:T(8,128)(2,1)S(1)}, u32[]{:S(2)}, u32[]{:S(2)}) collective-permute-start(bf16[2,320,512]{2,1,0:T(8,128)(2,1)S(1)} %get-tuple-element.49), channel_id=1, source_target_pairs={{0,1},{1,0},{2,3},{3,2},{4,5},{5,4},{6,7},{7,6},{8,9},{9,8},{10,11... | collective-permute-start | bytes 1966088 | tf_op jit(solution)/shard_map/ppermute | solution.py:536
  47.6 17.1 %copy-start.1 = (f32[320,512]{1,0:T(8,128)}, f32[320,512]{1,0:T(8,128)S(1)}, u32[]{:S(2)}) copy-start(f32[320,512]{1,0:T(8,128)S(1)} %get-tuple-element.50.here.refs_2_) | copy-start | bytes 1966084
  47.6 10.5 %collective-permute-start.7 = (bf16[320,512]{1,0:T(8,128)(2,1)S(1)}, bf16[320,512]{1,0:T(8,128)(2,1)S(1)}, u32[]{:S(2)}, u32[]{:S(2)}) collective-permute-start(bf16[320,512]{1,0:T(8,128)(2,1)S(1)} %get-tuple-element.51), channel_id=1, source_target_pairs={{0,8},{1,9},{2,10},{3,11},{4,12},{5,13},{6,14},{7,15},{8,0},{9,1},... | collective-permute-start | bytes 983048 | tf_op jit(solution)/shard_map/ppermute | solution.py:543
  59.9 12.6 %collective-permute-start.12 = (bf16[320,512]{1,0:T(8,128)(2,1)S(1)}, bf16[320,512]{1,0:T(8,128)(2,1)S(1)}, u32[]{:S(2)}, u32[]{:S(2)}) collective-permute-start(bf16[320,512]{1,0:T(8,128)(2,1)S(1)} %get-tuple-element.52.refs_0_), channel_id=1, source_target_pairs={{0,4},{1,5},{2,6},{3,7},{4,0},{5,1},{6,2},{7,3},{8,12},{9,13},{10,... | collective-permute-start | bytes 983048 | tf_op jit(solution)/shard_map/ppermute | solution.py:456
  60.4 12.1 %collective-permute-start.8 = (bf16[320,512]{1,0:T(8,128)(2,1)S(1)}, bf16[320,512]{1,0:T(8,128)(2,1)S(1)}, u32[]{:S(2)}, u32[]{:S(2)}) collective-permute-start(bf16[320,512]{1,0:T(8,128)(2,1)S(1)} %get-tuple-element.52.refs_0_), channel_id=1, source_target_pairs={{0,8},{1,9},{2,10},{3,11},{4,12},{5,13},{6,14},{7,15},{8,0},{9,1},... | collective-permute-start | bytes 983048 | tf_op jit(solution)/shard_map/ppermute | solution.py:456
  63.3 14.6 %collective-permute-start.10 = (bf16[320,512]{1,0:T(8,128)(2,1)S(1)}, bf16[320,512]{1,0:T(8,128)(2,1)S(1)}, u32[]{:S(2)}, u32[]{:S(2)}) collective-permute-start(bf16[320,512]{1,0:T(8,128)(2,1)S(1)} %get-tuple-element.52.refs_0_), channel_id=1, source_target_pairs={{0,6},{1,7},{2,0},{3,1},{4,2},{5,3},{6,4},{7,5},{8,14},{9,15},{10,... | collective-permute-start | bytes 983048 | tf_op jit(solution)/shard_map/ppermute | solution.py:456
  64.4 13.5 %collective-permute-start.9 = (bf16[320,512]{1,0:T(8,128)(2,1)S(1)}, bf16[320,512]{1,0:T(8,128)(2,1)}, u32[]{:S(2)}, u32[]{:S(2)}) collective-permute-start(bf16[320,512]{1,0:T(8,128)(2,1)S(1)} %get-tuple-element.52.refs_0_), channel_id=1, source_target_pairs={{0,2},{1,3},{2,4},{3,5},{4,6},{5,7},{6,0},{7,1},{8,10},{9,11},{10,... | collective-permute-start | bytes 983048 | tf_op jit(solution)/shard_map/ppermute | solution.py:456
  67.3 31.1 %all-to-all-start.1 = ((bf16[8,192,640]{2,1,0:T(8,128)(2,1)}), bf16[8,192,640]{2,1,0:T(8,128)(2,1)S(1)}, u32[]{:S(2)}, u32[]{:S(2)}) async-start(bf16[8,192,640]{2,1,0:T(8,128)(2,1)} %suffix_sums.1), calls=%async_computation.1 | async-start | bytes 3932160 | tf_op jit(solution)/shard_map/all_to_all | solution.py:538
  72.5 13.1 %collective-permute-start.17 = (bf16[320,512]{1,0:T(8,128)(2,1)S(1)}, bf16[320,512]{1,0:T(8,128)(2,1)}, u32[]{:S(2)}, u32[]{:S(2)}) collective-permute-start(bf16[320,512]{1,0:T(8,128)(2,1)S(1)} %collective-permute-done.8.refs_3_), channel_id=1, source_target_pairs={{0,4},{1,5},{2,6},{3,7},{4,0},{5,1},{6,2},{7,3},{8,12},{9,13},{10,... | collective-permute-start | bytes 983048 | tf_op jit(solution)/shard_map/ppermute | solution.py:456
  75.0 10.5 %collective-permute-start.18 = (bf16[320,512]{1,0:T(8,128)(2,1)S(1)}, bf16[320,512]{1,0:T(8,128)(2,1)}, u32[]{:S(2)}, u32[]{:S(2)}) collective-permute-start(bf16[320,512]{1,0:T(8,128)(2,1)S(1)} %collective-permute-done.12.refs_4_), channel_id=1, source_target_pairs={{0,1},{1,0},{2,3},{3,2},{4,5},{5,4},{6,7},{7,6},{8,9},{9,8},{10,11... | collective-permute-start | bytes 983048 | tf_op jit(solution)/shard_map/ppermute | solution.py:456
  77.9 13.8 %collective-permute-start.11 = (bf16[320,512]{1,0:T(8,128)(2,1)S(1)}, bf16[320,512]{1,0:T(8,128)(2,1)}, u32[]{:S(2)}, u32[]{:S(2)}) collective-permute-start(bf16[320,512]{1,0:T(8,128)(2,1)S(1)} %collective-permute-done.8.refs_3_), channel_id=1, source_target_pairs={{0,2},{1,3},{2,4},{3,5},{4,6},{5,7},{6,0},{7,1},{8,10},{9,11},{10,... | collective-permute-start | bytes 983048 | tf_op jit(solution)/shard_map/ppermute | solution.py:456
  78.4 13.4 %collective-permute-start.13 = (bf16[320,512]{1,0:T(8,128)(2,1)S(1)}, bf16[320,512]{1,0:T(8,128)(2,1)}, u32[]{:S(2)}, u32[]{:S(2)}) collective-permute-start(bf16[320,512]{1,0:T(8,128)(2,1)S(1)} %collective-permute-done.8.refs_3_), channel_id=1, source_target_pairs={{0,1},{1,0},{2,3},{3,2},{4,5},{5,4},{6,7},{7,6},{8,9},{9,8},{10,11... | collective-permute-start | bytes 983048 | tf_op jit(solution)/shard_map/ppermute | solution.py:456
  79.9 11.8 %collective-permute-start.15 = (bf16[320,512]{1,0:T(8,128)(2,1)S(1)}, bf16[320,512]{1,0:T(8,128)(2,1)}, u32[]{:S(2)}, u32[]{:S(2)}) collective-permute-start(bf16[320,512]{1,0:T(8,128)(2,1)S(1)} %collective-permute-done.8.refs_3_), channel_id=1, source_target_pairs={{0,6},{1,7},{2,0},{3,1},{4,2},{5,3},{6,4},{7,5},{8,14},{9,15},{10,... | collective-permute-start | bytes 983048 | tf_op jit(solution)/shard_map/ppermute | solution.py:456
  83.0 12.2 %copy-start.6 = (s32[16]{0:T(128)}, s32[16]{0:T(128)S(1)}, u32[]{:S(2)}) copy-start(s32[16]{0:T(128)S(1)} %stack.67.base_ref) | copy-start | bytes 196
  85.5 8.6 %collective-permute-start.19 = (bf16[320,512]{1,0:T(8,128)(2,1)}, bf16[320,512]{1,0:T(8,128)(2,1)S(1)}, u32[]{:S(2)}, u32[]{:S(2)}) collective-permute-start(bf16[320,512]{1,0:T(8,128)(2,1)} %collective-permute-done.17.refs_2_), channel_id=1, source_target_pairs={{0,1},{1,0},{2,3},{3,2},{4,5},{5,4},{6,7},{7,6},{8,9},{9,8},{10,11... | collective-permute-start | bytes 983048 | tf_op jit(solution)/shard_map/ppermute | solution.py:456
  91.7 2.4 %collective-permute-start.16 = (bf16[320,512]{1,0:T(8,128)(2,1)}, bf16[320,512]{1,0:T(8,128)(2,1)S(1)}, u32[]{:S(2)}, u32[]{:S(2)}) collective-permute-start(bf16[320,512]{1,0:T(8,128)(2,1)} %collective-permute-done.15.refs_1_), channel_id=1, source_target_pairs={{0,1},{1,0},{2,3},{3,2},{4,5},{5,4},{6,7},{7,6},{8,9},{9,8},{10,11... | collective-permute-start | bytes 983048 | tf_op jit(solution)/shard_map/ppermute | solution.py:456
  92.7 2.1 %collective-permute-start.14 = (bf16[320,512]{1,0:T(8,128)(2,1)}, bf16[320,512]{1,0:T(8,128)(2,1)}, u32[]{:S(2)}, u32[]{:S(2)}) collective-permute-start(bf16[320,512]{1,0:T(8,128)(2,1)} %collective-permute-done.11.refs_0_), channel_id=1, source_target_pairs={{0,1},{1,0},{2,3},{3,2},{4,5},{5,4},{6,7},{7,6},{8,9},{9,8},{10,11... | collective-permute-start | bytes 983048 | tf_op jit(solution)/shard_map/ppermute | solution.py:456
  94.1 1.0 copy-start.9
  94.1 1.0 copy-start.8
  94.7 3.6 %collective-permute-start.20 = (bf16[960,512]{1,0:T(8,128)(2,1)}, bf16[960,512]{1,0:T(8,128)(2,1)S(1)}, u32[]{:S(2)}, u32[]{:S(2)}) collective-permute-start(bf16[960,512]{1,0:T(8,128)(2,1)} %get-tuple-element.62), channel_id=1, source_target_pairs={{0,1},{1,0},{2,3},{3,2},{4,5},{5,4},{6,7},{7,6},{8,9},{9,8},{10,11... | collective-permute-start | bytes 2949128 | tf_op jit(solution)/shard_map/ppermute | solution.py:456
  98.4 0.6 copy-start.7
